TPU v7x, 32 devices: a whole 2x2x4 slice. The times are simulated.
32 devices in a mesh: shard: 8 (over y, x, core), context: 4 (over z).
Axes of the slice: x: 2, y: 2, z: 4, core: 2. Of those that a mesh axis runs over, the one named last changes fastest.
Arguments:
- block_input: float32 [8192, 2048], P(('shard', 'context')), may hold values from -6 to 6
- input_weight: bfloat16 [2048, 14336], P('shard')
- input_bias: bfloat16 [14336], P('shard'), may hold values from -3 to 3
- output_weight: bfloat16 [10240, 2048], P('shard')
- output_bias: bfloat16 [2, 2048], P(None, 'shard'), may hold values from -3 to 3
- norm_gain: bfloat16 [2048], P('shard'), may hold values from 0.5 to 1.5
- norm_bias: bfloat16 [2048], P('shard'), may hold values from -2 to 2
- assignment: int32 [8], replicated, may hold values from 0 to 7, as said below
- positions: int32 [8192], P(('shard', 'context')), may hold values from 0 to 2046, as said below
- cotangent: float32 [8192, 2048], P(('shard', 'context')), may hold values from -6 to 6
Outputs:
- block_output: float32 [8192, 2048], P(('shard', 'context'))
- block_input_gradient: float32 [8192, 2048], P(('shard', 'context'))
- input_weight_gradient: float32 [2048, 14336], P('shard')
- input_bias_gradient: float32 [14336], P('shard')
- output_weight_gradient: float32 [10240, 2048], P('shard')
- output_bias_gradient: float32 [2, 2048], P(None, 'shard')
- norm_gain_gradient: float32 [2048], P('shard')
- norm_bias_gradient: float32 [2048], P('shard')
Inputs may be any that keep to these rules, and one draw needn't show every extreme that they name: `assignment`: a permutation: each of 0 to 7 once, the same for every context group. `positions`: within a sequence, a token's position is the sequence's start offset (0 to 1023) plus its causal index inside the sequence.
All inputs are finite; a program needn't handle non-finite values.
Results may differ from a plain program's by a relative error of at most 0.015.
Values may be sent and summed in bfloat16 or wider, within the bound.
No kernel may reach another device: no remote copies, remote signals or barrier semaphores. Data moves between devices by JAX's collectives and lax.ppermute only.
A program may use at most 640 MiB of HBM per device.

v0:
```python
import math

import jax
import jax.numpy as jnp
from jax import lax
from jax.sharding import PartitionSpec as P

D = 2048
HEADS = 32
HEAD_DIM = 64
ROT = 32
SEQ_LEN = 1024


epsilon = 1e-05
floor_score = -1e30


def causal_index(row_index, assignment, half_rows):
    block_index = row_index // half_rows
    matches = block_index[:, None] == jnp.arange(assignment.shape[0], dtype=jnp.int32)[None, :]
    chosen = jnp.sum(jnp.where(matches, assignment[None, :], 0), axis=1)
    return chosen * half_rows + row_index % half_rows


def rotary_tables(position_ids):
    half_rot = ROT // 2
    frequency = 10000.0 ** (-2.0 * jnp.arange(half_rot, dtype=jnp.float32) / ROT)
    angles = position_ids.astype(jnp.float32)[:, None] * frequency[None, :]
    return (jnp.cos(angles), jnp.sin(angles))


def rotate(field, cosine_table, sine_table, direction):
    half_rot = ROT // 2
    first_half = field[..., :half_rot]
    second_half = field[..., half_rot:ROT]
    remainder = field[..., ROT:]
    cosine = cosine_table[:, None, :]
    sine_part = sine_table[:, None, :] * direction
    return jnp.concatenate(
        [
            first_half * cosine - second_half * sine_part,
            second_half * cosine + first_half * sine_part,
            remainder,
        ],
        axis=-1,
    )


def gelu_tanh(value):
    return jax.nn.gelu(value, approximate=True)


def attend(query, keys, values, allowed, heads_per):
    query_count, head_count, head_size = query.shape
    scaling = head_size ** (-0.5)

    def head_step(group_index, carry):
        output, log_total = carry
        first_head = group_index * heads_per
        query_part = lax.dynamic_slice_in_dim(query, first_head, heads_per, 1)
        key_part = lax.dynamic_slice_in_dim(keys, first_head, heads_per, 1)
        value_part = lax.dynamic_slice_in_dim(values, first_head, heads_per, 1)
        scores = (
            jnp.einsum("qhd,khd->hqk", query_part, key_part, preferred_element_type=jnp.float32)
            * scaling
        )
        scores = jnp.where(allowed[None], scores, floor_score)
        highest = jnp.max(scores, axis=2, keepdims=True)
        part_total = highest + jnp.log(jnp.sum(jnp.exp(scores - highest), axis=2, keepdims=True))
        rounded = jnp.exp(scores - part_total).astype(jnp.bfloat16)
        mixture = jnp.einsum(
            "hqk,khd->qhd", rounded, value_part, preferred_element_type=jnp.float32
        )
        output = lax.dynamic_update_slice_in_dim(
            output, mixture.astype(jnp.bfloat16), first_head, 1
        )
        log_total = lax.dynamic_update_slice_in_dim(log_total, part_total[:, :, 0], first_head, 0)
        return (output, log_total)

    initial = (
        jnp.zeros((query_count, head_count, head_size), jnp.bfloat16),
        jnp.zeros((head_count, query_count), jnp.float32),
    )
    return lax.fori_loop(0, head_count // heads_per, head_step, initial)


def attend_back(query, keys, values, allowed, log_total, upstream, delta, heads_per):
    query_count, head_count, head_size = query.shape
    key_count = keys.shape[0]
    scaling = head_size ** (-0.5)

    def head_step(group_index, carry):
        query_total, key_total, value_total = carry
        first_head = group_index * heads_per
        query_part = lax.dynamic_slice_in_dim(query, first_head, heads_per, 1)
        key_part = lax.dynamic_slice_in_dim(keys, first_head, heads_per, 1)
        value_part = lax.dynamic_slice_in_dim(values, first_head, heads_per, 1)
        upstream_part = lax.dynamic_slice_in_dim(upstream, first_head, heads_per, 1)
        total_part = lax.dynamic_slice_in_dim(log_total, first_head, heads_per, 0)
        delta_part = lax.dynamic_slice_in_dim(delta, first_head, heads_per, 0)
        scores = (
            jnp.einsum("qhd,khd->hqk", query_part, key_part, preferred_element_type=jnp.float32)
            * scaling
        )
        scores = jnp.where(allowed[None], scores, floor_score)
        weights = jnp.exp(scores - total_part[:, :, None])
        rounded = weights.astype(jnp.bfloat16)
        value_term = jnp.einsum(
            "hqk,qhd->khd", rounded, upstream_part, preferred_element_type=jnp.float32
        )
        weight_slope = jnp.einsum(
            "qhd,khd->hqk", upstream_part, value_part, preferred_element_type=jnp.float32
        )
        score_grad = (weights * (weight_slope - delta_part[:, :, None])).astype(jnp.bfloat16)
        query_term = (
            jnp.einsum("hqk,khd->qhd", score_grad, key_part, preferred_element_type=jnp.float32)
            * scaling
        )
        key_term = (
            jnp.einsum("hqk,qhd->khd", score_grad, query_part, preferred_element_type=jnp.float32)
            * scaling
        )
        query_total = lax.dynamic_update_slice_in_dim(query_total, query_term, first_head, 1)
        key_total = lax.dynamic_update_slice_in_dim(key_total, key_term, first_head, 1)
        value_total = lax.dynamic_update_slice_in_dim(value_total, value_term, first_head, 1)
        return (query_total, key_total, value_total)

    initial = (
        jnp.zeros((query_count, head_count, head_size), jnp.float32),
        jnp.zeros((key_count, head_count, head_size), jnp.float32),
        jnp.zeros((key_count, head_count, head_size), jnp.float32),
    )
    return lax.fori_loop(0, head_count // heads_per, head_step, initial)


def local(
    block_input,
    input_weight,
    input_bias,
    output_weight,
    output_bias,
    norm_gain,
    norm_bias,
    assignment,
    positions,
    cotangent,
):
    tokens_here = block_input.shape[0]
    half_rows = tokens_here // 2
    context_size = lax.axis_size("context")
    shard_size = lax.axis_size("shard")
    group = tokens_here * context_size
    heads_per = math.gcd(HEADS, 8)
    weight_in, weight_out, bias_in, bias_out, gain_full, shift_full = (
        lax.all_gather(input_weight, "shard", axis=0, tiled=True),
        lax.all_gather(output_weight, "shard", axis=0, tiled=True),
        lax.all_gather(input_bias, "shard", axis=0, tiled=True),
        lax.all_gather(output_bias, "shard", axis=1, tiled=True),
        lax.all_gather(norm_gain, "shard", axis=0, tiled=True),
        lax.all_gather(norm_bias, "shard", axis=0, tiled=True),
    )
    query_rows = lax.axis_index("context") * tokens_here + jnp.arange(tokens_here, dtype=jnp.int32)
    query_causal = causal_index(query_rows, assignment, half_rows)
    key_causal = causal_index(jnp.arange(group, dtype=jnp.int32), assignment, half_rows)
    allowed = (key_causal[None, :] <= query_causal[:, None]) & (
        key_causal[None, :] // SEQ_LEN == query_causal[:, None] // SEQ_LEN
    )
    gain = gain_full.astype(jnp.float32)
    shift = shift_full.astype(jnp.float32)
    centred = block_input - jnp.mean(block_input, axis=1, keepdims=True)
    inverse_std = lax.rsqrt(jnp.mean(centred * centred, axis=1, keepdims=True) + epsilon)
    normalized = centred * inverse_std
    normed = (normalized * gain + shift).astype(jnp.bfloat16)
    projected = jnp.dot(normed, weight_in, preferred_element_type=jnp.float32) + bias_in.astype(
        jnp.float32
    )
    cosine_table, sine_table = rotary_tables(positions)
    query = rotate(
        projected[:, :D].reshape(tokens_here, HEADS, HEAD_DIM), cosine_table, sine_table, 1.0
    ).astype(jnp.bfloat16)
    key_here = rotate(
        projected[:, D : 2 * D].reshape(tokens_here, HEADS, HEAD_DIM), cosine_table, sine_table, 1.0
    ).astype(jnp.bfloat16)
    value_here = (
        projected[:, 2 * D : 3 * D].astype(jnp.bfloat16).reshape(tokens_here, HEADS, HEAD_DIM)
    )
    keys, values = (
        lax.all_gather(key_here, "context", axis=0, tiled=True),
        lax.all_gather(value_here, "context", axis=0, tiled=True),
    )
    hidden_pre = projected[:, 3 * D :]
    activation = gelu_tanh(hidden_pre).astype(jnp.bfloat16)
    attended, log_total = attend(query, keys, values, allowed, heads_per)
    joined = jnp.concatenate([attended.reshape(tokens_here, D), activation], axis=1)
    bias_sum = bias_out[0].astype(jnp.float32) + bias_out[1].astype(jnp.float32)
    block_output = (
        block_input + jnp.dot(joined, weight_out, preferred_element_type=jnp.float32) + bias_sum
    )
    upstream = cotangent.astype(jnp.bfloat16)
    joined_grad = jnp.dot(upstream, weight_out.T, preferred_element_type=jnp.float32)
    attended_grad = joined_grad[:, :D].astype(jnp.bfloat16).reshape(tokens_here, HEADS, HEAD_DIM)
    hidden_grad = jax.vjp(gelu_tanh, hidden_pre)[1](joined_grad[:, D:])[0]
    delta = jnp.sum(attended_grad.astype(jnp.float32) * attended.astype(jnp.float32), axis=2).T
    query_total, key_whole, value_whole = attend_back(
        query, keys, values, allowed, log_total, attended_grad, delta, heads_per
    )
    key_total, value_total = (
        lax.psum_scatter(key_whole.reshape(group, D), "context", scatter_dimension=0, tiled=True),
        lax.psum_scatter(value_whole.reshape(group, D), "context", scatter_dimension=0, tiled=True),
    )
    query_total = rotate(query_total, cosine_table, sine_table, -1.0).reshape(tokens_here, D)
    key_total = rotate(
        key_total.reshape(tokens_here, HEADS, HEAD_DIM), cosine_table, sine_table, -1.0
    ).reshape(tokens_here, D)
    projected_grad = jnp.concatenate([query_total, key_total, value_total, hidden_grad], axis=1)
    rounded_grad = projected_grad.astype(jnp.bfloat16)
    normed_grad = jnp.dot(rounded_grad, weight_in.T, preferred_element_type=jnp.float32)
    piece = normed
    weight_in_grad = lax.psum_scatter(
        lax.dot_general(
            piece, rounded_grad, (((0,), (0,)), ((), ())), preferred_element_type=jnp.float32
        ).astype(jnp.bfloat16),
        "shard",
        scatter_dimension=0,
        tiled=True,
    ).astype(jnp.float32)
    piece = joined
    weight_out_grad = lax.psum_scatter(
        lax.dot_general(
            piece, upstream, (((0,), (0,)), ((), ())), preferred_element_type=jnp.float32
        ).astype(jnp.bfloat16),
        "shard",
        scatter_dimension=0,
        tiled=True,
    ).astype(jnp.float32)
    weight_in_grad, weight_out_grad = (
        lax.psum(weight_in_grad.astype(jnp.bfloat16), "context").astype(jnp.float32),
        lax.psum(weight_out_grad.astype(jnp.bfloat16), "context").astype(jnp.float32),
    )
    bias_in_sum, bias_out_sum, gain_sum, shift_sum = lax.psum(
        (
            jnp.sum(projected_grad, axis=0),
            jnp.sum(cotangent, axis=0),
            jnp.sum(normed_grad * normalized, axis=0),
            jnp.sum(normed_grad, axis=0),
        ),
        ("shard", "context"),
    )
    shard_here = lax.axis_index("shard")

    def own_share(vector):
        length = vector.shape[0] // shard_size
        return lax.dynamic_slice_in_dim(vector, shard_here * length, length, 0)

    bias_row = own_share(bias_out_sum)
    scaled = normed_grad * gain
    input_grad = cotangent + inverse_std * (
        scaled
        - jnp.mean(scaled, axis=1, keepdims=True)
        - normalized * jnp.mean(scaled * normalized, axis=1, keepdims=True)
    )
    return (
        block_output,
        input_grad,
        weight_in_grad,
        own_share(bias_in_sum),
        weight_out_grad,
        jnp.stack([bias_row, bias_row]),
        own_share(gain_sum),
        own_share(shift_sum),
    )


def solution(mesh):
    return jax.shard_map(
        local,
        mesh=mesh,
        in_specs=(
            P(("shard", "context"), None),
            P("shard", None),
            P("shard"),
            P("shard", None),
            P(None, "shard"),
            P("shard"),
            P("shard"),
            P(),
            P(("shard", "context")),
            P(("shard", "context"), None),
        ),
        out_specs=(
            P(("shard", "context"), None),
            P(("shard", "context"), None),
            P("shard", None),
            P("shard"),
            P("shard", None),
            P(None, "shard"),
            P("shard"),
            P("shard"),
        ),
        check_vma=False,
    )
```

profile of v0, /device:TPU:0, one launch (start us, length us, event | category | flops | bytes accessed | tf_op | source)
XLA Modules:
  0.0 2209.7 jit_solution(16406592540616920704)
XLA Ops:
  8.8 10.7 all-gather.2
  19.5 8.9 all-gather.1
  37.0 243.1 %all-gather.8.cloned.1.call-done = bf16[2048,14336]{1,0:T(8,128)(2,1)} async-done(((bf16[256,14336]{1,0:T(8,128)(2,1)}), bf16[2048,14336]{1,0:T(8,128)(2,1)}) %all-gather.8.cloned.1.call-update) | async-done | bytes 58720272 | tf_op jit(solution)/shard_map/all_gather | solution.py:156
  280.1 32.4 %convolution_add_fusion = f32[256,14336]{1,0:T(8,128)} fusion(bf16[2048,14336]{1,0:T(8,128)(2,1)} %all-gather.8.cloned.1.call-done, f32[14336]{0:T(1024)S(1)} %bitcast.71, f32[256,2048]{1,0:T(8,128)S(1)} %copy-done.1, f32[2048]{0:T(1024)S(1)} %bitcast.68, f32[2048]{0:T(1024)S(1)} %bitcast.64, f32[256]{0:T(256)S(1)} %add_rsqrt_fusion, ...), kind=kOutput, calls=%fused_computation.52 | convolution fusion | flops 15038676992 | bytes 75573248 | tf_op jit(solution)/shard_map/dot_general | solution.py:175
  332.5 146.6 %all-gather.14.cloned.1.call-done = bf16[10240,2048]{1,0:T(8,128)(2,1)} async-done(((bf16[1280,2048]{1,0:T(8,128)(2,1)}), bf16[10240,2048]{1,0:T(8,128)(2,1)}) %all-gather.14.cloned.1.call-update) | async-done | bytes 41943056 | tf_op jit(solution)/shard_map/all_gather | solution.py:157
  479.2 22.1 %fusion.53 = f32[256,10240]{1,0:T(8,128)} fusion(bf16[10240,2048]{1,0:T(8,128)(2,1)} %all-gather.14.cloned.1.call-done, f32[256,2048]{1,0:T(8,128)S(1)} %copy-done.4), kind=kOutput, calls=%fused_computation.90 | convolution fusion | flops 10737942528 | bytes 54525952 | tf_op jit(solution)/shard_map/dot_general | solution.py:201
  505.9 55.4 %all-gather.10.cloned.1.call-done = bf16[1024,32,64]{0,2,1:T(8,128)(2,1)} async-done(((bf16[256,32,64]{0,2,1:T(8,128)(2,1)}), bf16[1024,32,64]{0,2,1:T(8,128)(2,1)}) %all-gather.10.cloned.1.call-update) | async-done | bytes 4194320 | tf_op jit(solution)/shard_map/all_gather | solution.py:190
  561.3 80.8 %all-gather.12.cloned.1.call-done = bf16[1024,32,64]{0,2,1:T(8,128)(2,1)} async-done(((bf16[256,32,64]{0,2,1:T(8,128)(2,1)}), bf16[1024,32,64]{0,2,1:T(8,128)(2,1)}) %all-gather.12.cloned.1.call-update) | async-done | bytes 4194320 | tf_op jit(solution)/shard_map/all_gather | solution.py:189
  642.2 35.1 %while.34 = (s32[]{:T(128)}, bf16[256,32,64]{0,2,1:T(8,128)(2,1)S(1)}, f32[32,256]{1,0:T(8,128)S(1)}, bf16[1024,32,64]{0,2,1:T(8,128)(2,1)}, bf16[256,32,64]{0,2...) while((s32[]{:T(128)}, ...), condition=%wide.region_7.8_spmd.clone, body=%wide.region_4.7_spmd.clone.sunk | while | flops 560855040 | bytes 28913856 | solution.py:85
  688.0 67.1 %while.35 = (s32[]{:T(128)}, f32[256,32,64]{0,2,1:T(8,128)}, f32[1024,32,64]{0,2,1:T(8,128)}, f32[1024,32,64]{0,2,1:T(8,128)}, bf16[1024,32,64]{0,2,1:T(8,128)(2...) while((s32[]{:T(128)}, f32[256,32,64]{0,2,1:T(8,128)}, ...), condition=%wide.region_10.11_spmd.clone, body=%wide.region_9.10_spmd.clone.sunk | while | flops 1364590592 | bytes 47520992 | solution.py:134
  755.2 9.3 copy.52
  764.6 12.4 fusion.48
  777.6 19.2 convolution_convert_fusion.1
  799.4 98.6 %reduce-scatter.7.cloned.1.call-done = f32[256,2048]{0,1:T(8,128)} async-done(((f32[1024,2048]{0,1:T(8,128)}), f32[256,2048]{0,1:T(8,128)}) %reduce-scatter.7.cloned.1.call-update) | async-done | bytes 2097168 | tf_op jit(solution)/shard_map/reduce_scatter | solution.py:209
  909.8 135.6 %reduce-scatter.9.cloned.1.call-done = f32[256,2048]{1,0:T(8,128)} async-done(((f32[1024,2048]{1,0:T(8,128)}), f32[256,2048]{1,0:T(8,128)}) %reduce-scatter.9.cloned.1.call-update) | async-done | bytes 2097168 | tf_op jit(solution)/shard_map/reduce_scatter | solution.py:210
  1053.0 39.2 %convolution_convert_fusion = bf16[2048,14336]{1,0:T(8,128)(2,1)} fusion(f32[256,2048]{1,0:T(8,128)} %param.14, f32[2048]{0:T(1024)S(1)} %bitcast.69, f32[2048]{0:T(1024)S(1)} %bitcast.65, f32[256]{0:T(256)S(1)} %copy-done.14, f32[256]{0:T(256)S(1)} %copy-done.12, bf16[256,14336]{1,0:T(8,128)(2,1)} %fusion.86), kind=kOutput, calls=%fused_computation.50 | convolution fusion | flops 15064367104 | bytes 68175872 | tf_op jit(solution)/shard_map/dot_general | solution.py:221
  1092.3 10.9 fusion.72.clone.4
  1103.2 29.6 %multiply_reduce_fusion = (f32[2048]{0:T(1024)}, f32[256]{0:T(256)S(1)}, f32[256]{0:T(256)S(1)}, f32[2048]{0:T(1024)}, f32[256,2048]{1,0:T(8,128)}) fusion(f32[256,2048]{1,0:T(8,128)} %param.14, f32[256]{0:T(256)S(1)} %copy-done.14, f32[256]{0:T(256)S(1)} %copy-done.12, f32[2048]{0:T(1024)S(1)} %bitcast.66, ...), kind=kOutput, calls=%fused_computation.73 | convolution fusion | flops 15037100032 | bytes 70283264 | tf_op jit(solution)/shard_map/dot_general | solution.py:218
  1144.3 150.2 %reduce-scatter.13.cloned.1.call-done = bf16[1280,2048]{1,0:T(8,128)(2,1)} async-done(((bf16[10240,2048]{1,0:T(8,128)(2,1)}), bf16[1280,2048]{1,0:T(8,128)(2,1)}) %reduce-scatter.13.cloned.1.call-update) | async-done | bytes 5242896
  1294.6 333.4 %reduce-scatter.11.cloned.1.call-done = bf16[256,14336]{1,0:T(8,128)(2,1)} async-done(((bf16[2048,14336]{1,0:T(8,128)(2,1)}), bf16[256,14336]{1,0:T(8,128)(2,1)}) %reduce-scatter.11.cloned.1.call-update) | async-done | bytes 7340048 | tf_op jit(solution)/shard_map/reduce_scatter | solution.py:220
  1636.8 20.9 fusion.51
  1657.6 98.1 %all-reduce.6.cloned.1.call-done = (f32[14336]{0:T(1024)}, f32[2048]{0:T(1024)}, f32[2048]{0:T(1024)}, f32[2048]{0:T(1024)}) async-done(((f32[14336]{0:T(1024)}, f32[2048]{0:T(1024)}, f32[2048]{0:T(1024)}, f32[2048]{0:T(1024)}), (f32[14336]{0:T(1024)}, f32[2048]{0:T(1024)}, f32[2048]{0:T(1024)}, f32[2048]{0:T(1024)})) %all-reduce.6.cloned.1.call-update) | async-done | bytes 81936 | tf_op jit(solution)/shard_map/psum | solution.py:241
  1761.0 425.7 %all-reduce.8.cloned.1.call-done = (bf16[256,14336]{1,0:T(8,128)(2,1)}, bf16[1280,2048]{1,0:T(8,128)(2,1)}) async-done(((bf16[256,14336]{1,0:T(8,128)(2,1)}, bf16[1280,2048]{1,0:T(8,128)(2,1)}), (bf16[256,14336]{1,0:T(8,128)(2,1)}, bf16[1280,2048]{1,0:T(8,128)(2,1)})) %all-reduce.8.cloned.1.call-update) | async-done | bytes 12582928 | tf_op jit(solution)/shard_map/psum | solution.py:238
  2186.6 10.4 convert_element_type.102
  (174 shorter events, 201.1 us)
Async XLA Ops:
  7.2 12.3 copy-start.22
  7.2 21.2 copy-start.23
  7.2 29.2 %copy-start.1 = (f32[256,2048]{1,0:T(8,128)S(1)}, f32[256,2048]{1,0:T(8,128)}, u32[]{:S(2)}) copy-start(f32[256,2048]{1,0:T(8,128)} %param.14) | copy-start | bytes 6291460
  7.2 272.9 %all-gather.8.cloned.1.call-start = ((), (), s32[]{:S(2)}) async-start(), calls=%async_computation.4 | async-start | bytes 66060288 | tf_op jit(solution)/shard_map/all_gather | solution.py:156
  7.9 471.2 %all-gather.14.cloned.1.call-start = ((), (), s32[]{:S(2)}) async-start(), calls=%async_computation.7 | async-start | bytes 47185920 | tf_op jit(solution)/shard_map/all_gather | solution.py:157
  8.7 552.6 %all-gather.10.cloned.1.call-start = ((), (), s32[]{:S(2)}) async-start(), calls=%async_computation.5 | async-start | bytes 5242880 | tf_op jit(solution)/shard_map/all_gather | solution.py:190
  28.4 284.1 %copy-start.9 = (f32[8,1,256]{2,1,0:T(1,128)}, f32[8,1,256]{2,1,0:T(1,128)S(1)}, u32[]{:S(2)}) copy-start(f32[8,1,256]{2,1,0:T(1,128)S(1)} %convert_element_type.106) | copy-start | bytes 24580
  36.4 276.1 %copy-start.7 = (f32[8,1,256]{2,1,0:T(1,128)}, f32[8,1,256]{2,1,0:T(1,128)S(1)}, u32[]{:S(2)}) copy-start(f32[8,1,256]{2,1,0:T(1,128)S(1)} %convert_element_type.105) | copy-start | bytes 24580
  36.6 275.9 %copy-start.11 = (f32[256]{0:T(256)}, f32[256]{0:T(256)S(1)}, u32[]{:S(2)}) copy-start(f32[256]{0:T(256)S(1)} %broadcast_multiply_fusion.3) | copy-start | bytes 3076
  37.0 275.5 %copy-start.13 = (f32[256]{0:T(256)}, f32[256]{0:T(256)S(1)}, u32[]{:S(2)}) copy-start(f32[256]{0:T(256)S(1)} %add_rsqrt_fusion) | copy-start | bytes 3076
  280.1 35.5 %copy-start.21 = (s32[256]{0:T(256)S(1)}, s32[256]{0:T(256)}, u32[]{:S(2)}) copy-start(s32[256]{0:T(256)} %param.22) | copy-start | bytes 3076
  315.6 326.5 %all-gather.12.cloned.1.call-start = ((), (), s32[]{:S(2)}) async-start(), calls=%async_computation.6 | async-start | bytes 5242880 | tf_op jit(solution)/shard_map/all_gather | solution.py:189
  316.4 12.0 copy-start.15
  321.1 158.0 %copy-start.4 = (f32[256,2048]{1,0:T(8,128)S(1)}, f32[256,2048]{1,0:T(8,128)}, u32[]{:S(2)}) copy-start(f32[256,2048]{1,0:T(8,128)} %param.23) | copy-start | bytes 6291460
  332.0 565.9 %reduce-scatter.7.cloned.1.call-start = ((), (), s32[]{:S(2)}) async-start(), calls=%async_computation.8 | async-start | bytes 10485760 | tf_op jit(solution)/shard_map/reduce_scatter | solution.py:209
  755.2 290.2 %reduce-scatter.9.cloned.1.call-start = ((), (), s32[]{:S(2)}) async-start(), calls=%async_computation.9 | async-start | bytes 10485760 | tf_op jit(solution)/shard_map/reduce_scatter | solution.py:210
  764.5 530.0 %reduce-scatter.13.cloned.1.call-start = ((), (), s32[]{:S(2)}) async-start(), calls=%async_computation.11 | async-start | bytes 47185920
  796.8 102.5 %copy-start.16 = (f32[256,16]{0,1:T(8,128)S(1)}, f32[256,16]{0,1:T(8,128)}, u32[]{:S(2)}) copy-start(f32[256,16]{0,1:T(8,128)} %copy-done.15) | copy-start | bytes 49156
  796.8 102.5 %copy-start.17 = (f32[256,16]{0,1:T(8,128)S(1)}, f32[256,16]{0,1:T(8,128)}, u32[]{:S(2)}) copy-start(f32[256,16]{0,1:T(8,128)} %get-tuple-element.484) | copy-start | bytes 49156
  796.8 831.1 %reduce-scatter.11.cloned.1.call-start = ((), (), s32[]{:S(2)}) async-start(), calls=%async_computation.10 | async-start | bytes 66060288 | tf_op jit(solution)/shard_map/reduce_scatter | solution.py:220
  1092.2 663.4 %all-reduce.6.cloned.1.call-start = ((), (), s32[]{:S(2)}) async-start(), calls=%async_computation.12 | async-start | bytes 163840 | tf_op jit(solution)/shard_map/psum | solution.py:241
  1144.3 483.7 %copy-start.20 = (bf16[2,256]{1,0:T(2,128)(2,1)S(1)}, bf16[2,256]{1,0:T(2,128)(2,1)}, u32[]{:S(2)}) copy-start(bf16[2,256]{1,0:T(2,128)(2,1)} %param.18) | copy-start | bytes 3076
  1144.3 492.5 %copy-start.2 = (f32[256,2048]{1,0:T(8,128)S(1)}, f32[256,2048]{1,0:T(8,128)}, u32[]{:S(2)}) copy-start(f32[256,2048]{1,0:T(8,128)} %param.14) | copy-start | bytes 6291460
  1144.3 1042.3 %all-reduce.8.cloned.1.call-start = ((), (), s32[]{:S(2)}) async-start(), calls=%async_computation.13 | async-start | bytes 25165824 | tf_op jit(solution)/shard_map/psum | solution.py:238
  (10 other events, 67.4 us)
Sparse Core Ops, SparseCore 0:
  10.0 270.0 all-gather.7
  282.0 197.1 all-gather.13
  480.7 80.5 all-gather.9
  563.3 78.7 all-gather.11
  755.3 142.6 reduce-scatter.6
  900.2 145.1 reduce-scatter.8
  1049.0 245.4 reduce-scatter.12
  1298.6 329.3 reduce-scatter.10
  1634.6 121.0 all-reduce.5
  1758.1 428.4 all-reduce.7
where the time goes:
time: 2220 us; the launch traced here: 2210 us
  waiting for transfers between devices  1770 us (80%)
  matrix products  254 us (11%)
  other arithmetic  81.9 us (4%)
  local copies, waits for them, and re-layouts  52.9 us (2%)
  blocking collectives  36.2 us (2%)
    psum x1, waiting for transfers between devices, local(): lax.psum(weight_in_grad.astype(jnp.bfloat16), 'context').astype(jnp.float32)  426 us
    reduce_scatter x1, waiting for transfers between devices, local(): lax.psum_scatter(lax.dot_general(piece, rounded_grad, (((0,), (0,)), ((),...  333 us
    all_gather x1, waiting for transfers between devices, local(): lax.all_gather(input_weight, 'shard', axis=0, tiled=True)  243 us
    unnamed x11, waiting for transfers between devices  152 us
    all_gather x1, waiting for transfers between devices, local(): lax.all_gather(output_weight, 'shard', axis=0, tiled=True)  147 us
    reduce_scatter x1, waiting for transfers between devices, local(): lax.psum_scatter(value_whole.reshape(group, D), 'context', scatter_dimens...  136 us
    reduce_scatter x1, waiting for transfers between devices, local(): lax.psum_scatter(key_whole.reshape(group, D), 'context', scatter_dimensio...  98.6 us
    psum x1, waiting for transfers between devices, local(): lax.psum((jnp.sum(projected_grad, axis=0), jnp.sum(cotangent, axis=0), jn...  98.1 us
  transfers between devices with their start and end apart: 10, of which 10 were waited for; matrix products, arithmetic and copies ran while one was open for 12% of the time, Pallas kernels for 0%

commit v1 on v0

v1 whole, which is shorter than its diff:
```python
import functools

import jax
import jax.numpy as jnp
from jax import lax
from jax.experimental import pallas as pl
from jax.experimental.pallas import tpu as pltpu
from jax.sharding import PartitionSpec as P

D = 2048
FF = 8192
HEADS = 32
HEAD_DIM = 64
ROT = 32
SEQ_LEN = 1024
BLK = 128
TILE = 256

epsilon = 1e-05
floor_score = -1e30

F32 = jnp.float32
BF16 = jnp.bfloat16


def dot(a, b, dims=((1,), (0,))):
    return lax.dot_general(a, b, (dims, ((), ())), preferred_element_type=F32)


def column_plan(shard_size, context_size):
    rows = (D + FF) // shard_size
    blocks = rows // HEAD_DIM
    split = HEADS % blocks
    if rows % HEAD_DIM == 0 and split % context_size == 0 and (blocks - split) % context_size == 0:
        inner = [
            (at * HEAD_DIM, size * HEAD_DIM // context_size)
            for at, size in ((0, split), (split, blocks - split))
            if size
        ]
        segments = [(s * rows + at, width) for s in range(shard_size) for at, width in inner]
        return inner, segments
    return None, [(0, D // context_size), (D, FF // context_size)]


def take(array, segments, context, axis):
    parts = [
        lax.dynamic_slice_in_dim(array, base + context * width, width, axis)
        for base, width in segments
    ]
    return jnp.concatenate(parts, axis) if len(parts) > 1 else parts[0]


def untake(gathered, segments, axis):
    parts = []
    at = 0
    for _, width in segments:
        for c in range(gathered.shape[0]):
            parts.append(lax.slice_in_dim(gathered[c], at, at + width, axis=axis))
        at += width
    return jnp.concatenate(parts, axis)


def lane_mask(shape, head):
    lane = lax.broadcasted_iota(jnp.int32, shape, len(shape) - 1)
    return (lane // HEAD_DIM) == head


def rotated(x, cosine, sine_low, sine_high):
    half = ROT // 2
    width = x.shape[1]
    return (
        x * cosine
        + pltpu.roll(x, width - half, 1) * sine_low
        + pltpu.roll(x, half, 1) * sine_high
    )


def stored(place_ref, p):
    return pl.ds(pl.multiple_of(place_ref[p] * BLK, BLK), BLK)


def attend_kernel(
    place_ref, q_ref, k_ref, v_ref, cos_ref, low_ref, high_ref,
    out_ref, total_ref, qr_ref, kr_ref, vr_ref,
):
    tokens = q_ref.shape[0]
    for p in range(tokens // BLK):
        here = pl.ds(p * BLK, BLK)
        there = stored(place_ref, p)
        cosine, low, high = cos_ref[there, :], low_ref[there, :], high_ref[there, :]
        query = rotated(q_ref[there, :], cosine, low, high).astype(BF16)
        qr_ref[here, :] = (query.astype(F32) * HEAD_DIM**-0.5).astype(BF16)
        kr_ref[here, :] = rotated(k_ref[there, :], cosine, low, high).astype(BF16)
        vr_ref[here, :] = v_ref[there, :].astype(BF16)
    for tile in range(tokens // TILE):
        first = tile * TILE // SEQ_LEN * SEQ_LEN
        last = (tile + 1) * TILE
        count = last - first
        query = qr_ref[pl.ds(tile * TILE, TILE), :]
        keys = kr_ref[pl.ds(first, count), :]
        values = vr_ref[pl.ds(first, count), :]
        row = lax.broadcasted_iota(jnp.int32, (TILE, count), 0) + (tile * TILE - first)
        allowed = lax.broadcasted_iota(jnp.int32, (TILE, count), 1) <= row
        outs, totals = [], []
        for head in range(2):
            mine = jnp.where(lane_mask(query.shape, head), query, jnp.zeros_like(query))
            scores = jnp.where(allowed, dot(mine, keys, ((1,), (1,))), floor_score)
            highest = jnp.max(scores, axis=1, keepdims=True)
            weights = jnp.exp(scores - highest)
            total = jnp.sum(weights, axis=1, keepdims=True)
            outs.append(dot(weights.astype(BF16), values) / total)
            totals.append(highest + jnp.log(total))
        wide = (TILE, 2 * HEAD_DIM)
        first_head = lane_mask(wide, 0)
        out = jnp.where(first_head, outs[0], outs[1]).astype(BF16)
        total_ref[pl.ds(tile * TILE, TILE), :] = jnp.where(
            first_head, jnp.broadcast_to(totals[0], wide), jnp.broadcast_to(totals[1], wide)
        )
        for part in range(TILE // BLK):
            out_ref[stored(place_ref, tile * (TILE // BLK) + part), :] = out[
                part * BLK : (part + 1) * BLK
            ]


def attend_back_kernel(
    place_ref, q_ref, k_ref, v_ref, total_ref, out_ref, grad_ref, cos_ref, low_ref, high_ref,
    dq_ref, dk_ref, dv_ref, sums_ref, dq_acc, dk_acc, dv_acc,
):
    tokens = q_ref.shape[0]
    blocks = TILE // BLK
    dk_acc[...] = jnp.zeros_like(dk_acc)
    dv_acc[...] = jnp.zeros_like(dv_acc)
    for tile in range(tokens // TILE):
        first = tile * TILE // SEQ_LEN * SEQ_LEN
        last = (tile + 1) * TILE
        count = last - first
        places = [stored(place_ref, tile * blocks + part) for part in range(blocks)]
        query = q_ref[pl.ds(tile * TILE, TILE), :]
        keys = k_ref[pl.ds(first, count), :]
        values = v_ref[pl.ds(first, count), :]
        grad = jnp.concatenate([grad_ref[place, :] for place in places], 0)
        out = jnp.concatenate([out_ref[place, :] for place in places], 0)
        product = grad.astype(F32) * out.astype(F32)
        row = lax.broadcasted_iota(jnp.int32, (TILE, count), 0) + (tile * TILE - first)
        allowed = lax.broadcasted_iota(jnp.int32, (TILE, count), 1) <= row
        dq = jnp.zeros((TILE, 2 * HEAD_DIM), F32)
        for head in range(2):
            narrow = lane_mask(query.shape, head)
            mine = jnp.where(narrow, query, jnp.zeros_like(query))
            grad_mine = jnp.where(narrow, grad, jnp.zeros_like(grad))
            delta = jnp.sum(jnp.where(narrow, product, 0.0), axis=1, keepdims=True)
            total = total_ref[pl.ds(tile * TILE, TILE), pl.ds(head * HEAD_DIM, 1)]
            scores = jnp.where(allowed, dot(mine, keys, ((1,), (1,))), floor_score)
            weights = jnp.exp(scores - total)
            slope = dot(grad_mine, values, ((1,), (1,)))
            score_grad = (weights * (slope - delta)).astype(BF16)
            rounded = weights.astype(BF16)
            keys_mine = jnp.where(
                lane_mask(keys.shape, head), keys, jnp.zeros_like(keys)
            )
            dq = dq + dot(score_grad, keys_mine)
            dk_acc[pl.ds(first, count), :] += dot(score_grad, mine, ((0,), (0,)))
            dv_acc[pl.ds(first, count), :] += dot(rounded, grad_mine, ((0,), (0,)))
        dq_acc[pl.ds(tile * TILE, TILE), :] = dq * HEAD_DIM**-0.5
    sums = [jnp.zeros((1, 2 * HEAD_DIM), F32) for _ in range(3)]
    for p in range(tokens // BLK):
        here = pl.ds(p * BLK, BLK)
        there = stored(place_ref, p)
        cosine, low, high = cos_ref[there, :], -low_ref[there, :], -high_ref[there, :]
        for i, (acc, ref) in enumerate(((dq_acc, dq_ref), (dk_acc, dk_ref), (dv_acc, dv_ref))):
            part = acc[here, :]
            if i < 2:
                part = rotated(part, cosine, low, high)
            sums[i] = sums[i] + jnp.sum(part, axis=0, keepdims=True)
            ref[there, :] = part.astype(BF16)
    zero = jnp.zeros((5, 2 * HEAD_DIM), F32)
    sums_ref[...] = jnp.concatenate(sums + [zero], 0)


def attend(place, projected, tables, heads):
    tokens = projected.shape[0]
    pairs = heads // 2
    wide = 2 * HEAD_DIM

    def block(offset):
        return pl.BlockSpec((tokens, wide), lambda h, place: (0, h + offset))

    table = pl.BlockSpec((tokens, wide), lambda h, place: (0, 0))
    shape = (tokens, heads * HEAD_DIM)
    return pl.pallas_call(
        attend_kernel,
        grid_spec=pltpu.PrefetchScalarGridSpec(
            num_scalar_prefetch=1,
            grid=(pairs,),
            in_specs=[block(0), block(pairs), block(2 * pairs), table, table, table],
            out_specs=[block(0)] * 5,
        ),
        out_shape=[
            jax.ShapeDtypeStruct(shape, BF16),
            jax.ShapeDtypeStruct(shape, F32),
            jax.ShapeDtypeStruct(shape, BF16),
            jax.ShapeDtypeStruct(shape, BF16),
            jax.ShapeDtypeStruct(shape, BF16),
        ],
        compiler_params=pltpu.CompilerParams(vmem_limit_bytes=48 * 2**20),
        cost_estimate=pl.CostEstimate(
            flops=8 * tokens * tokens * wide * pairs, bytes_accessed=30 * tokens * wide * pairs,
            transcendentals=tokens * tokens * heads,
        ),
    )(place, projected, projected, projected, *tables)


def attend_back(place, query, keys, values, total, out, grad, tables, heads):
    tokens = query.shape[0]
    pairs = heads // 2
    wide = 2 * HEAD_DIM
    block = pl.BlockSpec((tokens, wide), lambda h, place: (0, h))
    table = pl.BlockSpec((tokens, wide), lambda h, place: (0, 0))
    shape = jax.ShapeDtypeStruct((tokens, heads * HEAD_DIM), BF16)
    return pl.pallas_call(
        attend_back_kernel,
        grid_spec=pltpu.PrefetchScalarGridSpec(
            num_scalar_prefetch=1,
            grid=(pairs,),
            in_specs=[block] * 6 + [table] * 3,
            out_specs=[block] * 3 + [pl.BlockSpec((8, wide), lambda h, place: (0, h))],
            scratch_shapes=[pltpu.VMEM((tokens, wide), F32)] * 3,
        ),
        out_shape=[shape] * 3 + [jax.ShapeDtypeStruct((8, heads * HEAD_DIM), F32)],
        compiler_params=pltpu.CompilerParams(vmem_limit_bytes=48 * 2**20),
        cost_estimate=pl.CostEstimate(
            flops=20 * tokens * tokens * wide * pairs, bytes_accessed=30 * tokens * wide * pairs,
            transcendentals=tokens * tokens * heads,
        ),
    )(place, query, keys, values, total, out, grad, *tables)


def causal_blocks(assignment):
    count = assignment.shape[0]
    number = jnp.arange(count, dtype=jnp.int32)
    return jnp.sum(jnp.where(assignment[None, :] == number[:, None], number[None, :], 0), axis=1)


def group_positions(positions, assignment, context, group):
    if group == SEQ_LEN:
        blocks_here = positions.shape[0] // BLK
        start = positions[0] - lax.dynamic_index_in_dim(
            assignment, context * blocks_here, 0, keepdims=False
        ) * BLK
        index = assignment[:, None] * BLK + jnp.arange(BLK, dtype=jnp.int32)[None, :]
        return start + index.reshape(group)
    return lax.all_gather(positions, "context", axis=0, tiled=True)


def rotary_tables(positions):
    half = ROT // 2
    lane = jnp.arange(2 * HEAD_DIM) % HEAD_DIM
    exponent = (lane % half).astype(F32)
    frequency = jnp.where(lane < ROT, 10000.0 ** (-2.0 * exponent / ROT), 0.0)
    angles = positions.astype(F32)[:, None] * frequency[None, :]
    cosine, sine = jnp.cos(angles), jnp.sin(angles)
    low = jnp.where(lane[None, :] < half, -sine, 0.0)
    high = jnp.where((lane[None, :] >= half) & (lane[None, :] < ROT), sine, 0.0)
    return cosine, low, high


def gelu_tanh(value):
    return jax.nn.gelu(value, approximate=True)


def gather_shard(x):
    return lax.all_gather(x, "shard", axis=0, tiled=True)


def scatter_shard(x):
    return lax.psum_scatter(x, "shard", scatter_dimension=0, tiled=True)


def gather_context(x):
    return lax.all_gather(x, "context", axis=0, tiled=True)


def scatter_context(x):
    return lax.psum_scatter(x, "context", scatter_dimension=0, tiled=True)


def local(
    block_input,
    input_weight,
    input_bias,
    output_weight,
    output_bias,
    norm_gain,
    norm_bias,
    assignment,
    positions,
    cotangent,
):
    tokens_here = block_input.shape[0]
    context_size = lax.axis_size("context")
    shard_size = lax.axis_size("shard")
    context = lax.axis_index("context")
    shard_here = lax.axis_index("shard")
    group = tokens_here * context_size
    heads = HEADS // context_size
    attn = heads * HEAD_DIM
    rows_here = input_weight.shape[0]
    inner, segments = column_plan(shard_size, context_size)
    attn_segments = [(base, width) for base, width in segments if base < D]
    hidden_segments = [(base, width) for base, width in segments if base >= D]
    qkv_columns = [(base + i * D, width) for i in range(3) for base, width in attn_segments]
    hidden_columns = [(base + 2 * D, width) for base, width in hidden_segments]

    small = jnp.concatenate(
        [input_bias, output_bias[0], output_bias[1], norm_gain, norm_bias], 0
    ).reshape(1, -1)
    small = gather_shard(small).astype(F32)
    cut = input_bias.shape[0]
    share = norm_gain.shape[0]
    bias_in = small[:, :cut].reshape(-1)
    bias_sum = (small[:, cut : cut + share] + small[:, cut + share : cut + 2 * share]).reshape(-1)
    gain = small[:, cut + 2 * share : cut + 3 * share].reshape(-1)
    shift = small[:, cut + 3 * share :].reshape(-1)

    weight_qkv = gather_shard(take(input_weight, qkv_columns, context, 1))
    weight_hidden = gather_shard(take(input_weight, hidden_columns, context, 1))
    if inner is not None:
        weight_out = gather_shard(take(output_weight, inner, context, 0))
    else:
        weight_out = take(gather_shard(output_weight), segments, context, 0)
    bias_qkv = take(bias_in, qkv_columns, context, 0)
    bias_hidden = take(bias_in, hidden_columns, context, 0)

    centred = block_input - jnp.mean(block_input, axis=1, keepdims=True)
    inverse_std = lax.rsqrt(jnp.mean(centred * centred, axis=1, keepdims=True) + epsilon)
    normalized = centred * inverse_std
    normed = gather_context((normalized * gain + shift).astype(BF16))
    upstream = gather_context(cotangent.astype(BF16))

    place = causal_blocks(assignment)
    tables = rotary_tables(group_positions(positions, assignment, context, group))

    projected = dot(normed, weight_qkv) + bias_qkv
    attended, log_total, query, keys, values = attend(place, projected, tables, heads)
    hidden_pre = dot(normed, weight_hidden) + bias_hidden
    activation = gelu_tanh(hidden_pre).astype(BF16)
    joined = jnp.concatenate([attended, activation], axis=1)
    partial_out = scatter_context(dot(joined, weight_out).astype(BF16))
    block_output = block_input + partial_out.astype(F32) + bias_sum

    attended_grad = dot(upstream, weight_out[:attn], ((1,), (1,))).astype(BF16)
    joined_grad = dot(upstream, weight_out[attn:], ((1,), (1,)))
    hidden_grad = jax.vjp(gelu_tanh, hidden_pre)[1](joined_grad)[0]
    hidden_rounded = hidden_grad.astype(BF16)
    hidden_sum = jnp.sum(hidden_grad, axis=0)
    dq, dk, dv, sums = attend_back(
        place, query, keys, values, log_total, attended, attended_grad, tables, heads
    )
    qkv_rounded = jnp.concatenate([dq, dk, dv], axis=1)
    normed_grad = dot(hidden_rounded, weight_hidden, ((1,), (1,))) + dot(
        qkv_rounded, weight_qkv, ((1,), (1,))
    )
    normed_grad = scatter_context(normed_grad.astype(BF16)).astype(F32)

    out_grad = dot(joined, upstream, ((0,), (0,))).astype(BF16)
    hidden_in_grad = scatter_shard(dot(normed, hidden_rounded, ((0,), (0,))).astype(BF16))
    qkv_in_grad = scatter_shard(dot(normed, qkv_rounded, ((0,), (0,))).astype(BF16))
    if inner is not None:
        out_grad = scatter_shard(out_grad)
        out_grad = gather_context(out_grad[None])
        weight_out_grad = untake(out_grad, inner, 0).astype(F32)
    else:
        whole = jnp.zeros((D + FF, D), BF16)
        at = 0
        for base, width in segments:
            whole = lax.dynamic_update_slice_in_dim(
                whole, out_grad[at : at + width], base + context * width, 0
            )
            at += width
        weight_out_grad = lax.psum(scatter_shard(whole), "context").astype(F32)
    hidden_in_grad = untake(gather_context(hidden_in_grad[None]), hidden_segments, 1)
    qkv_in_grad = gather_context(qkv_in_grad[None])
    qkv_in_grad = untake(qkv_in_grad, qkv_columns, 1)
    weight_in_grad = jnp.concatenate([qkv_in_grad, hidden_in_grad], 1).astype(F32)

    vectors = jnp.concatenate(
        [
            sums[0],
            sums[1],
            sums[2],
            hidden_sum,
            jnp.sum(cotangent, axis=0),
            jnp.sum(normed_grad * normalized, axis=0),
            jnp.sum(normed_grad, axis=0),
        ]
    )
    vectors = jnp.sum(gather_shard(vectors[None]), axis=0)
    vectors = gather_context(vectors[None])
    columns = 3 * attn + hidden_sum.shape[0]
    bias_in_sum = untake(vectors[:, :columns], qkv_columns + hidden_columns, 0)
    others = jnp.sum(vectors[:, columns:], axis=0)

    def own_share(vector):
        length = vector.shape[0] // shard_size
        return lax.dynamic_slice_in_dim(vector, shard_here * length, length, 0)

    bias_row = own_share(others[:D])
    scaled = normed_grad * gain
    input_grad = cotangent + inverse_std * (
        scaled
        - jnp.mean(scaled, axis=1, keepdims=True)
        - normalized * jnp.mean(scaled * normalized, axis=1, keepdims=True)
    )
    return (
        block_output,
        input_grad,
        weight_in_grad,
        own_share(bias_in_sum),
        weight_out_grad,
        jnp.stack([bias_row, bias_row]),
        own_share(others[D : 2 * D]),
        own_share(others[2 * D :]),
    )


def solution(mesh):
    return jax.shard_map(
        local,
        mesh=mesh,
        in_specs=(
            P(("shard", "context"), None),
            P("shard", None),
            P("shard"),
            P("shard", None),
            P(None, "shard"),
            P("shard"),
            P("shard"),
            P(),
            P(("shard", "context")),
            P(("shard", "context"), None),
        ),
        out_specs=(
            P(("shard", "context"), None),
            P(("shard", "context"), None),
            P("shard", None),
            P("shard"),
            P("shard", None),
            P(None, "shard"),
            P("shard"),
            P("shard"),
        ),
        check_vma=False,
    )
```

time: 2220 us -> 1020 us (0.46)
  waiting for transfers between devices: 1770 us -> 683 us
  matrix products: 254 us -> 132 us
  other arithmetic: 81.9 us -> 34.6 us
  Pallas kernels: 0 us -> 41.4 us
    psum x2 -> x0, waiting for transfers between devices: 524 us -> none  [the longest x1 426 us: local(): lax.psum(weight_in_grad.astype(jnp.bfloat16), 'context').astype(jnp.float32)]
    reduce_scatter x3 -> x5, waiting for transfers between devices: 568 us -> 246 us  [the longest x2 128 us: scatter_context(): return lax.psum_scatter(x, 'context', scatter_dimension=0, tiled=True)]
    unnamed x11 -> x13, waiting for transfers between devices: 152 us -> 0.85 us
    dot_general x34 -> x10, matrix products: 254 us -> 132 us  [dot(): return lax.dot_general(a, b, (dims, ((), ())), preferred_element_type=F32)]
    all_gather x4 -> x8, waiting for transfers between devices: 526 us -> 437 us  [the longest x5 311 us: gather_context(): return lax.all_gather(x, 'context', axis=0, tiled=True)]
    pallas_call x0 -> x2, Pallas kernels: none -> 41.4 us  [the longest x1 23.5 us: attend_back(): pl.pallas_call(attend_back_kernel, grid_spec=pltpu.PrefetchScalarGridSpec...]
  transfers between devices with their start and end apart: 10 -> 13, of which waited for: 10 -> 12; matrix products, arithmetic and copies ran while one was open for 12% -> 20% of each run, Pallas kernels for 0% -> 4%
where the time goes in v1:
time: 1020 us; the launch traced here: 1010 us
  waiting for transfers between devices  683 us (67%)
  matrix products  132 us (13%)
  local copies, waits for them, and re-layouts  68.8 us (7%)
  Pallas kernels  41.4 us (4%)
  blocking collectives  36.1 us (4%)
  other arithmetic  34.6 us (3%)
  between operations  16.1 us (2%)
    all_gather x5, waiting for transfers between devices, gather_context(): return lax.all_gather(x, 'context', axis=0, tiled=True)  311 us
    dot_general x10, matrix products, dot(): return lax.dot_general(a, b, (dims, ((), ())), preferred_element_type=F32)  132 us
    reduce_scatter x2, waiting for transfers between devices, scatter_context(): return lax.psum_scatter(x, 'context', scatter_dimension=0, tiled=True)  128 us
    all_gather x3, waiting for transfers between devices, gather_shard(): return lax.all_gather(x, 'shard', axis=0, tiled=True)  125 us
    reduce_scatter x3, waiting for transfers between devices, scatter_shard(): return lax.psum_scatter(x, 'shard', scatter_dimension=0, tiled=True)  118 us
    pallas_call x1, Pallas kernels, attend_back(): pl.pallas_call(attend_back_kernel, grid_spec=pltpu.PrefetchScalarGridSpec...  23.5 us
  transfers between devices with their start and end apart: 13, of which 12 were waited for; matrix products, arithmetic and copies ran while one was open for 20% of the time, Pallas kernels for 4%

profile of v1, /device:TPU:0, one launch (start us, length us, event | category | flops | bytes accessed | tf_op | source)
XLA Modules:
  0.0 1013.4 jit_solution(9652939925549805099)
XLA Ops:
  49.9 60.1 %all-gather.18.cloned.1.call-done = bf16[1024,2048]{1,0:T(8,128)(2,1)} async-done(((bf16[256,2048]{1,0:T(8,128)(2,1)}), bf16[1024,2048]{1,0:T(8,128)(2,1)}) %all-gather.18.cloned.1.call-update) | async-done | bytes 4194320 | tf_op jit(solution)/shard_map/all_gather | solution.py:280
  110.0 46.5 %all-gather.20.cloned.1.call-done = bf16[2048,1536]{1,0:T(8,128)(2,1)} async-done(((bf16[256,1536]{1,0:T(8,128)(2,1)}), bf16[2048,1536]{1,0:T(8,128)(2,1)}) %all-gather.20.cloned.1.call-update) | async-done | bytes 6291472 | tf_op jit(solution)/shard_map/all_gather | solution.py:272
  156.6 11.7 %convolution_add_fusion.q_ref.k_ref.v_ref = f32[1024,1536]{1,0:T(8,128)} fusion(bf16[1024,2048]{1,0:T(8,128)(2,1)} %all-gather.18.cloned.1.call-done, bf16[2048,1536]{1,0:T(8,128)(2,1)} %all-gather.20.cloned.1.call-done, f32[1536]{0:T(1024)S(1)} %concatenate.38), kind=kOutput, calls=%fused_computation.21 | convolution fusion | flops 6444023808 | bytes 16783360 | tf_op jit(solution)/shard_map/dot_general | solution.py:27
  168.2 17.9 %shard_map.161 = (bf16[1024,512]{1,0:T(8,128)(2,1)S(1)}, f32[1024,512]{1,0:T(8,128)}, bf16[1024,512]{1,0:T(8,128)(2,1)S(1)}, bf16[1024,512]{1,0:T(8,128)(2,1)S(1)}, bf16[1024,512]{1,0:T(8,128)(2,1)S(1)}) custom-call(s32[8]{0:T(128)S(1)} %select_reduce_fusion.place_ref, f32[1024,1536]{1,0:T(8,128)} %convolution_add_fusion.q_ref.k_ref.v_ref, ...), custom_call_target="tpu_custom_call" | custom-call | flops 4294967296 | bytes 15728640 | tf_op jit(solution)/shard_map/pallas_call | solution.py:190
  189.0 49.9 %all-gather.26.cloned.1.call-done = bf16[1024,2048]{1,0:T(8,128)(2,1)} async-done(((bf16[256,2048]{1,0:T(8,128)(2,1)}), bf16[1024,2048]{1,0:T(8,128)(2,1)}) %all-gather.26.cloned.1.call-update) | async-done | bytes 4194320 | tf_op jit(solution)/shard_map/all_gather | solution.py:280
  239.0 64.1 %all-gather.24.cloned.1.call-done = bf16[2560,2048]{1,0:T(8,128)(2,1)} async-done(((bf16[320,2048]{1,0:T(8,128)(2,1)}), bf16[2560,2048]{1,0:T(8,128)(2,1)}) %all-gather.24.cloned.1.call-update) | async-done | bytes 10485776 | tf_op jit(solution)/shard_map/all_gather | solution.py:272
  309.3 23.5 %shard_map.162 = (bf16[1024,512]{1,0:T(8,128)(2,1)S(1)}, bf16[1024,512]{1,0:T(8,128)(2,1)S(1)}, bf16[1024,512]{1,0:T(8,128)(2,1)S(1)}, f32[8,512]{1,0:T(8,128)S(1)}) custom-call(s32[8]{0:T(128)S(1)} %select_reduce_fusion.place_ref, bf16[1024,512]{1,0:T(8,128)(2,1)S(1)} %get-tuple-element.18.q_ref, bf16[1024,512]{1,0:T(8,128)(2,1)} %copy-done.2, ...), custom_call_target="tpu_custom_call" | custom-call | flops 10737418240 | bytes 15728640 | tf_op jit(solution)/shard_map/pallas_call | solution.py:220
  345.2 14.6 %all-gather.22.cloned.1.call-done = bf16[2048,2048]{1,0:T(8,128)(2,1)} async-done(((bf16[256,2048]{1,0:T(8,128)(2,1)}), bf16[2048,2048]{1,0:T(8,128)(2,1)}) %all-gather.22.cloned.1.call-update) | async-done | bytes 8388624 | tf_op jit(solution)/shard_map/all_gather | solution.py:272
  359.8 16.0 %multiply_convert_fusion = (bf16[1024,2048]{1,0:T(8,128)(2,1)}, f32[1024,2048]{1,0:T(8,128)S(1)}) fusion(f32[2048]{0:T(1024)S(1)} %concatenate.40, bf16[1024,2048]{1,0:T(8,128)(2,1)} %all-gather.18.cloned.1.call-done, bf16[2048,2048]{1,0:T(8,128)(2,1)} %all-gather.22.cloned.1.call-done), kind=kOutput, calls=%fused_computation.17 | convolution fusion | flops 8610906112 | bytes 25174016 | tf_op jit(solution)/shard_map/dot_general | solution.py:27
  375.9 18.1 %fusion.65 = (f32[2048]{0:T(1024)S(1)}, bf16[1024,2048]{1,0:T(8,128)(2,1)}) fusion(f32[1024,2048]{1,0:T(8,128)S(1)} %get-tuple-element.269, f32[2048]{0:T(1024)S(1)} %concatenate.40, bf16[1024,2048]{1,0:T(8,128)(2,1)S(1)} %copy-done.30, bf16[2560,2048]{1,0:T(8,128)(2,1)} %all-gather.24.cloned.1.call-done), kind=kOutput, calls=%fused_computation.187 | convolution fusion | flops 8636069888 | bytes 25182208 | tf_op jit(solution)/shard_map/dot_general | solution.py:27
  394.0 13.7 %convolution_convert_fusion.1 = bf16[2048,2048]{1,0:T(8,128)(2,1)} fusion(bf16[1024,2048]{1,0:T(8,128)(2,1)S(1)} %copy-done.29, bf16[1024,2048]{1,0:T(8,128)(2,1)} %get-tuple-element.271), kind=kOutput, calls=%fused_computation.18 | convolution fusion | flops 8594128896 | bytes 16777216 | tf_op jit(solution)/shard_map/dot_general | solution.py:27
  408.9 16.4 %convolution_convert_fusion = bf16[2560,2048]{1,0:T(8,128)(2,1)} fusion(bf16[1024,2048]{1,0:T(8,128)(2,1)} %all-gather.26.cloned.1.call-done, bf16[1024,2048]{1,0:T(8,128)(2,1)} %get-tuple-element.268, bf16[1024,512]{1,0:T(8,128)(2,1)S(1)} %copy-done.1), kind=kOutput, calls=%fused_computation.2 | convolution fusion | flops 10753146880 | bytes 19922944 | tf_op jit(solution)/shard_map/dot_general | solution.py:27
  425.4 12.9 %fusion.24 = f32[1024,2048]{1,0:T(8,128)S(1)} fusion(bf16[2048,2048]{1,0:T(8,128)(2,1)} %all-gather.22.cloned.1.call-done, bf16[1024,2048]{1,0:T(8,128)(2,1)} %get-tuple-element.271), kind=kOutput, calls=%fused_computation.37 | convolution fusion | flops 8589934592 | bytes 20971520 | tf_op jit(solution)/shard_map/dot_general | solution.py:27
  438.4 12.3 %add_convert_fusion = bf16[1024,2048]{1,0:T(8,128)(2,1)} fusion(f32[1024,2048]{1,0:T(8,128)S(1)} %fusion.24, bf16[1024,1536]{1,0:T(8,128)(2,1)S(1)} %copy-done.12, bf16[2048,1536]{1,0:T(8,128)(2,1)} %all-gather.20.cloned.1.call-done), kind=kOutput, calls=%fused_computation.16 | convolution fusion | flops 6446645248 | bytes 22020096 | tf_op jit(solution)/shard_map/dot_general | solution.py:27
  450.7 16.4 %convolution_convert_fusion.3 = bf16[1024,2048]{1,0:T(8,128)(2,1)} fusion(bf16[2560,2048]{1,0:T(8,128)(2,1)} %all-gather.24.cloned.1.call-done, bf16[1024,2048]{1,0:T(8,128)(2,1)} %get-tuple-element.268, bf16[1024,512]{1,0:T(8,128)(2,1)S(1)} %copy-done.1), kind=kOutput, calls=%fused_computation.22 | convolution fusion | flops 10750001152 | bytes 19922944 | tf_op jit(solution)/shard_map/dot_general | solution.py:27
  467.9 32.7 %reduce-scatter.12.cloned.1.call-done = bf16[256,2048]{1,0:T(8,128)(2,1)} async-done(((bf16[2048,2048]{1,0:T(8,128)(2,1)}), bf16[256,2048]{1,0:T(8,128)(2,1)}) %reduce-scatter.12.cloned.1.call-update) | async-done | bytes 1048592 | tf_op jit(solution)/shard_map/reduce_scatter | solution.py:276
  500.7 85.6 %reduce-scatter.14.cloned.1.call-done = bf16[320,2048]{1,0:T(8,128)(2,1)} async-done(((bf16[2560,2048]{1,0:T(8,128)(2,1)}), bf16[320,2048]{1,0:T(8,128)(2,1)}) %reduce-scatter.14.cloned.1.call-update) | async-done | bytes 1310736 | tf_op jit(solution)/shard_map/reduce_scatter | solution.py:276
  586.4 78.9 %reduce-scatter.8.cloned.1.call-done = bf16[256,2048]{1,0:T(8,128)(2,1)} async-done(((bf16[1024,2048]{1,0:T(8,128)(2,1)}), bf16[256,2048]{1,0:T(8,128)(2,1)}) %reduce-scatter.8.cloned.1.call-update) | async-done | bytes 1048592 | tf_op jit(solution)/shard_map/reduce_scatter | solution.py:284
  677.4 16.0 %all-gather.8 = f32[4,1,9728]{2,1,0:T(1,128)S(1)} all-gather(f32[1,1,9728]{2,1,0:T(1,128)S(1)} %reshape.232), channel_id=6, replica_groups=mesh['shard'=8,'context'=4] {'context'}, dimensions={0}, use_global_device_ids=true | all-gather | bytes 194560 | tf_op jit(solution)/shard_map/all_gather | solution.py:280
  698.6 48.8 %reduce-scatter.6.cloned.1.call-done = bf16[256,2048]{1,0:T(8,128)(2,1)} async-done(((bf16[1024,2048]{1,0:T(8,128)(2,1)}), bf16[256,2048]{1,0:T(8,128)(2,1)}) %reduce-scatter.6.cloned.1.call-update) | async-done | bytes 1048592 | tf_op jit(solution)/shard_map/reduce_scatter | solution.py:284
  752.2 60.7 %all-gather.28.cloned.1.call-done = bf16[1024,1536]{1,0:T(8,128)(2,1)} async-done(((bf16[256,1536]{1,0:T(8,128)(2,1)}), bf16[1024,1536]{1,0:T(8,128)(2,1)}) %all-gather.28.cloned.1.call-update) | async-done | bytes 3145744 | tf_op jit(solution)/shard_map/all_gather | solution.py:280
  819.5 74.3 %all-gather.30.cloned.1.call-done = bf16[1024,2048]{1,0:T(8,128)(2,1)} async-done(((bf16[256,2048]{1,0:T(8,128)(2,1)}), bf16[1024,2048]{1,0:T(8,128)(2,1)}) %all-gather.30.cloned.1.call-update) | async-done | bytes 4194320 | tf_op jit(solution)/shard_map/all_gather | solution.py:280
  902.9 12.5 %concatenate.44 = bf16[256,14336]{1,0:T(8,128)(2,1)} concatenate(bf16[256,192]{1,0:T(8,128)(2,1)S(1)} %get-tuple-element.140, bf16[256,192]{1,0:T(8,128)(2,1)S(1)} %get-tuple-element.139, bf16[256,192]{1,0:T(8,128)(2,1)S(1)} %get-tuple-element.138, bf16[256,192]{1,0:T(8,128)(2,1)S(1)} %get-tuple-element.141, bf16[256,128]{1,0:T(8,128)(2,1)} %get-tuple-element.136, ...), dimensions={1} | concatenate | bytes 14680064 | tf_op jit(solution)/shard_map/concatenate | solution.py:384
  925.8 66.2 %all-gather.32.cloned.1.call-done = bf16[1280,2048]{1,0:T(8,128)(2,1)} async-done(((bf16[320,2048]{1,0:T(8,128)(2,1)}), bf16[1280,2048]{1,0:T(8,128)(2,1)}) %all-gather.32.cloned.1.call-update) | async-done | bytes 5242896 | tf_op jit(solution)/shard_map/all_gather | solution.py:280
  (188 shorter events, 127.4 us)
Async XLA Ops:
  7.2 20.2 %copy-start.4 = (f32[256,2048]{1,0:T(8,128)S(1)}, f32[256,2048]{1,0:T(8,128)}, u32[]{:S(2)}) copy-start(f32[256,2048]{1,0:T(8,128)} %param.10) | copy-start | bytes 6291460
  7.2 102.9 %all-gather.18.cloned.1.call-start = ((), (), s32[]{:S(2)}) async-start(), calls=%async_computation.5 | async-start | bytes 5242880 | tf_op jit(solution)/shard_map/all_gather | solution.py:280
  28.8 127.8 %all-gather.20.cloned.1.call-start = ((), (), s32[]{:S(2)}) async-start(), calls=%async_computation.6 | async-start | bytes 7077888 | tf_op jit(solution)/shard_map/all_gather | solution.py:272
  36.3 202.7 %all-gather.26.cloned.1.call-start = ((), (), s32[]{:S(2)}) async-start(), calls=%async_computation.10 | async-start | bytes 5242880 | tf_op jit(solution)/shard_map/all_gather | solution.py:280
  38.1 265.0 %all-gather.24.cloned.1.call-start = ((), (), s32[]{:S(2)}) async-start(), calls=%async_computation.8 | async-start | bytes 11796480 | tf_op jit(solution)/shard_map/all_gather | solution.py:272
  41.7 318.1 %all-gather.22.cloned.1.call-start = ((), (), s32[]{:S(2)}) async-start(), calls=%async_computation.7 | async-start | bytes 9437184 | tf_op jit(solution)/shard_map/all_gather | solution.py:272
  44.7 422.5 %reduce-scatter.10.cloned.1.call-start = ((), (), s32[]{:S(2)}) async-start(), calls=%async_computation.12 | async-start | bytes 7077888 | tf_op jit(solution)/shard_map/reduce_scatter | solution.py:276
  345.1 155.5 %reduce-scatter.12.cloned.1.call-start = ((), (), s32[]{:S(2)}) async-start(), calls=%async_computation.13 | async-start | bytes 9437184 | tf_op jit(solution)/shard_map/reduce_scatter | solution.py:276
  359.8 16.0 %copy-start.30 = (bf16[1024,2048]{1,0:T(8,128)(2,1)S(1)}, bf16[1024,2048]{1,0:T(8,128)(2,1)}, u32[]{:S(2)}) copy-start(bf16[1024,2048]{1,0:T(8,128)(2,1)} %all-gather.26.cloned.1.call-done) | copy-start | bytes 12582916
  375.9 18.1 %copy-start.29 = (bf16[1024,2048]{1,0:T(8,128)(2,1)S(1)}, bf16[1024,2048]{1,0:T(8,128)(2,1)}, u32[]{:S(2)}) copy-start(bf16[1024,2048]{1,0:T(8,128)(2,1)} %all-gather.18.cloned.1.call-done) | copy-start | bytes 12582916
  407.7 178.5 %reduce-scatter.14.cloned.1.call-start = ((), (), s32[]{:S(2)}) async-start(), calls=%async_computation.14 | async-start | bytes 11796480 | tf_op jit(solution)/shard_map/reduce_scatter | solution.py:276
  425.4 239.9 %reduce-scatter.8.cloned.1.call-start = ((), (), s32[]{:S(2)}) async-start(), calls=%async_computation.11 | async-start | bytes 5242880 | tf_op jit(solution)/shard_map/reduce_scatter | solution.py:284
  425.4 12.9 %copy-start.12 = (bf16[1024,1536]{1,0:T(8,128)(2,1)S(1)}, bf16[1024,1536]{1,0:T(8,128)(2,1)}, u32[]{:S(2)}) copy-start(bf16[1024,1536]{1,0:T(8,128)(2,1)} %copy-done.11) | copy-start | bytes 9437188
  450.6 296.7 %reduce-scatter.6.cloned.1.call-start = ((), (), s32[]{:S(2)}) async-start(), calls=%async_computation.9 | async-start | bytes 5242880 | tf_op jit(solution)/shard_map/reduce_scatter | solution.py:284
  467.1 119.2 %copy-start.23 = (f32[1,2,8,128]{3,2,1,0:T(8,128)S(1)}, f32[1,2,8,128]{3,2,1,0:T(8,128)}, u32[]{:S(2)}) copy-start(f32[1,2,8,128]{3,2,1,0:T(8,128)} %get-tuple-element.234) | copy-start | bytes 24580
  467.1 119.3 %copy-start.22 = (f32[2048]{0:T(1024)S(1)}, f32[2048]{0:T(1024)}, u32[]{:S(2)}) copy-start(f32[2048]{0:T(1024)} %get-tuple-element.142) | copy-start | bytes 24580
  467.1 198.3 %copy-start.5 = (f32[256,2048]{1,0:T(8,128)S(1)}, f32[256,2048]{1,0:T(8,128)}, u32[]{:S(2)}) copy-start(f32[256,2048]{1,0:T(8,128)} %param.10) | copy-start | bytes 6291460
  467.1 198.3 %copy-start.21 = (f32[1,2,8,128]{3,1,2,0:T(2,128)S(1)}, f32[1,2,8,128]{3,1,2,0:T(2,128)}, u32[]{:S(2)}) copy-start(f32[1,2,8,128]{3,1,2,0:T(2,128)} %copy-done.20) | copy-start | bytes 24580
  467.1 198.2 %copy-start.25 = (f32[256]{0:T(256)S(1)}, f32[256]{0:T(256)}, u32[]{:S(2)}) copy-start(f32[256]{0:T(256)} %copy-done.24) | copy-start | bytes 3076
  467.1 198.2 %copy-start.27 = (f32[256]{0:T(256)S(1)}, f32[256]{0:T(256)}, u32[]{:S(2)}) copy-start(f32[256]{0:T(256)} %copy-done.26) | copy-start | bytes 3076
  467.1 345.8 %all-gather.28.cloned.1.call-start = ((), (), s32[]{:S(2)}) async-start(), calls=%async_computation.15 | async-start | bytes 3932160 | tf_op jit(solution)/shard_map/all_gather | solution.py:280
  467.9 425.9 %all-gather.30.cloned.1.call-start = ((), (), s32[]{:S(2)}) async-start(), calls=%async_computation.16 | async-start | bytes 5242880 | tf_op jit(solution)/shard_map/all_gather | solution.py:280
  500.6 491.4 %all-gather.32.cloned.1.call-start = ((), (), s32[]{:S(2)}) async-start(), calls=%async_computation.17 | async-start | bytes 6553600 | tf_op jit(solution)/shard_map/all_gather | solution.py:280
  665.3 82.0 %copy-start.8 = (bf16[256,2048]{1,0:T(8,128)(2,1)S(1)}, bf16[256,2048]{1,0:T(8,128)(2,1)}, u32[]{:S(2)}) copy-start(bf16[256,2048]{1,0:T(8,128)(2,1)} %reduce-scatter.8.cloned.1.call-done) | copy-start | bytes 3145732
  (22 other events, 93.0 us)
Sparse Core Ops, SparseCore 0:
  28.9 81.0 all-gather.17
  112.5 44.0 all-gather.19
  158.2 80.7 all-gather.25
  241.3 61.7 all-gather.23
  305.4 54.3 all-gather.21
  363.1 61.7 reduce-scatter.9
  429.3 71.2 reduce-scatter.11
  504.7 81.5 reduce-scatter.13
  588.5 76.7 reduce-scatter.7
  667.6 79.7 reduce-scatter.5
  749.0 63.9 all-gather.27
  814.3 79.3 all-gather.29
  895.4 96.5 all-gather.31

commit v2 on v1

--- a/solution.py
+++ b/solution.py
@@ -277,11 +277,40 @@
 
 
 def gather_context(x):
-    return lax.all_gather(x, "context", axis=0, tiled=True)
+    n = lax.axis_size("context")
+    context = lax.axis_index("context")
+    right = left = x
+    before, after = [], []
+    for t in range(1, n):
+        right = lax.ppermute(right, "context", [(a, a + 1) for a in range(t - 1, n - 1)])
+        left = lax.ppermute(left, "context", [(a, a - 1) for a in range(n - t, 0, -1)])
+        before.append(right)
+        after.append(left)
+    rows = x.shape[0]
+    line = jnp.concatenate(before[::-1] + [x] + after, 0)
+    return lax.dynamic_slice_in_dim(line, (n - 1 - context) * rows, n * rows, 0)
 
 
 def scatter_context(x):
-    return lax.psum_scatter(x, "context", scatter_dimension=0, tiled=True)
+    n = lax.axis_size("context")
+    context = lax.axis_index("context")
+    rows = x.shape[0] // n
+
+    def block(j):
+        start = jnp.clip(j, 0, n - 1) * rows
+        return lax.dynamic_slice_in_dim(x, start, rows, 0)
+
+    def add(mine, received):
+        return (mine.astype(F32) + received.astype(F32)).astype(BF16)
+
+    right = left = None
+    for t in range(1, n):
+        to_right, to_left = block(n - t + context), block(context - (n - t))
+        if t > 1:
+            to_right, to_left = add(to_right, right), add(to_left, left)
+        right = lax.ppermute(to_right, "context", [(a, a + 1) for a in range(t)])
+        left = lax.ppermute(to_left, "context", [(n - 1 - a, n - 2 - a) for a in range(t)])
+    return block(context).astype(F32) + right.astype(F32) + left.astype(F32)
 
 
 def local(
@@ -346,7 +375,7 @@
     activation = gelu_tanh(hidden_pre).astype(BF16)
     joined = jnp.concatenate([attended, activation], axis=1)
     partial_out = scatter_context(dot(joined, weight_out).astype(BF16))
-    block_output = block_input + partial_out.astype(F32) + bias_sum
+    block_output = block_input + partial_out + bias_sum
 
     attended_grad = dot(upstream, weight_out[:attn], ((1,), (1,))).astype(BF16)
     joined_grad = dot(upstream, weight_out[attn:], ((1,), (1,)))
@@ -360,7 +389,7 @@
     normed_grad = dot(hidden_rounded, weight_hidden, ((1,), (1,))) + dot(
         qkv_rounded, weight_qkv, ((1,), (1,))
     )
-    normed_grad = scatter_context(normed_grad.astype(BF16)).astype(F32)
+    normed_grad = scatter_context(normed_grad.astype(BF16))
 
     out_grad = dot(joined, upstream, ((0,), (0,))).astype(BF16)
     hidden_in_grad = scatter_shard(dot(normed, hidden_rounded, ((0,), (0,))).astype(BF16))
@@ -395,7 +424,7 @@
         ]
     )
     vectors = jnp.sum(gather_shard(vectors[None]), axis=0)
-    vectors = gather_context(vectors[None])
+    vectors = lax.all_gather(vectors, "context")
     columns = 3 * attn + hidden_sum.shape[0]
     bias_in_sum = untake(vectors[:, :columns], qkv_columns + hidden_columns, 0)
     others = jnp.sum(vectors[:, columns:], axis=0)

time: 1020 us -> 792 us (0.78)
  waiting for transfers between devices: 683 us -> 283 us
  starting transfers between devices: 0.7 us -> 97.3 us
  local copies, waits for them, and re-layouts: 68.8 us -> 97.9 us
  blocking collectives: 36.1 us -> 57.5 us
  other arithmetic: 34.6 us -> 49.4 us
    all_gather x5 -> x0, waiting for transfers between devices: 311 us -> none  [gather_context(): return lax.all_gather(x, 'context', axis=0, tiled=True)]
    ppermute x0 -> x42, waiting for transfers between devices: none -> 283 us  [the longest x15 156 us: gather_context(): lax.ppermute(left, 'context', [(a, a - 1) for a in range(n - t, 0, -1)])]
    reduce_scatter x2 -> x0, waiting for transfers between devices: 128 us -> none  [scatter_context(): return lax.psum_scatter(x, 'context', scatter_dimension=0, tiled=True)]
    all_gather x3, waiting for transfers between devices: 125 us -> 0.01 us  [gather_shard(): return lax.all_gather(x, 'shard', axis=0, tiled=True)]
    reduce_scatter x3, waiting for transfers between devices: 118 us -> 0.01 us  [scatter_shard(): return lax.psum_scatter(x, 'shard', scatter_dimension=0, tiled=True)]
    ppermute x0 -> x42, starting transfers between devices: none -> 97 us  [the longest x15 43.6 us: gather_context(): lax.ppermute(right, 'context', [(a, a + 1) for a in range(t - 1, n - 1)])]
    unnamed x93 -> x132, local copies, waits for them, and re-layouts: 19.2 us -> 47.7 us
    all_gather x1, blocking collectives: 16 us -> 37.3 us  [local(): vectors = lax.all_gather(vectors, 'context')]
  transfers between devices with their start and end apart: 13 -> 48, of which waited for: 12 -> 21; matrix products, arithmetic and copies ran while one was open for 20% -> 34% of each run, Pallas kernels for 4% -> 5%
where the time goes in v2:
time: 792 us; the launch traced here: 782 us
  waiting for transfers between devices  283 us (36%)
  matrix products  138 us (17%)
  local copies, waits for them, and re-layouts  97.9 us (12%)
  starting transfers between devices  97.3 us (12%)
  blocking collectives  57.5 us (7%)
  other arithmetic  49.4 us (6%)
  Pallas kernels  41.6 us (5%)
  between operations  16.8 us (2%)
    ppermute x15, waiting for transfers between devices, gather_context(): lax.ppermute(left, 'context', [(a, a - 1) for a in range(n - t, 0, -1)])  156 us
    dot_general x10, matrix products, dot(): return lax.dot_general(a, b, (dims, ((), ())), preferred_element_type=F32)  138 us
    ppermute x15, waiting for transfers between devices, gather_context(): lax.ppermute(right, 'context', [(a, a + 1) for a in range(t - 1, n - 1)])  71.1 us
    ppermute x6, waiting for transfers between devices, scatter_context(): right = lax.ppermute(to_right, 'context', [(a, a + 1) for a in range(t)])  48.9 us
    unnamed x132, local copies, waits for them, and re-layouts  47.7 us
    ppermute x15, starting transfers between devices, gather_context(): lax.ppermute(right, 'context', [(a, a + 1) for a in range(t - 1, n - 1)])  43.6 us
    all_gather x1, blocking collectives, local(): vectors = lax.all_gather(vectors, 'context')  37.3 us
    ppermute x6, starting transfers between devices, scatter_context(): right = lax.ppermute(to_right, 'context', [(a, a + 1) for a in range(t)])  25.6 us
  transfers between devices with their start and end apart: 48, of which 21 were waited for; matrix products, arithmetic and copies ran while one was open for 34% of the time, Pallas kernels for 5%

profile of v2, /device:TPU:0, one launch (start us, length us, event | category | flops | bytes accessed | tf_op | source)
XLA Modules:
  0.0 782.0 jit_solution(16888248702335894750)
XLA Ops:
  44.0 16.9 %collective-permute-done = bf16[256,2048]{1,0:T(8,128)(2,1)} collective-permute-done((bf16[256,2048]{1,0:T(8,128)(2,1)}, bf16[256,2048]{1,0:T(8,128)(2,1)}, u32[]{:S(2)}, u32[]{:S(2)}) %collective-permute-start) | collective-permute-done | bytes 1048608 | tf_op jit(solution)/shard_map/ppermute | solution.py:285
  62.5 20.1 %collective-permute-done.12 = bf16[256,2048]{1,0:T(8,128)(2,1)S(1)} collective-permute-done((bf16[256,2048]{1,0:T(8,128)(2,1)S(1)}, bf16[256,2048]{1,0:T(8,128)(2,1)S(1)}, u32[]{:S(2)}, u32[]{:S(2)}) %collective-permute-start.12) | collective-permute-done | bytes 1048608 | tf_op jit(solution)/shard_map/ppermute | solution.py:285
  97.8 21.3 %collective-permute-done.4 = bf16[256,2048]{1,0:T(8,128)(2,1)} collective-permute-done((bf16[256,2048]{1,0:T(8,128)(2,1)}, bf16[256,2048]{1,0:T(8,128)(2,1)}, u32[]{:S(2)}, u32[]{:S(2)}) %collective-permute-start.4) | collective-permute-done | bytes 1048608 | tf_op jit(solution)/shard_map/ppermute | solution.py:286
  120.4 21.2 %collective-permute-done.16 = bf16[256,2048]{1,0:T(8,128)(2,1)} collective-permute-done((bf16[256,2048]{1,0:T(8,128)(2,1)}, bf16[256,2048]{1,0:T(8,128)(2,1)}, u32[]{:S(2)}, u32[]{:S(2)}) %collective-permute-start.16) | collective-permute-done | bytes 1048608 | tf_op jit(solution)/shard_map/ppermute | solution.py:286
  164.1 20.4 %collective-permute-done.17 = bf16[256,2048]{1,0:T(8,128)(2,1)S(1)} collective-permute-done((bf16[256,2048]{1,0:T(8,128)(2,1)}, bf16[256,2048]{1,0:T(8,128)(2,1)S(1)}, u32[]{:S(2)}, u32[]{:S(2)}) %collective-permute-start.17) | collective-permute-done | bytes 1048608 | tf_op jit(solution)/shard_map/ppermute | solution.py:286
  197.2 17.9 %shard_map.161 = (bf16[1024,512]{1,0:T(8,128)(2,1)S(1)}, f32[1024,512]{1,0:T(8,128)}, bf16[1024,512]{1,0:T(8,128)(2,1)S(1)}, bf16[1024,512]{1,0:T(8,128)(2,1)S(1)}, bf16[1024,512]{1,0:T(8,128)(2,1)S(1)}) custom-call(s32[8]{0:T(128)S(1)} %select_reduce_fusion.place_ref, f32[1024,1536]{1,0:T(8,128)} %convolution_add_fusion.q_ref.k_ref.v_ref, ...), custom_call_target="tpu_custom_call" | custom-call | flops 4294967296 | bytes 15728640 | tf_op jit(solution)/shard_map/pallas_call | solution.py:190
  224.2 23.7 %shard_map.162 = (bf16[1024,512]{1,0:T(8,128)(2,1)S(1)}, bf16[1024,512]{1,0:T(8,128)(2,1)S(1)}, bf16[1024,512]{1,0:T(8,128)(2,1)S(1)}, f32[8,512]{1,0:T(8,128)S(1)}) custom-call(s32[8]{0:T(128)S(1)} %select_reduce_fusion.place_ref, bf16[1024,512]{1,0:T(8,128)(2,1)S(1)} %get-tuple-element.18.q_ref, bf16[1024,512]{1,0:T(8,128)(2,1)} %copy-done.2, ...), custom_call_target="tpu_custom_call" | custom-call | flops 10737418240 | bytes 15728640 | tf_op jit(solution)/shard_map/pallas_call | solution.py:220
  261.0 17.4 %multiply_convert_fusion = (bf16[1024,2048]{1,0:T(8,128)(2,1)}, f32[1024,2048]{1,0:T(8,128)}) fusion(f32[2048]{0:T(1024)S(1)} %concatenate.56, bf16[2048,2048]{1,0:T(8,128)(2,1)} %all-gather.12.cloned.1.call-done, bf16[1792,2048]{1,0:T(8,128)(2,1)} %copy-done.20, s32[]{:T(128)S(6)} %select_n.192), kind=kOutput, calls=%fused_computation.12 | convolution fusion | flops 8610906112 | bytes 25174020 | tf_op jit(solution)/shard_map/dot_general | solution.py:27
  278.4 21.4 %fusion.77 = (f32[2048]{0:T(1024)S(1)}, bf16[1024,2048]{1,0:T(8,128)(2,1)}) fusion(f32[1024,2048]{1,0:T(8,128)} %get-tuple-element.286, f32[2048]{0:T(1024)S(1)} %concatenate.56, bf16[2560,2048]{1,0:T(8,128)(2,1)} %all-gather.14.cloned.1.call-done, bf16[1792,2048]{1,0:T(8,128)(2,1)} %constant_dynamic-update-slice_fusion.7, s32[]{:T(128)S(6)} %select_n.192), kind=kOutput, calls=%fused_computation.254 | convolution fusion | flops 8636069888 | bytes 25182212 | tf_op jit(solution)/shard_map/dot_general | solution.py:27
  299.8 13.4 %convolution_convert_fusion.1 = bf16[2048,2048]{1,0:T(8,128)(2,1)} fusion(bf16[1792,2048]{1,0:T(8,128)(2,1)S(1)} %bitcast.233, s32[]{:T(128)S(6)} %select_n.192, bf16[1024,2048]{1,0:T(8,128)(2,1)} %get-tuple-element.288), kind=kOutput, calls=%fused_computation.13 | convolution fusion | flops 8594128896 | bytes 16777220 | tf_op jit(solution)/shard_map/dot_general | solution.py:27
  314.4 16.8 %convolution_convert_fusion = bf16[2560,2048]{1,0:T(8,128)(2,1)} fusion(bf16[1024,2048]{1,0:T(8,128)(2,1)} %get-tuple-element.285, bf16[1024,512]{1,0:T(8,128)(2,1)S(1)} %copy-done.1, bf16[1792,2048]{1,0:T(8,128)(2,1)} %constant_dynamic-update-slice_fusion.7, s32[]{:T(128)S(6)} %select_n.192), kind=kOutput, calls=%fused_computation.2 | convolution fusion | flops 10753146880 | bytes 19922948 | tf_op jit(solution)/shard_map/dot_general | solution.py:27
  331.3 15.0 %fusion.21 = f32[1024,2048]{1,0:T(8,128)} fusion(bf16[2048,2048]{1,0:T(8,128)(2,1)} %all-gather.12.cloned.1.call-done, bf16[1024,2048]{1,0:T(8,128)(2,1)} %get-tuple-element.288), kind=kOutput, calls=%fused_computation.37 | convolution fusion | flops 8589934592 | bytes 20971520 | tf_op jit(solution)/shard_map/dot_general | solution.py:27
  346.3 12.0 %add_convert_fusion = bf16[1024,2048]{1,0:T(8,128)(2,1)S(1)} fusion(f32[1024,2048]{1,0:T(8,128)} %fusion.21, bf16[1024,1536]{1,0:T(8,128)(2,1)S(1)} %copy-done.17, bf16[2048,1536]{1,0:T(8,128)(2,1)} %all-gather.10.cloned.1.call-done), kind=kOutput, calls=%fused_computation.11 | convolution fusion | flops 6446645248 | bytes 22020096 | tf_op jit(solution)/shard_map/dot_general | solution.py:27
  362.1 13.3 %convolution_convert_fusion.3 = bf16[1024,2048]{1,0:T(8,128)(2,1)S(1)} fusion(bf16[2560,2048]{1,0:T(8,128)(2,1)S(1)} %bitcast.290, bf16[1024,2048]{1,0:T(8,128)(2,1)} %get-tuple-element.285, bf16[1024,512]{1,0:T(8,128)(2,1)S(1)} %copy-done.1), kind=kOutput, calls=%fused_computation.17 | convolution fusion | flops 10750001152 | bytes 19922944 | tf_op jit(solution)/shard_map/dot_general | solution.py:27
  394.2 13.9 %collective-permute-done.6 = bf16[256,2048]{1,0:T(8,128)(2,1)} collective-permute-done((bf16[256,2048]{1,0:T(8,128)(2,1)S(1)}, bf16[256,2048]{1,0:T(8,128)(2,1)}, u32[]{:S(2)}, u32[]{:S(2)}) %collective-permute-start.6) | collective-permute-done | bytes 1048608 | tf_op jit(solution)/shard_map/ppermute | solution.py:311
  416.6 14.1 %collective-permute-done.19 = bf16[256,2048]{1,0:T(8,128)(2,1)} collective-permute-done((bf16[256,2048]{1,0:T(8,128)(2,1)}, bf16[256,2048]{1,0:T(8,128)(2,1)}, u32[]{:S(2)}, u32[]{:S(2)}) %collective-permute-start.19) | collective-permute-done | bytes 1048608 | tf_op jit(solution)/shard_map/ppermute | solution.py:311
  441.3 11.8 %collective-permute-done.7 = bf16[256,2048]{1,0:T(8,128)(2,1)} collective-permute-done((bf16[256,2048]{1,0:T(8,128)(2,1)}, bf16[256,2048]{1,0:T(8,128)(2,1)}, u32[]{:S(2)}, u32[]{:S(2)}) %collective-permute-start.7) | collective-permute-done | bytes 1048608 | tf_op jit(solution)/shard_map/ppermute | solution.py:311
  495.0 37.3 %all-gather.5 = f32[4,1,9728]{2,1,0:T(1,128)S(1)} all-gather(f32[1,1,9728]{2,1,0:T(1,128)S(1)} %reshape.213), channel_id=4, replica_groups=mesh['shard'=8,'context'=4] {'context'}, dimensions={0}, use_global_device_ids=true | all-gather | bytes 194560 | tf_op jit(solution)/shard_map/all_gather | solution.py:427
  539.7 12.2 %collective-permute-done.24 = bf16[1,256,1536]{2,1,0:T(8,128)(2,1)S(1)} collective-permute-done((bf16[1,256,1536]{2,1,0:T(8,128)(2,1)}, bf16[1,256,1536]{2,1,0:T(8,128)(2,1)S(1)}, u32[]{:S(2)}, u32[]{:S(2)}) %collective-permute-start.24) | collective-permute-done | bytes 786464 | tf_op jit(solution)/shard_map/ppermute | solution.py:285
  619.1 17.4 %collective-permute-done.36 = bf16[1,320,2048]{2,1,0:T(8,128)(2,1)S(1)} collective-permute-done((bf16[1,320,2048]{2,1,0:T(8,128)(2,1)}, bf16[1,320,2048]{2,1,0:T(8,128)(2,1)S(1)}, u32[]{:S(2)}, u32[]{:S(2)}) %collective-permute-start.36) | collective-permute-done | bytes 1310752 | tf_op jit(solution)/shard_map/ppermute | solution.py:285
  640.3 19.0 %collective-permute-done.33 = bf16[1,256,2048]{2,1,0:T(8,128)(2,1)S(1)} collective-permute-done((bf16[1,256,2048]{2,1,0:T(8,128)(2,1)}, bf16[1,256,2048]{2,1,0:T(8,128)(2,1)S(1)}, u32[]{:S(2)}, u32[]{:S(2)}) %collective-permute-start.33) | collective-permute-done | bytes 1048608 | tf_op jit(solution)/shard_map/ppermute | solution.py:286
  665.4 39.8 %collective-permute-done.34 = bf16[1,256,2048]{2,1,0:T(8,128)(2,1)S(1)} collective-permute-done((bf16[1,256,2048]{2,1,0:T(8,128)(2,1)S(1)}, bf16[1,256,2048]{2,1,0:T(8,128)(2,1)S(1)}, u32[]{:S(2)}, u32[]{:S(2)}) %collective-permute-start.34) | collective-permute-done | bytes 1048608 | tf_op jit(solution)/shard_map/ppermute | solution.py:286
  711.2 21.9 %collective-permute-done.35 = bf16[1,256,2048]{2,1,0:T(8,128)(2,1)S(1)} collective-permute-done((bf16[1,256,2048]{2,1,0:T(8,128)(2,1)S(1)}, bf16[1,256,2048]{2,1,0:T(8,128)(2,1)S(1)}, u32[]{:S(2)}, u32[]{:S(2)}) %collective-permute-start.35) | collective-permute-done | bytes 1048608 | tf_op jit(solution)/shard_map/ppermute | solution.py:286
  738.9 13.5 %concatenate.63 = bf16[256,14336]{1,0:T(8,128)(2,1)} concatenate(bf16[256,192]{1,0:T(8,128)(2,1)S(1)} %get-tuple-element.150, bf16[256,192]{1,0:T(8,128)(2,1)} %get-tuple-element.144, bf16[256,192]{1,0:T(8,128)(2,1)} %get-tuple-element.138, bf16[256,192]{1,0:T(8,128)(2,1)} %get-tuple-element.132, bf16[256,128]{1,0:T(8,128)(2,1)} %get-tuple-element.162, ...), dimensions={1} | concatenate | bytes 14680064 | tf_op jit(solution)/shard_map/concatenate | solution.py:413
  (313 shorter events, 313.7 us)
Async XLA Ops:
  7.2 178.3 %all-gather.10.cloned.1.call-start = ((), (), s32[]{:S(2)}) async-start(), calls=%async_computation.3 | async-start | bytes 7077888 | tf_op jit(solution)/shard_map/all_gather | solution.py:272
  12.3 205.7 %all-gather.14.cloned.1.call-start = ((), (), s32[]{:S(2)}) async-start(), calls=%async_computation.5 | async-start | bytes 11796480 | tf_op jit(solution)/shard_map/all_gather | solution.py:272
  15.9 245.1 %all-gather.12.cloned.1.call-start = ((), (), s32[]{:S(2)}) async-start(), calls=%async_computation.4 | async-start | bytes 9437184 | tf_op jit(solution)/shard_map/all_gather | solution.py:272
  18.9 514.8 %reduce-scatter.4.cloned.1.call-start = ((), (), s32[]{:S(2)}) async-start(), calls=%async_computation.6 | async-start | bytes 7077888 | tf_op jit(solution)/shard_map/reduce_scatter | solution.py:276
  38.8 43.8 %collective-permute-start.12 = (bf16[256,2048]{1,0:T(8,128)(2,1)S(1)}, bf16[256,2048]{1,0:T(8,128)(2,1)S(1)}, u32[]{:S(2)}, u32[]{:S(2)}) collective-permute-start(bf16[256,2048]{1,0:T(8,128)(2,1)S(1)} %get-tuple-element.72), channel_id=1, source_target_pairs={{0,1},{1,2},{2,3},{4,5},{5,6},{6,7},{8,9},{9,10},{10,11},{12,13},{... | collective-permute-start | bytes 3145736 | tf_op jit(solution)/shard_map/ppermute | solution.py:285
  41.4 45.5 %collective-permute-start.3 = (bf16[256,2048]{1,0:T(8,128)(2,1)}, bf16[256,2048]{1,0:T(8,128)(2,1)}, u32[]{:S(2)}, u32[]{:S(2)}) collective-permute-start(bf16[256,2048]{1,0:T(8,128)(2,1)} %add_convert_fusion.9), channel_id=1, source_target_pairs={{3,2},{2,1},{1,0},{7,6},{6,5},{5,4},{11,10},{10,9},{9,8},{15,14},{... | collective-permute-start | bytes 3145736 | tf_op jit(solution)/shard_map/ppermute | solution.py:286
  42.7 48.2 %collective-permute-start.15 = (bf16[256,2048]{1,0:T(8,128)(2,1)S(1)}, bf16[256,2048]{1,0:T(8,128)(2,1)}, u32[]{:S(2)}, u32[]{:S(2)}) collective-permute-start(bf16[256,2048]{1,0:T(8,128)(2,1)S(1)} %get-tuple-element.72), channel_id=1, source_target_pairs={{3,2},{2,1},{1,0},{7,6},{6,5},{5,4},{11,10},{10,9},{9,8},{15,14},{... | collective-permute-start | bytes 3145736 | tf_op jit(solution)/shard_map/ppermute | solution.py:286
  90.9 50.6 %collective-permute-start.16 = (bf16[256,2048]{1,0:T(8,128)(2,1)}, bf16[256,2048]{1,0:T(8,128)(2,1)}, u32[]{:S(2)}, u32[]{:S(2)}) collective-permute-start(bf16[256,2048]{1,0:T(8,128)(2,1)} %collective-permute-done.15), channel_id=1, source_target_pairs={{2,1},{1,0},{6,5},{5,4},{10,9},{9,8},{14,13},{13,12},{18,17},{17,1... | collective-permute-start | bytes 3145736 | tf_op jit(solution)/shard_map/ppermute | solution.py:286
  92.2 50.8 %collective-permute-start.2 = (bf16[256,2048]{1,0:T(8,128)(2,1)}, bf16[256,2048]{1,0:T(8,128)(2,1)}, u32[]{:S(2)}, u32[]{:S(2)}) collective-permute-start(bf16[256,2048]{1,0:T(8,128)(2,1)} %collective-permute-done.1), channel_id=1, source_target_pairs={{2,3},{6,7},{10,11},{14,15},{18,19},{22,23},{26,27},{30,31}} | collective-permute-start | bytes 3145736 | tf_op jit(solution)/shard_map/ppermute | solution.py:285
  94.1 53.0 %collective-permute-start.14 = (bf16[256,2048]{1,0:T(8,128)(2,1)}, bf16[256,2048]{1,0:T(8,128)(2,1)}, u32[]{:S(2)}, u32[]{:S(2)}) collective-permute-start(bf16[256,2048]{1,0:T(8,128)(2,1)} %collective-permute-done.13), channel_id=1, source_target_pairs={{2,3},{6,7},{10,11},{14,15},{18,19},{22,23},{26,27},{30,31}} | collective-permute-start | bytes 3145736 | tf_op jit(solution)/shard_map/ppermute | solution.py:285
  119.1 44.8 %collective-permute-start.5 = (bf16[256,2048]{1,0:T(8,128)(2,1)}, bf16[256,2048]{1,0:T(8,128)(2,1)S(1)}, u32[]{:S(2)}, u32[]{:S(2)}) collective-permute-start(bf16[256,2048]{1,0:T(8,128)(2,1)} %collective-permute-done.4), channel_id=1, source_target_pairs={{1,0},{5,4},{9,8},{13,12},{17,16},{21,20},{25,24},{29,28}} | collective-permute-start | bytes 3145736 | tf_op jit(solution)/shard_map/ppermute | solution.py:286
  260.8 319.7 %reduce-scatter.6.cloned.1.call-start = ((), (), s32[]{:S(2)}) async-start(), calls=%async_computation.7 | async-start | bytes 9437184 | tf_op jit(solution)/shard_map/reduce_scatter | solution.py:276
  313.2 281.8 %reduce-scatter.8.cloned.1.call-start = ((), (), s32[]{:S(2)}) async-start(), calls=%async_computation.8 | async-start | bytes 11796480 | tf_op jit(solution)/shard_map/reduce_scatter | solution.py:276
  392.5 48.8 %collective-permute-start.9 = (bf16[256,2048]{1,0:T(8,128)(2,1)S(1)}, bf16[256,2048]{1,0:T(8,128)(2,1)}, u32[]{:S(2)}, u32[]{:S(2)}) collective-permute-start(bf16[256,2048]{1,0:T(8,128)(2,1)S(1)} %get-tuple-element.70), channel_id=1, source_target_pairs={{3,2},{7,6},{11,10},{15,14},{19,18},{23,22},{27,26},{31,30}} | collective-permute-start | bytes 3145736 | tf_op jit(solution)/shard_map/ppermute | solution.py:312
  461.0 102.5 %collective-permute-start.8 = (bf16[256,2048]{1,0:T(8,128)(2,1)}, bf16[256,2048]{1,0:T(8,128)(2,1)S(1)}, u32[]{:S(2)}, u32[]{:S(2)}) collective-permute-start(bf16[256,2048]{1,0:T(8,128)(2,1)} %get-tuple-element.67), channel_id=1, source_target_pairs={{0,1},{1,2},{2,3},{4,5},{5,6},{6,7},{8,9},{9,10},{10,11},{12,13},{... | collective-permute-start | bytes 3145736 | tf_op jit(solution)/shard_map/ppermute | solution.py:311
  469.1 94.4 %collective-permute-start.11 = (bf16[256,2048]{1,0:T(8,128)(2,1)}, bf16[256,2048]{1,0:T(8,128)(2,1)}, u32[]{:S(2)}, u32[]{:S(2)}) collective-permute-start(bf16[256,2048]{1,0:T(8,128)(2,1)} %add_convert_fusion.5), channel_id=1, source_target_pairs={{3,2},{2,1},{1,0},{7,6},{6,5},{5,4},{11,10},{10,9},{9,8},{15,14},{... | collective-permute-start | bytes 3145736 | tf_op jit(solution)/shard_map/ppermute | solution.py:312
  608.0 51.2 %collective-permute-start.33 = (bf16[1,256,2048]{2,1,0:T(8,128)(2,1)}, bf16[1,256,2048]{2,1,0:T(8,128)(2,1)S(1)}, u32[]{:S(2)}, u32[]{:S(2)}) collective-permute-start(bf16[1,256,2048]{2,1,0:T(8,128)(2,1)} %bitcast.216), channel_id=1, source_target_pairs={{3,2},{2,1},{1,0},{7,6},{6,5},{5,4},{11,10},{10,9},{9,8},{15,14},{... | collective-permute-start | bytes 3145736 | tf_op jit(solution)/shard_map/ppermute | solution.py:286
  613.8 46.7 %collective-permute-start.31 = (bf16[1,256,2048]{2,1,0:T(8,128)(2,1)}, bf16[1,256,2048]{2,1,0:T(8,128)(2,1)S(1)}, u32[]{:S(2)}, u32[]{:S(2)}) collective-permute-start(bf16[1,256,2048]{2,1,0:T(8,128)(2,1)} %collective-permute-done.30), channel_id=1, source_target_pairs={{1,2},{2,3},{5,6},{6,7},{9,10},{10,11},{13,14},{14,15},{17,18},{18... | collective-permute-start | bytes 3145736 | tf_op jit(solution)/shard_map/ppermute | solution.py:285
  636.5 70.0 %collective-permute-start.37 = (bf16[1,320,2048]{2,1,0:T(8,128)(2,1)S(1)}, bf16[1,320,2048]{2,1,0:T(8,128)(2,1)}, u32[]{:S(2)}, u32[]{:S(2)}) collective-permute-start(bf16[1,320,2048]{2,1,0:T(8,128)(2,1)S(1)} %collective-permute-done.36), channel_id=1, source_target_pairs={{1,2},{2,3},{5,6},{6,7},{9,10},{10,11},{13,14},{14,15},{17,18},{18... | collective-permute-start | bytes 3932168 | tf_op jit(solution)/shard_map/ppermute | solution.py:285
  638.2 70.0 %collective-permute-start.40 = (bf16[1,320,2048]{2,1,0:T(8,128)(2,1)S(1)}, bf16[1,320,2048]{2,1,0:T(8,128)(2,1)}, u32[]{:S(2)}, u32[]{:S(2)}) collective-permute-start(bf16[1,320,2048]{2,1,0:T(8,128)(2,1)S(1)} %collective-permute-done.39), channel_id=1, source_target_pairs={{2,1},{1,0},{6,5},{5,4},{10,9},{9,8},{14,13},{13,12},{18,17},{17,1... | collective-permute-start | bytes 3932168 | tf_op jit(solution)/shard_map/ppermute | solution.py:286
  659.2 45.9 %collective-permute-start.34 = (bf16[1,256,2048]{2,1,0:T(8,128)(2,1)S(1)}, bf16[1,256,2048]{2,1,0:T(8,128)(2,1)S(1)}, u32[]{:S(2)}, u32[]{:S(2)}) collective-permute-start(bf16[1,256,2048]{2,1,0:T(8,128)(2,1)S(1)} %collective-permute-done.33), channel_id=1, source_target_pairs={{2,1},{1,0},{6,5},{5,4},{10,9},{9,8},{14,13},{13,12},{18,17},{17,1... | collective-permute-start | bytes 3145736 | tf_op jit(solution)/shard_map/ppermute | solution.py:286
  660.5 49.0 %collective-permute-start.32 = (bf16[1,256,2048]{2,1,0:T(8,128)(2,1)S(1)}, bf16[1,256,2048]{2,1,0:T(8,128)(2,1)S(1)}, u32[]{:S(2)}, u32[]{:S(2)}) collective-permute-start(bf16[1,256,2048]{2,1,0:T(8,128)(2,1)S(1)} %collective-permute-done.31), channel_id=1, source_target_pairs={{2,3},{6,7},{10,11},{14,15},{18,19},{22,23},{26,27},{30,31}} | collective-permute-start | bytes 3145736 | tf_op jit(solution)/shard_map/ppermute | solution.py:285
  706.4 56.2 %collective-permute-start.38 = (bf16[1,320,2048]{2,1,0:T(8,128)(2,1)}, bf16[1,320,2048]{2,1,0:T(8,128)(2,1)}, u32[]{:S(2)}, u32[]{:S(2)}) collective-permute-start(bf16[1,320,2048]{2,1,0:T(8,128)(2,1)} %collective-permute-done.37), channel_id=1, source_target_pairs={{2,3},{6,7},{10,11},{14,15},{18,19},{22,23},{26,27},{30,31}} | collective-permute-start | bytes 3932168 | tf_op jit(solution)/shard_map/ppermute | solution.py:285
  708.2 59.3 %collective-permute-start.41 = (bf16[1,320,2048]{2,1,0:T(8,128)(2,1)}, bf16[1,320,2048]{2,1,0:T(8,128)(2,1)}, u32[]{:S(2)}, u32[]{:S(2)}) collective-permute-start(bf16[1,320,2048]{2,1,0:T(8,128)(2,1)} %collective-permute-done.40), channel_id=1, source_target_pairs={{1,0},{5,4},{9,8},{13,12},{17,16},{21,20},{25,24},{29,28}} | collective-permute-start | bytes 3932168 | tf_op jit(solution)/shard_map/ppermute | solution.py:286
  (62 other events, 1816.3 us)
Sparse Core Ops, SparseCore 0:
  12.4 48.5 all-gather.9
  63.5 63.2 all-gather.13
  128.7 54.3 all-gather.11
  261.0 69.0 reduce-scatter.3
  333.7 71.3 reduce-scatter.5
  409.0 81.5 reduce-scatter.7

commit v3 on v1

--- a/solution.py
+++ b/solution.py
@@ -268,6 +268,132 @@
     return jax.nn.gelu(value, approximate=True)
 
 
+def tie(value, *after):
+    return lax.optimization_barrier((value, after))[0] if after else value
+
+
+def close(lines, *values):
+    arrived, values = lax.optimization_barrier(([line.latest for line in lines], values))
+    for line, arrays in zip(lines, arrived):
+        line.latest = arrays
+    return jax.tree.leaves(arrived) + jax.tree.leaves(values), values
+
+
+class LineGather:
+    def __init__(self, block):
+        self.block, self.before, self.after = block, [], []
+
+    def step(self, *after):
+        n = lax.axis_size("context")
+        t = len(self.before) + 1
+        right, left = (self.before[-1], self.after[-1]) if t > 1 else (self.block, self.block)
+        right, left = tie((right, left), *after)
+        self.before.append(
+            lax.ppermute(right, "context", [(a, a + 1) for a in range(t - 1, n - 1)])
+        )
+        self.after.append(lax.ppermute(left, "context", [(a, a - 1) for a in range(n - t, 0, -1)]))
+        return self.before[-1], self.after[-1]
+
+    @property
+    def latest(self):
+        return self.before[-1], self.after[-1]
+
+    @latest.setter
+    def latest(self, arrays):
+        self.before[-1], self.after[-1] = arrays
+
+    def whole(self, context):
+        return place(context, self.before[::-1] + [self.block] + self.after)
+
+
+class LineScatter:
+    def __init__(self, partial):
+        self.partial, self.steps = partial, 0
+        self.right = self.left = None
+
+    def mine(self, j):
+        n = lax.axis_size("context")
+        rows = self.partial.shape[0] // n
+        return lax.dynamic_slice_in_dim(self.partial, jnp.clip(j, 0, n - 1) * rows, rows, 0)
+
+    def step(self, *after):
+        n = lax.axis_size("context")
+        context = lax.axis_index("context")
+        self.steps = t = self.steps + 1
+        right, left = self.mine(n - t + context), self.mine(context - (n - t))
+        if t > 1:
+            right = (right.astype(F32) + self.right.astype(F32)).astype(BF16)
+            left = (left.astype(F32) + self.left.astype(F32)).astype(BF16)
+        right, left = tie((right, left), *after)
+        self.right = lax.ppermute(right, "context", [(a, a + 1) for a in range(t)])
+        self.left = lax.ppermute(left, "context", [(n - 1 - a, n - 2 - a) for a in range(t)])
+        return self.right, self.left
+
+    @property
+    def latest(self):
+        return self.right, self.left
+
+    @latest.setter
+    def latest(self, arrays):
+        self.right, self.left = arrays
+
+    def result(self):
+        own = self.mine(lax.axis_index("context")).astype(F32)
+        return own + self.right.astype(F32) + self.left.astype(F32)
+
+
+def place_kernel(context_ref, *refs):
+    *blocks, out_ref, held, taken, given = refs
+    n = (len(blocks) + 1) // 2
+    rows = blocks[0].shape[0]
+
+    def give(j):
+        return pltpu.make_async_copy(
+            held.at[j], out_ref.at[pl.ds(j * rows, rows), :], given.at[j]
+        )
+
+    for c in range(n):
+
+        @pl.when(context_ref[0] == c)
+        def _():
+            copies = [
+                pltpu.make_async_copy(blocks[j - c + n - 1], held.at[j], taken.at[j])
+                for j in range(n)
+            ]
+            for copy in copies:
+                copy.start()
+            for j, copy in enumerate(copies):
+                copy.wait()
+                give(j).start()
+            for j in range(n):
+                give(j).wait()
+
+
+def place(context, line):
+    n = (len(line) + 1) // 2
+    rows, columns = line[0].shape
+    anywhere = pl.BlockSpec(memory_space=pl.ANY)
+    return pl.pallas_call(
+        place_kernel,
+        grid_spec=pltpu.PrefetchScalarGridSpec(
+            num_scalar_prefetch=1,
+            grid=(1,),
+            in_specs=[anywhere] * len(line),
+            out_specs=anywhere,
+            scratch_shapes=[
+                pltpu.VMEM((n, rows, columns), line[0].dtype),
+                pltpu.SemaphoreType.DMA((n,)),
+                pltpu.SemaphoreType.DMA((n,)),
+            ],
+        ),
+        out_shape=jax.ShapeDtypeStruct((n * rows, columns), line[0].dtype),
+        compiler_params=pltpu.CompilerParams(vmem_limit_bytes=32 * 2**20),
+        cost_estimate=pl.CostEstimate(
+            flops=0, bytes_accessed=4 * n * rows * columns, transcendentals=0
+        ),
+    )(context.reshape(1), *line)
+
+
 def gather_shard(x):
     return lax.all_gather(x, "shard", axis=0, tiled=True)
 
@@ -276,12 +402,84 @@
     return lax.psum_scatter(x, "shard", scatter_dimension=0, tiled=True)
 
 
-def gather_context(x):
-    return lax.all_gather(x, "context", axis=0, tiled=True)
-
-
-def scatter_context(x):
-    return lax.psum_scatter(x, "context", scatter_dimension=0, tiled=True)
+def spread_kernel(segments, in_ref, *refs):
+    out_ref = refs[-1]
+    for c in range(in_ref.shape[0]):
+        part = in_ref[c].astype(F32)
+        at = 0
+        for base, width in segments:
+            out_ref[:, base + c * width : base + (c + 1) * width] = part[:, at : at + width]
+            at += width
+
+
+def finish_hidden(parts, segments, rows, columns):
+    n = parts.shape[0]
+    step = 32
+    return pl.pallas_call(
+        functools.partial(spread_kernel, segments),
+        grid=(rows // step,),
+        in_specs=[pl.BlockSpec((n, step, parts.shape[2]), lambda i: (0, i, 0))],
+        out_specs=pl.BlockSpec((step, columns), lambda i: (i, 0)),
+        out_shape=jax.ShapeDtypeStruct((rows, columns), F32),
+        compiler_params=pltpu.CompilerParams(vmem_limit_bytes=48 * 2**20),
+        cost_estimate=pl.CostEstimate(
+            flops=0, bytes_accessed=5 * rows * columns, transcendentals=0
+        ),
+    )(parts)
+
+
+def finish_qkv(whole, parts, segments):
+    n = parts.shape[0]
+    rows = whole.shape[0]
+    step = 32
+    columns = n * sum(width for _, width in segments)
+    return pl.pallas_call(
+        functools.partial(spread_kernel, segments),
+        grid=(rows // step,),
+        in_specs=[
+            pl.BlockSpec((n, step, parts.shape[2]), lambda i: (0, i, 0)),
+            pl.BlockSpec(memory_space=pl.ANY),
+        ],
+        out_specs=pl.BlockSpec((step, columns), lambda i: (i, 0)),
+        out_shape=jax.ShapeDtypeStruct(whole.shape, F32),
+        input_output_aliases={1: 0},
+        compiler_params=pltpu.CompilerParams(vmem_limit_bytes=48 * 2**20),
+        cost_estimate=pl.CostEstimate(
+            flops=0, bytes_accessed=6 * rows * columns, transcendentals=0
+        ),
+    )(parts, whole)
+
+
+def finish_out_kernel(in_ref, out_ref):
+    out_ref[...] = in_ref[0].astype(F32)
+
+
+def finish_out(gathered, inner):
+    n, rows, columns = gathered.shape
+    step = HEAD_DIM
+    bounds, at = [], 0
+    for base, width in inner:
+        bounds.append((base // step, width // step, at // step))
+        at += width
+
+    def source(b):
+        c = first = 0
+        for base, width, start in bounds:
+            inside = b >= base
+            c = jnp.where(inside, (b - base) // width, c)
+            first = jnp.where(inside, start + (b - base) % width, first)
+        return (c, first, 0)
+
+    return pl.pallas_call(
+        finish_out_kernel,
+        grid=(n * rows // step,),
+        in_specs=[pl.BlockSpec((1, step, columns), source)],
+        out_specs=pl.BlockSpec((step, columns), lambda b: (b, 0)),
+        out_shape=jax.ShapeDtypeStruct((n * rows, columns), F32),
+        cost_estimate=pl.CostEstimate(
+            flops=0, bytes_accessed=6 * n * rows * columns, transcendentals=0
+        ),
+    )(gathered)
 
 
 def local(
@@ -305,11 +503,15 @@
     heads = HEADS // context_size
     attn = heads * HEAD_DIM
     rows_here = input_weight.shape[0]
+    steps = context_size - 1
     inner, segments = column_plan(shard_size, context_size)
     attn_segments = [(base, width) for base, width in segments if base < D]
     hidden_segments = [(base, width) for base, width in segments if base >= D]
     qkv_columns = [(base + i * D, width) for i in range(3) for base, width in attn_segments]
     hidden_columns = [(base + 2 * D, width) for base, width in hidden_segments]
+
+    up = LineGather(cotangent.astype(BF16))
+    up.step()
 
     small = jnp.concatenate(
         [input_bias, output_bias[0], output_bias[1], norm_gain, norm_bias], 0
@@ -322,7 +524,15 @@
     gain = small[:, cut + 2 * share : cut + 3 * share].reshape(-1)
     shift = small[:, cut + 3 * share :].reshape(-1)
 
+    centred = block_input - jnp.mean(block_input, axis=1, keepdims=True)
+    inverse_std = lax.rsqrt(jnp.mean(centred * centred, axis=1, keepdims=True) + epsilon)
+    normalized = centred * inverse_std
+    normed_here = (normalized * gain + shift).astype(BF16)
+
     weight_qkv = gather_shard(take(input_weight, qkv_columns, context, 1))
+    gate, (normed_here, input_weight, output_weight) = close(
+        [up], normed_here, input_weight, output_weight
+    )
     weight_hidden = gather_shard(take(input_weight, hidden_columns, context, 1))
     if inner is not None:
         weight_out = gather_shard(take(output_weight, inner, context, 0))
@@ -330,46 +540,127 @@
         weight_out = take(gather_shard(output_weight), segments, context, 0)
     bias_qkv = take(bias_in, qkv_columns, context, 0)
     bias_hidden = take(bias_in, hidden_columns, context, 0)
-
-    centred = block_input - jnp.mean(block_input, axis=1, keepdims=True)
-    inverse_std = lax.rsqrt(jnp.mean(centred * centred, axis=1, keepdims=True) + epsilon)
-    normalized = centred * inverse_std
-    normed = gather_context((normalized * gain + shift).astype(BF16))
-    upstream = gather_context(cotangent.astype(BF16))
-
-    place = causal_blocks(assignment)
-    tables = rotary_tables(group_positions(positions, assignment, context, group))
-
+    places = causal_blocks(assignment)
+
+    norm = LineGather(normed_here)
+    for t in range(steps):
+        gate = norm.step(*gate)
+        if t == 0:
+            positions = tie(positions, *gate)
+            tables = rotary_tables(group_positions(positions, assignment, context, group))
+    normed = norm.whole(context)
+
+    normed = tie(normed, *gate)
     projected = dot(normed, weight_qkv) + bias_qkv
-    attended, log_total, query, keys, values = attend(place, projected, tables, heads)
+    up.step(*gate)
+    attended, log_total, query, keys, values = attend(places, projected, tables, heads)
+    gate, (attended, normed) = close([up], attended, normed)
+    for t in range(steps - 2):
+        up.step(*gate)
     hidden_pre = dot(normed, weight_hidden) + bias_hidden
     activation = gelu_tanh(hidden_pre).astype(BF16)
     joined = jnp.concatenate([attended, activation], axis=1)
-    partial_out = scatter_context(dot(joined, weight_out).astype(BF16))
-    block_output = block_input + partial_out.astype(F32) + bias_sum
-
-    attended_grad = dot(upstream, weight_out[:attn], ((1,), (1,))).astype(BF16)
+    partial_out = dot(joined, weight_out).astype(BF16)
+    gate, (partial_out, joined) = close([up], partial_out, joined)
+    upstream = up.whole(context)
+
+    out = LineScatter(partial_out)
+    out.step()
+    out_grad = dot(joined, upstream, ((0,), (0,))).astype(BF16)
+    gate, (out_grad, upstream) = close([out], out_grad, upstream)
+    if inner is not None:
+        out_grad_sum = scatter_shard(out_grad)
+
+    out.step()
     joined_grad = dot(upstream, weight_out[attn:], ((1,), (1,)))
     hidden_grad = jax.vjp(gelu_tanh, hidden_pre)[1](joined_grad)[0]
     hidden_rounded = hidden_grad.astype(BF16)
     hidden_sum = jnp.sum(hidden_grad, axis=0)
+    gate, (hidden_rounded, upstream) = close([out], hidden_rounded, upstream)
+
+    for t in range(steps - 2):
+        out.step()
+    hidden_in_grad = dot(normed, hidden_rounded, ((0,), (0,))).astype(BF16)
+    gate, (hidden_in_grad, hidden_rounded, upstream) = close(
+        [out], hidden_in_grad, hidden_rounded, upstream
+    )
+    hidden_in_sum = scatter_shard(hidden_in_grad)
+    block_output = block_input + out.result() + bias_sum
+
+    attended_grad = dot(upstream, weight_out[:attn], ((1,), (1,))).astype(BF16)
+    normed_grad = dot(hidden_rounded, weight_hidden, ((1,), (1,)))
+    attended_grad, normed_grad = lax.optimization_barrier((attended_grad, normed_grad))
+
+    gathers = []
+    if inner is not None:
+        gathers.append(LineGather(out_grad_sum))
+        gathers[0].step(attended_grad)
     dq, dk, dv, sums = attend_back(
-        place, query, keys, values, log_total, attended, attended_grad, tables, heads
+        places, query, keys, values, log_total, attended, attended_grad, tables, heads
     )
     qkv_rounded = jnp.concatenate([dq, dk, dv], axis=1)
-    normed_grad = dot(hidden_rounded, weight_hidden, ((1,), (1,))) + dot(
-        qkv_rounded, weight_qkv, ((1,), (1,))
-    )
-    normed_grad = scatter_context(normed_grad.astype(BF16)).astype(F32)
-
-    out_grad = dot(joined, upstream, ((0,), (0,))).astype(BF16)
-    hidden_in_grad = scatter_shard(dot(normed, hidden_rounded, ((0,), (0,))).astype(BF16))
-    qkv_in_grad = scatter_shard(dot(normed, qkv_rounded, ((0,), (0,))).astype(BF16))
+    gate, (qkv_rounded,) = close(gathers, qkv_rounded)
+
+    for gather in gathers:
+        gather.step()
+    normed_grad = normed_grad + dot(qkv_rounded, weight_qkv, ((1,), (1,)))
+    gain_sum = jnp.sum(normed_grad * ((normed.astype(F32) - shift) / gain), axis=0)
+    shift_sum = jnp.sum(normed_grad, axis=0)
+    partial_grad = normed_grad.astype(BF16)
+    gate, (partial_grad, qkv_rounded) = close(gathers, partial_grad, qkv_rounded)
+
+    grad = LineScatter(partial_grad)
+    for gather in gathers:
+        for t in range(2, steps):
+            gather.step()
+    grad.step()
+    qkv_in_grad = dot(normed, qkv_rounded, ((0,), (0,))).astype(BF16)
+    gate, (qkv_in_grad,) = close(gathers + [grad], qkv_in_grad)
+    vectors = jnp.concatenate(
+        [sums[0], sums[1], sums[2], hidden_sum, jnp.sum(cotangent, axis=0), gain_sum, shift_sum]
+    )
+    wide = 3 * attn
+    extra = -(-vectors.shape[0] // (16 * wide)) * 16
+    vectors = jnp.pad(vectors, (0, extra * wide - vectors.shape[0])).reshape(1, extra, wide)
+    vectors = jnp.broadcast_to(vectors.astype(BF16), (shard_size, extra, wide))
+    qkv_in_sum = scatter_shard(
+        jnp.concatenate([qkv_in_grad.reshape(shard_size, rows_here, wide), vectors], 1).reshape(
+            -1, wide
+        )
+    )
+
+    hidden_gather, qkv_gather = LineGather(hidden_in_sum), LineGather(qkv_in_sum)
     if inner is not None:
-        out_grad = scatter_shard(out_grad)
-        out_grad = gather_context(out_grad[None])
-        weight_out_grad = untake(out_grad, inner, 0).astype(F32)
+        weight_out_grad = finish_out(
+            tie(gathers[0].whole(context), *gate).reshape(context_size, -1, D), inner
+        )
+        done = (weight_out_grad,)
     else:
+        done = ()
+    for t in range(steps):
+        lines = [hidden_gather]
+        hidden_gather.step(*gate)
+        if t == steps - 1 and grad.steps < steps:
+            grad.step()
+            lines.append(grad)
+        gate, done = close(lines, *done)
+        if inner is not None and t == 0:
+            (weight_out_grad,) = done
+            done = ()
+    hidden_parts = hidden_gather.whole(context).reshape(context_size, rows_here, -1)
+    weight_in_grad = finish_hidden(
+        tie(hidden_parts, *gate), hidden_columns, rows_here, input_weight.shape[1]
+    )
+    for t in range(steps):
+        lines = [qkv_gather]
+        qkv_gather.step(*gate)
+        if grad.steps < steps:
+            grad.step()
+            lines.append(grad)
+        gate, done = close(lines, *((weight_in_grad,) if t == 0 else ()))
+        if t == 0:
+            (weight_in_grad,) = done
+    if inner is None:
         whole = jnp.zeros((D + FF, D), BF16)
         at = 0
         for base, width in segments:
@@ -378,33 +669,20 @@
             )
             at += width
         weight_out_grad = lax.psum(scatter_shard(whole), "context").astype(F32)
-    hidden_in_grad = untake(gather_context(hidden_in_grad[None]), hidden_segments, 1)
-    qkv_in_grad = gather_context(qkv_in_grad[None])
-    qkv_in_grad = untake(qkv_in_grad, qkv_columns, 1)
-    weight_in_grad = jnp.concatenate([qkv_in_grad, hidden_in_grad], 1).astype(F32)
-
-    vectors = jnp.concatenate(
-        [
-            sums[0],
-            sums[1],
-            sums[2],
-            hidden_sum,
-            jnp.sum(cotangent, axis=0),
-            jnp.sum(normed_grad * normalized, axis=0),
-            jnp.sum(normed_grad, axis=0),
-        ]
-    )
-    vectors = jnp.sum(gather_shard(vectors[None]), axis=0)
-    vectors = gather_context(vectors[None])
-    columns = 3 * attn + hidden_sum.shape[0]
+    qkv_parts = qkv_gather.whole(context).reshape(context_size, rows_here + extra, wide)
+    weight_in_grad = finish_qkv(weight_in_grad, qkv_parts, qkv_columns)
+
+    vectors = qkv_parts[:, rows_here:].astype(F32).reshape(context_size, -1)
+    columns = wide + hidden_sum.shape[0]
     bias_in_sum = untake(vectors[:, :columns], qkv_columns + hidden_columns, 0)
-    others = jnp.sum(vectors[:, columns:], axis=0)
+    others = jnp.sum(vectors[:, columns : columns + 3 * D], axis=0)
 
     def own_share(vector):
         length = vector.shape[0] // shard_size
         return lax.dynamic_slice_in_dim(vector, shard_here * length, length, 0)
 
     bias_row = own_share(others[:D])
+    normed_grad = grad.result()
     scaled = normed_grad * gain
     input_grad = cotangent + inverse_std * (
         scaled

time: 1020 us -> 627 us (0.61)
  waiting for transfers between devices: 683 us -> 197 us
  starting transfers between devices: 0.7 us -> 94 us
  Pallas kernels: 41.4 us -> 74.9 us
  blocking collectives: 36.1 us -> 9.5 us
  local copies, waits for them, and re-layouts: 68.8 us -> 51.7 us
    all_gather x5 -> x0, waiting for transfers between devices: 311 us -> none  [gather_context(): return lax.all_gather(x, 'context', axis=0, tiled=True)]
    ppermute x0 -> x42, waiting for transfers between devices: none -> 190 us  [the longest x15 132 us: step(): lax.ppermute(left, 'context', [(a, a - 1) for a in range(n - t, 0, -1)])]
    reduce_scatter x2 -> x0, waiting for transfers between devices: 128 us -> none  [scatter_context(): return lax.psum_scatter(x, 'context', scatter_dimension=0, tiled=True)]
    all_gather x3, waiting for transfers between devices: 125 us -> 0.04 us  [gather_shard(): return lax.all_gather(x, 'shard', axis=0, tiled=True)]
    reduce_scatter x3, waiting for transfers between devices: 118 us -> 7.16 us  [scatter_shard(): return lax.psum_scatter(x, 'shard', scatter_dimension=0, tiled=True)]
    ppermute x0 -> x42, starting transfers between devices: none -> 93.3 us  [the longest x6 33.4 us: step(): self.right = lax.ppermute(right, 'context', [(a, a + 1) for a in range(t)])]
    pallas_call x0 -> x8, Pallas kernels: none -> 33.7 us  [the longest x1 13.4 us: finish_out(): pl.pallas_call(finish_out_kernel, grid=(n * rows // step,), in_specs=[pl....]
    slice x13 -> x6, local copies, waits for them, and re-layouts: 17.3 us -> 0.51 us  [untake(): parts.append(lax.slice_in_dim(gathered[c], at, at + width, axis=axis))]
  transfers between devices with their start and end apart: 13 -> 48, of which waited for: 12 -> 22; matrix products, arithmetic and copies ran while one was open for 20% -> 31% of each run, Pallas kernels for 4% -> 11%
where the time goes in v3:
time: 627 us; the launch traced here: 619 us
  waiting for transfers between devices  197 us (31%)
  matrix products  133 us (21%)
  starting transfers between devices  94 us (15%)
  Pallas kernels  74.9 us (12%)
  local copies, waits for them, and re-layouts  51.7 us (8%)
  other arithmetic  42 us (7%)
  between operations  16.7 us (3%)
  blocking collectives  9.5 us (2%)
    dot_general x10, matrix products, dot(): return lax.dot_general(a, b, (dims, ((), ())), preferred_element_type=F32)  133 us
    ppermute x15, waiting for transfers between devices, step(): lax.ppermute(left, 'context', [(a, a - 1) for a in range(n - t, 0, -1)])  132 us
    ppermute x6, starting transfers between devices, step(): self.right = lax.ppermute(right, 'context', [(a, a + 1) for a in range(t)])  33.4 us
    ppermute x15, waiting for transfers between devices, step(): lax.ppermute(right, 'context', [(a, a + 1) for a in range(t - 1, n - 1)])  33.3 us
    ppermute x15, starting transfers between devices, step(): lax.ppermute(right, 'context', [(a, a + 1) for a in range(t - 1, n - 1)])  33.2 us
    unnamed x138, local copies, waits for them, and re-layouts  31.5 us
    pallas_call x1, Pallas kernels, attend_back(): pl.pallas_call(attend_back_kernel, grid_spec=pltpu.PrefetchScalarGridSpec...  23.5 us
    ppermute x15, starting transfers between devices, step(): lax.ppermute(left, 'context', [(a, a - 1) for a in range(n - t, 0, -1)])  20 us
  transfers between devices with their start and end apart: 48, of which 22 were waited for; matrix products, arithmetic and copies ran while one was open for 31% of the time, Pallas kernels for 11%

profile of v3, /device:TPU:0, one launch (start us, length us, event | category | flops | bytes accessed | tf_op | source)
XLA Modules:
  0.0 619.3 jit_solution(16606855281537522109)
XLA Ops:
  22.8 9.5 %all-gather.1 = bf16[8,1,2816]{2,1,0:T(2,128)(2,1)S(1)} all-gather(bf16[1,1,2816]{2,1,0:T(2,128)(2,1)S(1)} %reshape.246), channel_id=2, replica_groups=mesh['shard'=8,'context'=4] {'shard'}, dimensions={0}, use_global_device_ids=true | all-gather | bytes 50688 | tf_op jit(solution)/shard_map/all_gather | solution.py:398
  60.2 19.8 %collective-permute-done.2.refs_2_ = bf16[256,2048]{1,0:T(8,128)(2,1)S(1)} collective-permute-done((bf16[256,2048]{1,0:T(8,128)(2,1)S(1)}, bf16[256,2048]{1,0:T(8,128)(2,1)S(1)}, u32[]{:S(2)}, u32[]{:S(2)}) %collective-permute-start.2) | collective-permute-done | bytes 1048608 | tf_op jit(solution)/shard_map/ppermute | solution.py:292
  89.9 22.9 %collective-permute-done.5.refs_5_ = bf16[256,2048]{1,0:T(8,128)(2,1)} collective-permute-done((bf16[256,2048]{1,0:T(8,128)(2,1)}, bf16[256,2048]{1,0:T(8,128)(2,1)}, u32[]{:S(2)}, u32[]{:S(2)}) %collective-permute-start.5) | collective-permute-done | bytes 1048608 | tf_op jit(solution)/shard_map/ppermute | solution.py:294
  119.2 18.2 %collective-permute-done.7.refs_6_ = bf16[256,2048]{1,0:T(8,128)(2,1)S(1)} collective-permute-done((bf16[256,2048]{1,0:T(8,128)(2,1)}, bf16[256,2048]{1,0:T(8,128)(2,1)S(1)}, u32[]{:S(2)}, u32[]{:S(2)}) %collective-permute-start.7) | collective-permute-done | bytes 1048608 | tf_op jit(solution)/shard_map/ppermute | solution.py:294
  145.8 11.7 %convolution_add_fusion.q_ref.k_ref.v_ref = f32[1024,1536]{1,0:T(8,128)} fusion(bf16[1024,2048]{1,0:T(8,128)(2,1)} %copy-done.1, bf16[2048,1536]{1,0:T(8,128)(2,1)} %all-gather.6.cloned.1.call-done, f32[1536]{0:T(1024)S(1)} %concatenate.36), kind=kOutput, calls=%fused_computation.17 | convolution fusion | flops 6444023808 | bytes 16783360 | tf_op jit(solution)/shard_map/dot_general | solution.py:27
  157.5 17.8 %shard_map.162 = (bf16[1024,512]{1,0:T(8,128)(2,1)S(1)}, f32[1024,512]{1,0:T(8,128)}, bf16[1024,512]{1,0:T(8,128)(2,1)S(1)}, bf16[1024,512]{1,0:T(8,128)(2,1)S(1)}, bf16[1024,512]{1,0:T(8,128)(2,1)S(1)}) custom-call(s32[8]{0:T(128)S(1)} %select_reduce_fusion.place_ref, f32[1024,1536]{1,0:T(8,128)} %convolution_add_fusion.q_ref.k_ref.v_ref, ...), custom_call_target="tpu_custom_call" | custom-call | flops 4294967296 | bytes 15728640 | tf_op jit(solution)/shard_map/pallas_call | solution.py:190
  182.7 16.1 %multiply_convert_fusion = (bf16[1024,2048]{1,0:T(8,128)(2,1)S(1)}, f32[1024,2048]{1,0:T(8,128)}) fusion(f32[2048]{0:T(1024)S(1)} %concatenate.38, bf16[1024,2048]{1,0:T(8,128)(2,1)} %copy-done.1, bf16[2048,2048]{1,0:T(8,128)(2,1)} %all-gather.8.cloned.1.call-done), kind=kOutput, calls=%fused_computation.12 | convolution fusion | flops 8610906112 | bytes 25174016 | tf_op jit(solution)/shard_map/dot_general | solution.py:27
  203.5 15.2 %convolution_convert_fusion.3 = bf16[1024,2048]{1,0:T(8,128)(2,1)S(1)} fusion(bf16[2560,2048]{1,0:T(8,128)(2,1)} %all-gather.10.cloned.1.call-done, bf16[1024,2048]{1,0:T(8,128)(2,1)} %copy-done.37, bf16[1024,512]{1,0:T(8,128)(2,1)} %copy-done.16), kind=kOutput, calls=%fused_computation.19 | convolution fusion | flops 10750001152 | bytes 19922944 | tf_op jit(solution)/shard_map/dot_general | solution.py:27
  232.9 13.4 %convolution_convert_fusion = bf16[2560,2048]{1,0:T(8,128)(2,1)} fusion(bf16[1024,2560]{1,0:T(8,128)(2,1)S(1)} %bitcast.177, bf16[1024,2048]{1,0:T(8,128)(2,1)S(1)} %shard_map.163), kind=kOutput, calls=%fused_computation.2 | convolution fusion | flops 10742661120 | bytes 19922944 | tf_op jit(solution)/shard_map/dot_general | solution.py:27
  253.2 20.1 %fusion.25 = (bf16[2048]{0:T(1024)(128)(2,1)S(1)}, bf16[1024,2048]{1,0:T(8,128)(2,1)}) fusion(f32[1024,2048]{1,0:T(8,128)} %get-tuple-element.368, f32[2048]{0:T(1024)S(1)} %concatenate.38, bf16[1024,2048]{1,0:T(8,128)(2,1)S(1)} %copy-done.6, bf16[2560,2048]{1,0:T(8,128)(2,1)} %all-gather.10.cloned.1.call-done), kind=kOutput, calls=%fused_computation.147 | convolution fusion | flops 8636069888 | bytes 25178112 | tf_op jit(solution)/shard_map/dot_general | solution.py:27
  283.5 13.8 %convolution_convert_fusion.2 = bf16[2048,2048]{1,0:T(8,128)(2,1)} fusion(bf16[1024,2048]{1,0:T(8,128)(2,1)S(1)} %copy-done.2, bf16[1024,2048]{1,0:T(8,128)(2,1)} %get-tuple-element.140), kind=kOutput, calls=%fused_computation.14 | convolution fusion | flops 8594128896 | bytes 16777216 | tf_op jit(solution)/shard_map/dot_general | solution.py:27
  308.7 13.3 %fusion.33 = f32[1024,2048]{1,0:T(8,128)} fusion(bf16[1024,2048]{1,0:T(8,128)(2,1)S(1)} %copy-done.58, bf16[2048,2048]{1,0:T(8,128)(2,1)} %all-gather.8.cloned.1.call-done), kind=kOutput, calls=%fused_computation.155 | convolution fusion | flops 8589934592 | bytes 20971520 | tf_op jit(solution)/shard_map/dot_general | solution.py:27
  336.1 23.5 %shard_map.164 = (bf16[1024,512]{1,0:T(8,128)(2,1)S(1)}, bf16[1024,512]{1,0:T(8,128)(2,1)S(1)}, bf16[1024,512]{1,0:T(8,128)(2,1)S(1)}, f32[8,512]{1,0:T(8,128)S(1)}) custom-call(s32[8]{0:T(128)S(1)} %select_reduce_fusion.place_ref, bf16[1024,512]{1,0:T(8,128)(2,1)S(1)} %copy-done.28, bf16[1024,512]{1,0:T(8,128)(2,1)} %copy-done.29, ...), custom_call_target="tpu_custom_call" | custom-call | flops 10737418240 | bytes 15728640 | tf_op jit(solution)/shard_map/pallas_call | solution.py:220
  368.1 13.0 %fusion.24 = (bf16[2048]{0:T(1024)(128)(2,1)S(1)}, bf16[2048]{0:T(1024)(128)(2,1)S(1)}, bf16[1024,2048]{1,0:T(8,128)(2,1)}) fusion(f32[2048]{0:T(1024)S(1)} %bitcast.188, f32[2048]{0:T(1024)S(1)} %bitcast.192, bf16[1024,2048]{1,0:T(8,128)(2,1)S(1)} %copy-done.3, f32[1024,2048]{1,0:T(8,128)} %fusion.33, bf16[1024,1536]{1,0:T(8,128)(2,1)S(1)} %pad_maximum_fusion.2, ...), kind=kOutput, calls=%fused_computation.146 | convolution fusion | flops 6459224064 | bytes 26238976 | tf_op jit(solution)/shard_map/dot_general | solution.py:27
  381.7 17.9 %collective-permute-done.21.refs_5_ = bf16[320,2048]{1,0:T(8,128)(2,1)S(1)} collective-permute-done((bf16[320,2048]{1,0:T(8,128)(2,1)}, bf16[320,2048]{1,0:T(8,128)(2,1)S(1)}, u32[]{:S(2)}, u32[]{:S(2)}) %collective-permute-start.21) | collective-permute-done | bytes 1310752 | tf_op jit(solution)/shard_map/ppermute | solution.py:294
  409.1 10.6 %convolution_convert_fusion.1 = bf16[2048,1536]{1,0:T(8,128)(2,1)} fusion(bf16[1024,2048]{1,0:T(8,128)(2,1)S(1)} %copy-done.4, bf16[1024,1536]{1,0:T(8,128)(2,1)} %copy-done.38), kind=kOutput, calls=%fused_computation.13 | convolution fusion | flops 6445596672 | bytes 13631488 | tf_op jit(solution)/shard_map/dot_general | solution.py:27
  419.7 8.6 %collective-permute-done.24 = bf16[256,2048]{1,0:T(8,128)(2,1)S(1)} collective-permute-done((bf16[256,2048]{1,0:T(8,128)(2,1)S(1)}, bf16[256,2048]{1,0:T(8,128)(2,1)S(1)}, u32[]{:S(2)}, u32[]{:S(2)}) %collective-permute-start.24) | collective-permute-done | bytes 1048608 | tf_op jit(solution)/shard_map/ppermute | solution.py:328
  452.7 13.4 %shard_map.166 = f32[1280,2048]{1,0:T(8,128)} custom-call(bf16[4,320,2048]{2,1,0:T(8,128)(2,1)} %bitcast.170), custom_call_target="tpu_custom_call" | custom-call | bytes 15728640 | tf_op jit(solution)/shard_map/pallas_call | solution.py:473
  471.4 7.8 %collective-permute-start.32 = (bf16[256,2048]{1,0:T(8,128)(2,1)S(1)}, bf16[256,2048]{1,0:T(8,128)(2,1)S(1)}, u32[]{:S(2)}, u32[]{:S(2)}) collective-permute-start(bf16[256,2048]{1,0:T(8,128)(2,1)S(1)} %get-tuple-element.235), channel_id=1, source_target_pairs={{0,1},{1,2},{4,5},{5,6},{8,9},{9,10},{12,13},{13,14},{16,17},{17,1... | collective-permute-start | bytes 3145736 | tf_op jit(solution)/shard_map/ppermute | solution.py:328
  480.0 14.6 %collective-permute-done.29.refs_5_ = bf16[256,2048]{1,0:T(8,128)(2,1)S(1)} collective-permute-done((bf16[256,2048]{1,0:T(8,128)(2,1)}, bf16[256,2048]{1,0:T(8,128)(2,1)S(1)}, u32[]{:S(2)}, u32[]{:S(2)}) %collective-permute-start.29) | collective-permute-done | bytes 1048608 | tf_op jit(solution)/shard_map/ppermute | solution.py:294
  499.4 19.0 %collective-permute-done.31.refs_6_ = bf16[256,2048]{1,0:T(8,128)(2,1)S(1)} collective-permute-done((bf16[256,2048]{1,0:T(8,128)(2,1)S(1)}, bf16[256,2048]{1,0:T(8,128)(2,1)S(1)}, u32[]{:S(2)}, u32[]{:S(2)}) %collective-permute-start.31) | collective-permute-done | bytes 1048608 | tf_op jit(solution)/shard_map/ppermute | solution.py:294
  554.1 7.3 %collective-permute-done.34.refs_2_ = bf16[272,1536]{1,0:T(8,128)(2,1)} collective-permute-done((bf16[272,1536]{1,0:T(8,128)(2,1)}, bf16[272,1536]{1,0:T(8,128)(2,1)}, u32[]{:S(2)}, u32[]{:S(2)}) %collective-permute-start.34) | collective-permute-done | bytes 835616 | tf_op jit(solution)/shard_map/ppermute | solution.py:292
  572.2 13.3 %collective-permute-done.39.refs_5_ = bf16[272,1536]{1,0:T(8,128)(2,1)S(1)} collective-permute-done((bf16[272,1536]{1,0:T(8,128)(2,1)}, bf16[272,1536]{1,0:T(8,128)(2,1)S(1)}, u32[]{:S(2)}, u32[]{:S(2)}) %collective-permute-start.39) | collective-permute-done | bytes 835616 | tf_op jit(solution)/shard_map/ppermute | solution.py:294
  593.9 8.5 %collective-permute-done.41.refs_6_ = bf16[272,1536]{1,0:T(8,128)(2,1)S(1)} collective-permute-done((bf16[272,1536]{1,0:T(8,128)(2,1)S(1)}, bf16[272,1536]{1,0:T(8,128)(2,1)S(1)}, u32[]{:S(2)}, u32[]{:S(2)}) %collective-permute-start.41) | collective-permute-done | bytes 835616 | tf_op jit(solution)/shard_map/ppermute | solution.py:294
  (306 shorter events, 253.5 us)
Async XLA Ops:
  7.2 138.6 %all-gather.6.cloned.1.call-start = ((), (), s32[]{:S(2)}) async-start(), calls=%async_computation.3 | async-start | bytes 7077888 | tf_op jit(solution)/shard_map/all_gather | solution.py:398
  11.3 171.3 %all-gather.8.cloned.1.call-start = ((), (), s32[]{:S(2)}) async-start(), calls=%async_computation.4 | async-start | bytes 9437184 | tf_op jit(solution)/shard_map/all_gather | solution.py:398
  14.5 27.3 %collective-permute-start = (bf16[256,2048]{1,0:T(8,128)(2,1)S(1)}, bf16[256,2048]{1,0:T(8,128)(2,1)}, u32[]{:S(2)}, u32[]{:S(2)}) collective-permute-start(bf16[256,2048]{1,0:T(8,128)(2,1)S(1)} %get-tuple-element.247.refs_3_), channel_id=1, source_target_pairs={{0,1},{1,2},{2,3},{4,5},{5,6},{6,7},{8,9},{9,10},{10,11},{12,13},{... | collective-permute-start | bytes 3145736 | tf_op jit(solution)/shard_map/ppermute | solution.py:292
  20.4 26.6 %collective-permute-start.1 = (bf16[256,2048]{1,0:T(8,128)(2,1)S(1)}, bf16[256,2048]{1,0:T(8,128)(2,1)}, u32[]{:S(2)}, u32[]{:S(2)}) collective-permute-start(bf16[256,2048]{1,0:T(8,128)(2,1)S(1)} %get-tuple-element.247.refs_3_), channel_id=1, source_target_pairs={{3,2},{2,1},{1,0},{7,6},{6,5},{5,4},{11,10},{10,9},{9,8},{15,14},{... | collective-permute-start | bytes 3145736 | tf_op jit(solution)/shard_map/ppermute | solution.py:294
  52.7 150.8 %all-gather.10.cloned.1.call-start = ((), (), s32[]{:S(2)}) async-start(), calls=%async_computation.5 | async-start | bytes 11796480 | tf_op jit(solution)/shard_map/all_gather | solution.py:398
  56.2 272.9 %reduce-scatter.4.cloned.1.call-start = ((), (), s32[]{:S(2)}) async-start(), calls=%async_computation.6 | async-start | bytes 11796480 | tf_op jit(solution)/shard_map/reduce_scatter | solution.py:402
  142.5 36.7 %collective-permute-start.8 = (bf16[256,2048]{1,0:T(8,128)(2,1)}, bf16[256,2048]{1,0:T(8,128)(2,1)}, u32[]{:S(2)}, u32[]{:S(2)}) collective-permute-start(bf16[256,2048]{1,0:T(8,128)(2,1)} %collective-permute-done.refs_2_), channel_id=1, source_target_pairs={{1,2},{2,3},{5,6},{6,7},{9,10},{10,11},{13,14},{14,15},{17,18},{18... | collective-permute-start | bytes 3145736 | tf_op jit(solution)/shard_map/ppermute | solution.py:292
  144.3 34.9 %collective-permute-start.9 = (bf16[256,2048]{1,0:T(8,128)(2,1)}, bf16[256,2048]{1,0:T(8,128)(2,1)}, u32[]{:S(2)}, u32[]{:S(2)}) collective-permute-start(bf16[256,2048]{1,0:T(8,128)(2,1)} %collective-permute-done.1.refs_4_), channel_id=1, source_target_pairs={{2,1},{1,0},{6,5},{5,4},{10,9},{9,8},{14,13},{13,12},{18,17},{17,1... | collective-permute-start | bytes 3145736 | tf_op jit(solution)/shard_map/ppermute | solution.py:294
  179.2 39.5 %collective-permute-start.10 = (bf16[256,2048]{1,0:T(8,128)(2,1)}, bf16[256,2048]{1,0:T(8,128)(2,1)}, u32[]{:S(2)}, u32[]{:S(2)}) collective-permute-start(bf16[256,2048]{1,0:T(8,128)(2,1)} %collective-permute-done.8.refs_1_), channel_id=1, source_target_pairs={{2,3},{6,7},{10,11},{14,15},{18,19},{22,23},{26,27},{30,31}} | collective-permute-start | bytes 3145736 | tf_op jit(solution)/shard_map/ppermute | solution.py:292
  180.9 37.8 %collective-permute-start.11 = (bf16[256,2048]{1,0:T(8,128)(2,1)}, bf16[256,2048]{1,0:T(8,128)(2,1)}, u32[]{:S(2)}, u32[]{:S(2)}) collective-permute-start(bf16[256,2048]{1,0:T(8,128)(2,1)} %collective-permute-done.9.refs_5_), channel_id=1, source_target_pairs={{1,0},{5,4},{9,8},{13,12},{17,16},{21,20},{25,24},{29,28}} | collective-permute-start | bytes 3145736 | tf_op jit(solution)/shard_map/ppermute | solution.py:294
  246.4 191.9 %reduce-scatter.8.cloned.1.call-start = ((), (), s32[]{:S(2)}) async-start(), calls=%async_computation.8 | async-start | bytes 9437184 | tf_op jit(solution)/shard_map/reduce_scatter | solution.py:402
  301.8 225.3 %reduce-scatter.6.cloned.1.call-start = ((), (), s32[]{:S(2)}) async-start(), calls=%async_computation.7 | async-start | bytes 7520256 | tf_op jit(solution)/shard_map/reduce_scatter | solution.py:402
  329.1 35.7 %collective-permute-start.18 = (bf16[320,2048]{1,0:T(8,128)(2,1)}, bf16[320,2048]{1,0:T(8,128)(2,1)}, u32[]{:S(2)}, u32[]{:S(2)}) collective-permute-start(bf16[320,2048]{1,0:T(8,128)(2,1)} %reduce-scatter.4.cloned.1.call-done.refs_3_), channel_id=1, source_target_pairs={{0,1},{1,2},{2,3},{4,5},{5,6},{6,7},{8,9},{9,10},{10,11},{12,13},{... | collective-permute-start | bytes 3932168 | tf_op jit(solution)/shard_map/ppermute | solution.py:292
  333.6 32.4 %collective-permute-start.19 = (bf16[320,2048]{1,0:T(8,128)(2,1)}, bf16[320,2048]{1,0:T(8,128)(2,1)}, u32[]{:S(2)}, u32[]{:S(2)}) collective-permute-start(bf16[320,2048]{1,0:T(8,128)(2,1)} %reduce-scatter.4.cloned.1.call-done.refs_3_), channel_id=1, source_target_pairs={{3,2},{2,1},{1,0},{7,6},{6,5},{5,4},{11,10},{10,9},{9,8},{15,14},{... | collective-permute-start | bytes 3932168 | tf_op jit(solution)/shard_map/ppermute | solution.py:294
  366.7 32.8 %collective-permute-start.21 = (bf16[320,2048]{1,0:T(8,128)(2,1)}, bf16[320,2048]{1,0:T(8,128)(2,1)S(1)}, u32[]{:S(2)}, u32[]{:S(2)}) collective-permute-start(bf16[320,2048]{1,0:T(8,128)(2,1)} %collective-permute-done.19.refs_4_), channel_id=1, source_target_pairs={{2,1},{1,0},{6,5},{5,4},{10,9},{9,8},{14,13},{13,12},{18,17},{17,1... | collective-permute-start | bytes 3932168 | tf_op jit(solution)/shard_map/ppermute | solution.py:294
  399.6 28.7 %collective-permute-start.22 = (bf16[320,2048]{1,0:T(8,128)(2,1)S(1)}, bf16[320,2048]{1,0:T(8,128)(2,1)S(1)}, u32[]{:S(2)}, u32[]{:S(2)}) collective-permute-start(bf16[320,2048]{1,0:T(8,128)(2,1)S(1)} %collective-permute-done.20.refs_1_), channel_id=1, source_target_pairs={{2,3},{6,7},{10,11},{14,15},{18,19},{22,23},{26,27},{30,31}} | collective-permute-start | bytes 3932168 | tf_op jit(solution)/shard_map/ppermute | solution.py:292
  400.3 30.6 %collective-permute-start.23 = (bf16[320,2048]{1,0:T(8,128)(2,1)S(1)}, bf16[320,2048]{1,0:T(8,128)(2,1)S(1)}, u32[]{:S(2)}, u32[]{:S(2)}) collective-permute-start(bf16[320,2048]{1,0:T(8,128)(2,1)S(1)} %collective-permute-done.21.refs_5_), channel_id=1, source_target_pairs={{1,0},{5,4},{9,8},{13,12},{17,16},{21,20},{25,24},{29,28}} | collective-permute-start | bytes 3932168 | tf_op jit(solution)/shard_map/ppermute | solution.py:294
  438.3 27.8 %collective-permute-start.26 = (bf16[256,2048]{1,0:T(8,128)(2,1)}, bf16[256,2048]{1,0:T(8,128)(2,1)}, u32[]{:S(2)}, u32[]{:S(2)}) collective-permute-start(bf16[256,2048]{1,0:T(8,128)(2,1)} %reduce-scatter.8.cloned.1.call-done.refs_3_), channel_id=1, source_target_pairs={{0,1},{1,2},{2,3},{4,5},{5,6},{6,7},{8,9},{9,10},{10,11},{12,13},{... | collective-permute-start | bytes 3145736 | tf_op jit(solution)/shard_map/ppermute | solution.py:292
  467.1 27.4 %collective-permute-start.29 = (bf16[256,2048]{1,0:T(8,128)(2,1)}, bf16[256,2048]{1,0:T(8,128)(2,1)S(1)}, u32[]{:S(2)}, u32[]{:S(2)}) collective-permute-start(bf16[256,2048]{1,0:T(8,128)(2,1)} %collective-permute-done.27.refs_4_), channel_id=1, source_target_pairs={{2,1},{1,0},{6,5},{5,4},{10,9},{9,8},{14,13},{13,12},{18,17},{17,1... | collective-permute-start | bytes 3145736 | tf_op jit(solution)/shard_map/ppermute | solution.py:294
  471.4 27.0 %collective-permute-start.32 = (bf16[256,2048]{1,0:T(8,128)(2,1)S(1)}, bf16[256,2048]{1,0:T(8,128)(2,1)S(1)}, u32[]{:S(2)}, u32[]{:S(2)}) collective-permute-start(bf16[256,2048]{1,0:T(8,128)(2,1)S(1)} %get-tuple-element.235), channel_id=1, source_target_pairs={{0,1},{1,2},{4,5},{5,6},{8,9},{9,10},{12,13},{13,14},{16,17},{17,1... | collective-permute-start | bytes 3145736 | tf_op jit(solution)/shard_map/ppermute | solution.py:328
  521.5 27.2 %collective-permute-start.36 = (bf16[256,2048]{1,0:T(8,128)(2,1)}, bf16[256,2048]{1,0:T(8,128)(2,1)}, u32[]{:S(2)}, u32[]{:S(2)}) collective-permute-start(bf16[256,2048]{1,0:T(8,128)(2,1)} %get-tuple-element.233), channel_id=1, source_target_pairs={{0,1},{1,2},{2,3},{4,5},{5,6},{6,7},{8,9},{9,10},{10,11},{12,13},{... | collective-permute-start | bytes 3145736 | tf_op jit(solution)/shard_map/ppermute | solution.py:328
  525.8 28.3 %collective-permute-start.37 = (bf16[256,2048]{1,0:T(8,128)(2,1)}, bf16[256,2048]{1,0:T(8,128)(2,1)}, u32[]{:S(2)}, u32[]{:S(2)}) collective-permute-start(bf16[256,2048]{1,0:T(8,128)(2,1)} %get-tuple-element.232), channel_id=1, source_target_pairs={{3,2},{2,1},{1,0},{7,6},{6,5},{5,4},{11,10},{10,9},{9,8},{15,14},{... | collective-permute-start | bytes 3145736 | tf_op jit(solution)/shard_map/ppermute | solution.py:329
  527.2 34.3 %collective-permute-start.34 = (bf16[272,1536]{1,0:T(8,128)(2,1)}, bf16[272,1536]{1,0:T(8,128)(2,1)}, u32[]{:S(2)}, u32[]{:S(2)}) collective-permute-start(bf16[272,1536]{1,0:T(8,128)(2,1)} %reduce-scatter.6.cloned.1.call-done.refs_3_), channel_id=1, source_target_pairs={{0,1},{1,2},{2,3},{4,5},{5,6},{6,7},{8,9},{9,10},{10,11},{12,13},{... | collective-permute-start | bytes 2506760 | tf_op jit(solution)/shard_map/ppermute | solution.py:292
  532.6 33.9 %collective-permute-start.35 = (bf16[272,1536]{1,0:T(8,128)(2,1)}, bf16[272,1536]{1,0:T(8,128)(2,1)}, u32[]{:S(2)}, u32[]{:S(2)}) collective-permute-start(bf16[272,1536]{1,0:T(8,128)(2,1)} %reduce-scatter.6.cloned.1.call-done.refs_3_), channel_id=1, source_target_pairs={{3,2},{2,1},{1,0},{7,6},{6,5},{5,4},{11,10},{10,9},{9,8},{15,14},{... | collective-permute-start | bytes 2506760 | tf_op jit(solution)/shard_map/ppermute | solution.py:294
  (85 other events, 1179.9 us)
Sparse Core Ops, SparseCore 0:
  11.5 48.5 all-gather.5
  62.5 54.3 all-gather.7
  119.4 63.2 all-gather.9
  246.5 82.5 reduce-scatter.3
  332.4 71.2 reduce-scatter.7
  438.4 62.6 reduce-scatter.5

commit v4 on v3

--- a/solution.py
+++ b/solution.py
@@ -60,6 +60,109 @@
     return jnp.concatenate(parts, axis)
 
 
+def columns_kernel(n, parts, context_ref, in_ref, *out_refs):
+    for c in range(n):
+
+        @pl.when(context_ref[0] == c)
+        def _():
+            for out_ref, segments in zip(out_refs, parts):
+                at = 0
+                for base, width in segments:
+                    out_ref[:, at : at + width] = in_ref[
+                        :, base + c * width : base + (c + 1) * width
+                    ]
+                    at += width
+
+
+def take_columns(array, parts, context, n):
+    rows, columns = array.shape
+    step = 32
+    widths = [sum(width for _, width in segments) for segments in parts]
+    return pl.pallas_call(
+        functools.partial(columns_kernel, n, parts),
+        grid_spec=pltpu.PrefetchScalarGridSpec(
+            num_scalar_prefetch=1,
+            grid=(rows // step,),
+            in_specs=[pl.BlockSpec((step, columns), lambda i, context: (i, 0))],
+            out_specs=[pl.BlockSpec((step, width), lambda i, context: (i, 0)) for width in widths],
+        ),
+        out_shape=[jax.ShapeDtypeStruct((rows, width), array.dtype) for width in widths],
+        compiler_params=pltpu.CompilerParams(vmem_limit_bytes=14 * 2**20),
+        cost_estimate=pl.CostEstimate(
+            flops=0, bytes_accessed=2 * rows * (columns + sum(widths)), transcendentals=0
+        ),
+    )(context.reshape(1), array)
+
+
+def rows_kernel(context_ref, in_ref, out_ref):
+    out_ref[...] = in_ref[...]
+
+
+def take_rows(array, segments, context):
+    rows = sum(width for _, width in segments)
+    columns = array.shape[1]
+    step = HEAD_DIM
+
+    def source(i, context):
+        at, block = 0, 0
+        for base, width in segments:
+            block = jnp.where(
+                i >= at // step, base // step + context[0] * (width // step) + i - at // step, block
+            )
+            at += width
+        return (block, 0)
+
+    return pl.pallas_call(
+        rows_kernel,
+        grid_spec=pltpu.PrefetchScalarGridSpec(
+            num_scalar_prefetch=1,
+            grid=(rows // step,),
+            in_specs=[pl.BlockSpec((step, columns), source)],
+            out_specs=pl.BlockSpec((step, columns), lambda i, context: (i, 0)),
+        ),
+        out_shape=jax.ShapeDtypeStruct((rows, columns), array.dtype),
+        compiler_params=pltpu.CompilerParams(vmem_limit_bytes=8 * 2**20),
+        cost_estimate=pl.CostEstimate(
+            flops=0, bytes_accessed=4 * rows * columns, transcendentals=0
+        ),
+    )(context.reshape(1), array)
+
+
+def join_kernel(places, *refs):
+    *parts, out_ref, held, taken, given = refs
+    copies, gives = [], []
+    for i, (part, (row, column)) in enumerate(zip(parts, places)):
+        where = (pl.ds(row, part.shape[0]), pl.ds(column, part.shape[1]))
+        copies.append(pltpu.make_async_copy(part, held.at[where], taken.at[i]))
+        gives.append(pltpu.make_async_copy(held.at[where], out_ref.at[where], given.at[i]))
+    for copy in copies:
+        copy.start()
+    for copy, give in zip(copies, gives):
+        copy.wait()
+        give.start()
+    for give in gives:
+        give.wait()
+
+
+def join(parts, places, shape):
+    anywhere = pl.BlockSpec(memory_space=pl.ANY)
+    return pl.pallas_call(
+        functools.partial(join_kernel, places),
+        in_specs=[anywhere] * len(parts),
+        out_specs=anywhere,
+        scratch_shapes=[
+            pltpu.VMEM(shape, parts[0].dtype),
+            pltpu.SemaphoreType.DMA((len(parts),)),
+            pltpu.SemaphoreType.DMA((len(parts),)),
+        ],
+        out_shape=jax.ShapeDtypeStruct(shape, parts[0].dtype),
+        compiler_params=pltpu.CompilerParams(vmem_limit_bytes=8 * 2**20),
+        cost_estimate=pl.CostEstimate(
+            flops=0, bytes_accessed=4 * shape[0] * shape[1], transcendentals=0
+        ),
+    )(*parts)
+
+
 def lane_mask(shape, head):
     lane = lax.broadcasted_iota(jnp.int32, shape, len(shape) - 1)
     return (lane // HEAD_DIM) == head
@@ -80,10 +183,15 @@
 
 
 def attend_kernel(
-    place_ref, q_ref, k_ref, v_ref, cos_ref, low_ref, high_ref,
-    out_ref, total_ref, qr_ref, kr_ref, vr_ref,
+    place_ref, q_main, k_main, v_main, q_rest, k_rest, v_rest, cos_ref, low_ref, high_ref,
+    out_ref, total_ref, qr_ref, kr_ref, vr_ref, q_ref, k_ref, v_ref,
 ):
     tokens = q_ref.shape[0]
+    for ref, main, rest in (
+        (q_ref, q_main, q_rest), (k_ref, k_main, k_rest), (v_ref, v_main, v_rest)
+    ):
+        ref[: main.shape[0], :] = main[...]
+        ref[main.shape[0] :, :] = rest[...]
     for p in range(tokens // BLK):
         here = pl.ds(p * BLK, BLK)
         there = stored(place_ref, p)
@@ -97,18 +205,25 @@
         last = (tile + 1) * TILE
         count = last - first
         query = qr_ref[pl.ds(tile * TILE, TILE), :]
-        keys = kr_ref[pl.ds(first, count), :]
-        values = vr_ref[pl.ds(first, count), :]
-        row = lax.broadcasted_iota(jnp.int32, (TILE, count), 0) + (tile * TILE - first)
-        allowed = lax.broadcasted_iota(jnp.int32, (TILE, count), 1) <= row
+        spans = [(tile * TILE, TILE)] + ([(first, count - TILE)] if count > TILE else [])
+        keys = [kr_ref[pl.ds(*span), :] for span in spans]
+        values = [vr_ref[pl.ds(*span), :] for span in spans]
+        square = (TILE, TILE)
+        allowed = lax.broadcasted_iota(jnp.int32, square, 1) <= lax.broadcasted_iota(
+            jnp.int32, square, 0
+        )
         outs, totals = [], []
         for head in range(2):
             mine = jnp.where(lane_mask(query.shape, head), query, jnp.zeros_like(query))
-            scores = jnp.where(allowed, dot(mine, keys, ((1,), (1,))), floor_score)
-            highest = jnp.max(scores, axis=1, keepdims=True)
-            weights = jnp.exp(scores - highest)
-            total = jnp.sum(weights, axis=1, keepdims=True)
-            outs.append(dot(weights.astype(BF16), values) / total)
+            scores = [dot(mine, part, ((1,), (1,))) for part in keys]
+            scores[0] = jnp.where(allowed, scores[0], floor_score)
+            highest = functools.reduce(
+                jnp.maximum, [jnp.max(part, axis=1, keepdims=True) for part in scores]
+            )
+            weights = [jnp.exp(part - highest) for part in scores]
+            total = sum(jnp.sum(part, axis=1, keepdims=True) for part in weights)
+            out = sum(dot(part.astype(BF16), value) for part, value in zip(weights, values))
+            outs.append(out / total)
             totals.append(highest + jnp.log(total))
         wide = (TILE, 2 * HEAD_DIM)
         first_head = lane_mask(wide, 0)
@@ -177,23 +292,25 @@
     sums_ref[...] = jnp.concatenate(sums + [zero], 0)
 
 
-def attend(place, projected, tables, heads):
-    tokens = projected.shape[0]
+def attend(place, main, rest, tables, heads):
+    tokens = main.shape[0] + rest.shape[0]
     pairs = heads // 2
     wide = 2 * HEAD_DIM
 
-    def block(offset):
-        return pl.BlockSpec((tokens, wide), lambda h, place: (0, h + offset))
+    def block(offset, rows=tokens):
+        return pl.BlockSpec((rows, wide), lambda h, place: (0, h + offset))
 
     table = pl.BlockSpec((tokens, wide), lambda h, place: (0, 0))
     shape = (tokens, heads * HEAD_DIM)
+    parts = [block(i * pairs, part.shape[0]) for part in (main, rest) for i in range(3)]
     return pl.pallas_call(
         attend_kernel,
         grid_spec=pltpu.PrefetchScalarGridSpec(
             num_scalar_prefetch=1,
             grid=(pairs,),
-            in_specs=[block(0), block(pairs), block(2 * pairs), table, table, table],
+            in_specs=parts + [table, table, table],
             out_specs=[block(0)] * 5,
+            scratch_shapes=[pltpu.VMEM((tokens, wide), F32)] * 3,
         ),
         out_shape=[
             jax.ShapeDtypeStruct(shape, BF16),
@@ -202,12 +319,12 @@
             jax.ShapeDtypeStruct(shape, BF16),
             jax.ShapeDtypeStruct(shape, BF16),
         ],
-        compiler_params=pltpu.CompilerParams(vmem_limit_bytes=48 * 2**20),
+        compiler_params=pltpu.CompilerParams(vmem_limit_bytes=28 * 2**20),
         cost_estimate=pl.CostEstimate(
             flops=8 * tokens * tokens * wide * pairs, bytes_accessed=30 * tokens * wide * pairs,
             transcendentals=tokens * tokens * heads,
         ),
-    )(place, projected, projected, projected, *tables)
+    )(place, main, main, main, rest, rest, rest, *tables)
 
 
 def attend_back(place, query, keys, values, total, out, grad, tables, heads):
@@ -241,15 +358,17 @@
     return jnp.sum(jnp.where(assignment[None, :] == number[:, None], number[None, :], 0), axis=1)
 
 
-def group_positions(positions, assignment, context, group):
+def group_positions(positions, assignment, context, group, turn):
     if group == SEQ_LEN:
         blocks_here = positions.shape[0] // BLK
         start = positions[0] - lax.dynamic_index_in_dim(
             assignment, context * blocks_here, 0, keepdims=False
         ) * BLK
-        index = assignment[:, None] * BLK + jnp.arange(BLK, dtype=jnp.int32)[None, :]
+        turned = jnp.roll(assignment, -turn * blocks_here)
+        index = turned[:, None] * BLK + jnp.arange(BLK, dtype=jnp.int32)[None, :]
         return start + index.reshape(group)
-    return lax.all_gather(positions, "context", axis=0, tiled=True)
+    whole = lax.all_gather(positions, "context", axis=0, tiled=True)
+    return jnp.roll(whole, -turn * positions.shape[0])
 
 
 def rotary_tables(positions):
@@ -302,19 +421,27 @@
     def latest(self, arrays):
         self.before[-1], self.after[-1] = arrays
 
+    def rows(self, context, turn, first, count):
+        n = lax.axis_size("context")
+        before = self.before[::-1] + [self.block] + self.after
+        missing = n - 1 - len(self.before)
+        return place(context, turn, before, missing, first, count)
+
     def whole(self, context):
-        return place(context, self.before[::-1] + [self.block] + self.after)
+        n = lax.axis_size("context")
+        return self.rows(context, jnp.zeros_like(context), 0, n)
 
 
 class LineScatter:
-    def __init__(self, partial):
-        self.partial, self.steps = partial, 0
+    def __init__(self, partial, turn):
+        self.partial, self.turn, self.steps = partial, turn, 0
         self.right = self.left = None
 
     def mine(self, j):
         n = lax.axis_size("context")
         rows = self.partial.shape[0] // n
-        return lax.dynamic_slice_in_dim(self.partial, jnp.clip(j, 0, n - 1) * rows, rows, 0)
+        at = (jnp.clip(j, 0, n - 1) + n - self.turn) % n
+        return lax.dynamic_slice_in_dim(self.partial, at * rows, rows, 0)
 
     def step(self, *after):
         n = lax.axis_size("context")
@@ -342,60 +469,90 @@
         return own + self.right.astype(F32) + self.left.astype(F32)
 
 
-def place_kernel(context_ref, *refs):
+def place_kernel(n, missing, first, at_ref, *refs):
     *blocks, out_ref, held, taken, given = refs
-    n = (len(blocks) + 1) // 2
-    rows = blocks[0].shape[0]
+    count, rows = held.shape[0], held.shape[1]
 
     def give(j):
         return pltpu.make_async_copy(
             held.at[j], out_ref.at[pl.ds(j * rows, rows), :], given.at[j]
         )
 
-    for c in range(n):
-
-        @pl.when(context_ref[0] == c)
-        def _():
-            copies = [
-                pltpu.make_async_copy(blocks[j - c + n - 1], held.at[j], taken.at[j])
-                for j in range(n)
-            ]
-            for copy in copies:
-                copy.start()
-            for j, copy in enumerate(copies):
-                copy.wait()
-                give(j).start()
-            for j in range(n):
-                give(j).wait()
-
-
-def place(context, line):
-    n = (len(line) + 1) // 2
+    def move(context, turn):
+        copies = []
+        for j in range(count):
+            at = (turn + first + j) % n - context + n - 1 - missing
+            if 0 <= at < len(blocks):
+                copies.append((j, pltpu.make_async_copy(blocks[at], held.at[j], taken.at[j])))
+        for _, copy in copies:
+            copy.start()
+        for j, copy in copies:
+            copy.wait()
+            give(j).start()
+        for j, _ in copies:
+            give(j).wait()
+
+    for context in range(n):
+        for turn in range(2):
+
+            @pl.when((at_ref[0] == context) & (at_ref[1] == turn))
+            def _():
+                move(context, turn)
+
+
+def place(context, turn, line, missing, first, count):
+    n = (len(line) + 1) // 2 + missing
     rows, columns = line[0].shape
     anywhere = pl.BlockSpec(memory_space=pl.ANY)
     return pl.pallas_call(
-        place_kernel,
+        functools.partial(place_kernel, n, missing, first),
         grid_spec=pltpu.PrefetchScalarGridSpec(
             num_scalar_prefetch=1,
             grid=(1,),
             in_specs=[anywhere] * len(line),
             out_specs=anywhere,
             scratch_shapes=[
-                pltpu.VMEM((n, rows, columns), line[0].dtype),
-                pltpu.SemaphoreType.DMA((n,)),
-                pltpu.SemaphoreType.DMA((n,)),
+                pltpu.VMEM((count, rows, columns), line[0].dtype),
+                pltpu.SemaphoreType.DMA((count,)),
+                pltpu.SemaphoreType.DMA((count,)),
             ],
         ),
-        out_shape=jax.ShapeDtypeStruct((n * rows, columns), line[0].dtype),
-        compiler_params=pltpu.CompilerParams(vmem_limit_bytes=32 * 2**20),
+        out_shape=jax.ShapeDtypeStruct((count * rows, columns), line[0].dtype),
+        compiler_params=pltpu.CompilerParams(vmem_limit_bytes=8 * 2**20),
         cost_estimate=pl.CostEstimate(
-            flops=0, bytes_accessed=4 * n * rows * columns, transcendentals=0
-        ),
-    )(context.reshape(1), *line)
+            flops=0, bytes_accessed=4 * count * rows * columns, transcendentals=0
+        ),
+    )(jnp.stack([context, turn]).astype(jnp.int32), *line)
 
 
 def gather_shard(x):
     return lax.all_gather(x, "shard", axis=0, tiled=True)
+
+
+def swap_sum(vector, axis):
+    n = lax.axis_size(axis)
+    if n & (n - 1):
+        return lax.psum(vector, axis)
+    k = 1
+    while k < n:
+        vector = vector + lax.ppermute(vector, axis, [(i, i ^ k) for i in range(n)])
+        k *= 2
+    return vector
+
+
+def swap_gather(vector, axis):
+    n = lax.axis_size(axis)
+    if n & (n - 1):
+        return lax.all_gather(vector, axis)
+    here = lax.axis_index(axis)
+    held = vector[None]
+    k = 1
+    while k < n:
+        held = jnp.concatenate(
+            [held, lax.ppermute(held, axis, [(i, i ^ k) for i in range(n)])], axis=0
+        )
+        k *= 2
+    return jnp.stack([lax.dynamic_index_in_dim(held, j ^ here, 0, keepdims=False) for j in range(n)])
 
 
 def scatter_shard(x):
@@ -421,7 +578,7 @@
         in_specs=[pl.BlockSpec((n, step, parts.shape[2]), lambda i: (0, i, 0))],
         out_specs=pl.BlockSpec((step, columns), lambda i: (i, 0)),
         out_shape=jax.ShapeDtypeStruct((rows, columns), F32),
-        compiler_params=pltpu.CompilerParams(vmem_limit_bytes=48 * 2**20),
+        compiler_params=pltpu.CompilerParams(vmem_limit_bytes=14 * 2**20),
         cost_estimate=pl.CostEstimate(
             flops=0, bytes_accessed=5 * rows * columns, transcendentals=0
         ),
@@ -443,7 +600,7 @@
         out_specs=pl.BlockSpec((step, columns), lambda i: (i, 0)),
         out_shape=jax.ShapeDtypeStruct(whole.shape, F32),
         input_output_aliases={1: 0},
-        compiler_params=pltpu.CompilerParams(vmem_limit_bytes=48 * 2**20),
+        compiler_params=pltpu.CompilerParams(vmem_limit_bytes=14 * 2**20),
         cost_estimate=pl.CostEstimate(
             flops=0, bytes_accessed=6 * rows * columns, transcendentals=0
         ),
@@ -476,6 +633,7 @@
         in_specs=[pl.BlockSpec((1, step, columns), source)],
         out_specs=pl.BlockSpec((step, columns), lambda b: (b, 0)),
         out_shape=jax.ShapeDtypeStruct((n * rows, columns), F32),
+        compiler_params=pltpu.CompilerParams(vmem_limit_bytes=8 * 2**20),
         cost_estimate=pl.CostEstimate(
             flops=0, bytes_accessed=6 * n * rows * columns, transcendentals=0
         ),
@@ -529,42 +687,62 @@
     normalized = centred * inverse_std
     normed_here = (normalized * gain + shift).astype(BF16)
 
-    weight_qkv = gather_shard(take(input_weight, qkv_columns, context, 1))
-    gate, (normed_here, input_weight, output_weight) = close(
-        [up], normed_here, input_weight, output_weight
-    )
-    weight_hidden = gather_shard(take(input_weight, hidden_columns, context, 1))
-    if inner is not None:
-        weight_out = gather_shard(take(output_weight, inner, context, 0))
-    else:
-        weight_out = take(gather_shard(output_weight), segments, context, 0)
+    (in_part,) = take_columns(
+        input_weight, [qkv_columns + hidden_columns], context, context_size
+    )
+    weight_in = gather_shard(in_part)
+    weight_qkv, weight_hidden = weight_in[:, : 3 * attn], weight_in[:, 3 * attn :]
+    out_part = take_rows(output_weight, inner, context) if inner is not None else output_weight
+    gate, (normed_here,) = close([up], normed_here)
+    weight_out = gather_shard(out_part)
+    if inner is None:
+        weight_out = take(weight_out, segments, context, 0)
     bias_qkv = take(bias_in, qkv_columns, context, 0)
     bias_hidden = take(bias_in, hidden_columns, context, 0)
-    places = causal_blocks(assignment)
+
+    turn = (2 * context >= context_size).astype(jnp.int32)
+    places = causal_blocks(jnp.roll(assignment, -turn * (tokens_here // BLK)))
 
     norm = LineGather(normed_here)
-    for t in range(steps):
+    for t in range(steps - 1):
         gate = norm.step(*gate)
         if t == 0:
             positions = tie(positions, *gate)
-            tables = rotary_tables(group_positions(positions, assignment, context, group))
-    normed = norm.whole(context)
-
-    normed = tie(normed, *gate)
-    projected = dot(normed, weight_qkv) + bias_qkv
+            tables = rotary_tables(
+                group_positions(positions, assignment, context, group, turn)
+            )
+
+    normed_main = norm.rows(context, turn, 0, context_size - 1)
+    norm.step()
+    projected_main = dot(normed_main, weight_qkv) + bias_qkv
+    hidden_main = dot(tie(normed_main, projected_main), weight_hidden) + bias_hidden
+    active_main = gelu_tanh(hidden_main).astype(BF16)
+    gate, (projected_main, active_main, hidden_main) = close(
+        [norm], projected_main, active_main, hidden_main
+    )
+    normed_rest = norm.rows(context, turn, context_size - 1, 1)
+
     up.step(*gate)
-    attended, log_total, query, keys, values = attend(places, projected, tables, heads)
-    gate, (attended, normed) = close([up], attended, normed)
+    projected_rest = dot(normed_rest, weight_qkv) + bias_qkv
+    attended, log_total, query, keys, values = attend(
+        places, projected_main, projected_rest, tables, heads
+    )
+    gate, (attended, normed_rest) = close([up], attended, normed_rest)
+
     for t in range(steps - 2):
         up.step(*gate)
-    hidden_pre = dot(normed, weight_hidden) + bias_hidden
-    activation = gelu_tanh(hidden_pre).astype(BF16)
-    joined = jnp.concatenate([attended, activation], axis=1)
+    hidden_rest = dot(normed_rest, weight_hidden) + bias_hidden
+    active_rest = gelu_tanh(hidden_rest).astype(BF16)
+    joined = join(
+        [attended, active_main, active_rest],
+        [(0, 0), (0, attn), (active_main.shape[0], attn)],
+        (group, attn + active_main.shape[1]),
+    )
     partial_out = dot(joined, weight_out).astype(BF16)
     gate, (partial_out, joined) = close([up], partial_out, joined)
-    upstream = up.whole(context)
-
-    out = LineScatter(partial_out)
+    upstream = up.rows(context, turn, 0, context_size)
+
+    out = LineScatter(partial_out, turn)
     out.step()
     out_grad = dot(joined, upstream, ((0,), (0,))).astype(BF16)
     gate, (out_grad, upstream) = close([out], out_grad, upstream)
@@ -572,11 +750,16 @@
         out_grad_sum = scatter_shard(out_grad)
 
     out.step()
-    joined_grad = dot(upstream, weight_out[attn:], ((1,), (1,)))
-    hidden_grad = jax.vjp(gelu_tanh, hidden_pre)[1](joined_grad)[0]
-    hidden_rounded = hidden_grad.astype(BF16)
-    hidden_sum = jnp.sum(hidden_grad, axis=0)
-    gate, (hidden_rounded, upstream) = close([out], hidden_rounded, upstream)
+    cut = hidden_main.shape[0]
+    hidden_rounded, hidden_sum = [], 0.0
+    for pre, part in ((hidden_main, upstream[:cut]), (hidden_rest, upstream[cut:])):
+        joined_grad = dot(part, weight_out[attn:], ((1,), (1,)))
+        hidden_grad = jax.vjp(gelu_tanh, pre)[1](joined_grad)[0]
+        hidden_rounded.append(hidden_grad.astype(BF16))
+        hidden_sum = hidden_sum + jnp.sum(hidden_grad, axis=0)
+    hidden_rounded = join(hidden_rounded, [(0, 0), (cut, 0)], (group, hidden_sum.shape[0]))
+    normed = norm.rows(context, turn, 0, context_size)
+    gate, (hidden_rounded, upstream, normed) = close([out], hidden_rounded, upstream, normed)
 
     for t in range(steps - 2):
         out.step()
@@ -598,68 +781,70 @@
     dq, dk, dv, sums = attend_back(
         places, query, keys, values, log_total, attended, attended_grad, tables, heads
     )
-    qkv_rounded = jnp.concatenate([dq, dk, dv], axis=1)
+    qkv_rounded = join([dq, dk, dv], [(0, 0), (0, attn), (0, 2 * attn)], (group, 3 * attn))
     gate, (qkv_rounded,) = close(gathers, qkv_rounded)
 
     for gather in gathers:
         gather.step()
+    qkv_in_grad = dot(normed, qkv_rounded, ((0,), (0,))).astype(BF16)
+    gate, (qkv_in_grad, qkv_rounded, normed_grad) = close(
+        gathers, qkv_in_grad, qkv_rounded, normed_grad
+    )
+    qkv_in_sum = scatter_shard(qkv_in_grad)
+
+    for gather in gathers:
+        for t in range(2, steps):
+            gather.step()
     normed_grad = normed_grad + dot(qkv_rounded, weight_qkv, ((1,), (1,)))
     gain_sum = jnp.sum(normed_grad * ((normed.astype(F32) - shift) / gain), axis=0)
     shift_sum = jnp.sum(normed_grad, axis=0)
     partial_grad = normed_grad.astype(BF16)
-    gate, (partial_grad, qkv_rounded) = close(gathers, partial_grad, qkv_rounded)
-
-    grad = LineScatter(partial_grad)
-    for gather in gathers:
-        for t in range(2, steps):
-            gather.step()
-    grad.step()
-    qkv_in_grad = dot(normed, qkv_rounded, ((0,), (0,))).astype(BF16)
-    gate, (qkv_in_grad,) = close(gathers + [grad], qkv_in_grad)
-    vectors = jnp.concatenate(
-        [sums[0], sums[1], sums[2], hidden_sum, jnp.sum(cotangent, axis=0), gain_sum, shift_sum]
-    )
-    wide = 3 * attn
-    extra = -(-vectors.shape[0] // (16 * wide)) * 16
-    vectors = jnp.pad(vectors, (0, extra * wide - vectors.shape[0])).reshape(1, extra, wide)
-    vectors = jnp.broadcast_to(vectors.astype(BF16), (shard_size, extra, wide))
-    qkv_in_sum = scatter_shard(
-        jnp.concatenate([qkv_in_grad.reshape(shard_size, rows_here, wide), vectors], 1).reshape(
-            -1, wide
+    gate, (partial_grad, gain_sum, shift_sum) = close(gathers, partial_grad, gain_sum, shift_sum)
+    grad = LineScatter(partial_grad, turn)
+
+    hidden_gather, qkv_gather = LineGather(hidden_in_sum), LineGather(qkv_in_sum)
+    done = ()
+    if inner is not None:
+        done = (
+            finish_out(gathers[0].whole(context).reshape(context_size, -1, D), inner),
         )
-    )
-
-    hidden_gather, qkv_gather = LineGather(hidden_in_sum), LineGather(qkv_in_sum)
-    if inner is not None:
-        weight_out_grad = finish_out(
-            tie(gathers[0].whole(context), *gate).reshape(context_size, -1, D), inner
-        )
-        done = (weight_out_grad,)
-    else:
-        done = ()
     for t in range(steps):
         lines = [hidden_gather]
         hidden_gather.step(*gate)
-        if t == steps - 1 and grad.steps < steps:
-            grad.step()
+        if t > 0:
+            grad.step(*gate)
             lines.append(grad)
-        gate, done = close(lines, *done)
-        if inner is not None and t == 0:
-            (weight_out_grad,) = done
-            done = ()
-    hidden_parts = hidden_gather.whole(context).reshape(context_size, rows_here, -1)
-    weight_in_grad = finish_hidden(
-        tie(hidden_parts, *gate), hidden_columns, rows_here, input_weight.shape[1]
-    )
+        gate, out = close(lines, *done)
+        if done:
+            (weight_out_grad,), done = out, ()
+
     for t in range(steps):
-        lines = [qkv_gather]
         qkv_gather.step(*gate)
         if grad.steps < steps:
-            grad.step()
-            lines.append(grad)
-        gate, done = close(lines, *((weight_in_grad,) if t == 0 else ()))
-        if t == 0:
+            grad.step(*gate)
+        done = ()
+        if t == 1:
+            hidden_parts = tie(hidden_gather.whole(context), *gate)
+            done = (
+                finish_hidden(
+                    hidden_parts.reshape(context_size, rows_here, -1),
+                    hidden_columns,
+                    rows_here,
+                    input_weight.shape[1],
+                ),
+            )
+        gate, done = close([qkv_gather], *done)
+        if done:
             (weight_in_grad,) = done
+        if t == steps - 2:
+            vectors = jnp.concatenate(
+                [sums[0], sums[1], sums[2], hidden_sum, jnp.sum(cotangent, axis=0), gain_sum, shift_sum]
+            )
+            vectors = swap_gather(swap_sum(tie(vectors, *gate), "shard"), "context")
+            columns = 3 * attn + hidden_sum.shape[0]
+            bias_in_sum = untake(vectors[:, :columns], qkv_columns + hidden_columns, 0)
+            others = jnp.sum(vectors[:, columns:], axis=0)
+
     if inner is None:
         whole = jnp.zeros((D + FF, D), BF16)
         at = 0
@@ -669,13 +854,8 @@
             )
             at += width
         weight_out_grad = lax.psum(scatter_shard(whole), "context").astype(F32)
-    qkv_parts = qkv_gather.whole(context).reshape(context_size, rows_here + extra, wide)
+    qkv_parts = qkv_gather.whole(context).reshape(context_size, rows_here, -1)
     weight_in_grad = finish_qkv(weight_in_grad, qkv_parts, qkv_columns)
-
-    vectors = qkv_parts[:, rows_here:].astype(F32).reshape(context_size, -1)
-    columns = wide + hidden_sum.shape[0]
-    bias_in_sum = untake(vectors[:, :columns], qkv_columns + hidden_columns, 0)
-    others = jnp.sum(vectors[:, columns : columns + 3 * D], axis=0)
 
     def own_share(vector):
         length = vector.shape[0] // shard_size

time: 627 us -> 603 us (0.962)
  local copies, waits for them, and re-layouts: 51.7 us -> 27.9 us
  waiting for transfers between devices: 197 us -> 174 us
  starting transfers between devices: 94 us -> 108 us
  Pallas kernels: 74.9 us -> 83.1 us
    pallas_call x5 -> x12, Pallas kernels: 9.31 us -> 23.4 us  [the longest x7 15.6 us: place(): pl.pallas_call(functools.partial(place_kernel, n, missing, first), grid_s...]
    ppermute x6, waiting for transfers between devices: 14.8 us -> 1.97 us  [step(): self.right = lax.ppermute(right, 'context', [(a, a + 1) for a in range(t)])]
    concatenate x4 -> x3, other arithmetic: 12.2 us -> 0.26 us  [the longest x2 0.18 us: swap_gather(): jnp.concatenate([held, lax.ppermute(held, axis, [(i, i ^ k) for i in rang...]
    unnamed x138 -> x150, local copies, waits for them, and re-layouts: 31.5 us -> 21.7 us
    ppermute x15, starting transfers between devices: 33.2 us -> 41.9 us  [step(): lax.ppermute(right, 'context', [(a, a + 1) for a in range(t - 1, n - 1)])]
    dynamic_slice x8 -> x2, local copies, waits for them, and re-layouts: 8.12 us -> 0.26 us  [take(): lax.dynamic_slice_in_dim(array, base + context * width, width, axis)]
    ppermute x0 -> x5, waiting for transfers between devices: none -> 7.22 us  [the longest x2 3.96 us: swap_gather(): lax.ppermute(held, axis, [(i, i ^ k) for i in range(n)])]
    reduce_scatter x3, waiting for transfers between devices: 7.16 us -> 0.01 us  [scatter_shard(): return lax.psum_scatter(x, 'shard', scatter_dimension=0, tiled=True)]
  transfers between devices with their start and end apart: 48 -> 52, of which waited for: 22 -> 24; matrix products, arithmetic and copies ran while one was open for 31% -> 30% of each run, Pallas kernels for 11% -> 12%
where the time goes in v4:
time: 603 us; the launch traced here: 594 us
  waiting for transfers between devices  174 us (29%)
  matrix products  134 us (22%)
  starting transfers between devices  108 us (18%)
  Pallas kernels  83.1 us (14%)
  other arithmetic  38.8 us (6%)
  local copies, waits for them, and re-layouts  27.9 us (5%)
  between operations  16.8 us (3%)
  blocking collectives  9.99 us (2%)
    dot_general x13, matrix products, dot(): return lax.dot_general(a, b, (dims, ((), ())), preferred_element_type=F32)  134 us
    ppermute x15, waiting for transfers between devices, step(): lax.ppermute(left, 'context', [(a, a - 1) for a in range(n - t, 0, -1)])  132 us
    ppermute x15, starting transfers between devices, step(): lax.ppermute(right, 'context', [(a, a + 1) for a in range(t - 1, n - 1)])  41.9 us
    ppermute x6, starting transfers between devices, step(): self.right = lax.ppermute(right, 'context', [(a, a + 1) for a in range(t)])  34 us
    ppermute x15, waiting for transfers between devices, step(): lax.ppermute(right, 'context', [(a, a + 1) for a in range(t - 1, n - 1)])  28.1 us
    pallas_call x1, Pallas kernels, attend_back(): pl.pallas_call(attend_back_kernel, grid_spec=pltpu.PrefetchScalarGridSpec...  23.1 us
    unnamed x150, local copies, waits for them, and re-layouts  21.7 us
    ppermute x15, starting transfers between devices, step(): lax.ppermute(left, 'context', [(a, a - 1) for a in range(n - t, 0, -1)])  20.6 us
  transfers between devices with their start and end apart: 52, of which 24 were waited for; matrix products, arithmetic and copies ran while one was open for 30% of the time, Pallas kernels for 12%

profile of v4, /device:TPU:0, one launch (start us, length us, event | category | flops | bytes accessed | tf_op | source)
XLA Modules:
  0.0 593.5 jit_solution(13566620747869979723)
XLA Ops:
  30.6 10.0 %all-gather.1 = bf16[8,1,2816]{2,1,0:T(2,128)(2,1)S(1)} all-gather(bf16[1,1,2816]{2,1,0:T(2,128)(2,1)S(1)} %reshape.213), channel_id=2, replica_groups=mesh['shard'=8,'context'=4] {'shard'}, dimensions={0}, use_global_device_ids=true | all-gather | bytes 50688 | tf_op jit(solution)/shard_map/all_gather | solution.py:529
  56.8 20.1 %collective-permute-done.2.refs_1_.refs_2_ = bf16[256,2048]{1,0:T(8,128)(2,1)S(1)} collective-permute-done((bf16[256,2048]{1,0:T(8,128)(2,1)S(1)}, bf16[256,2048]{1,0:T(8,128)(2,1)S(1)}, u32[]{:S(2)}, u32[]{:S(2)}) %collective-permute-start.2) | collective-permute-done | bytes 1048608 | tf_op jit(solution)/shard_map/ppermute | solution.py:411
  89.0 20.5 %collective-permute-done.6.refs_4_.refs_5_ = bf16[256,2048]{1,0:T(8,128)(2,1)} collective-permute-done((bf16[256,2048]{1,0:T(8,128)(2,1)S(1)}, bf16[256,2048]{1,0:T(8,128)(2,1)}, u32[]{:S(2)}, u32[]{:S(2)}) %collective-permute-start.6) | collective-permute-done | bytes 1048608 | tf_op jit(solution)/shard_map/ppermute | solution.py:413
  114.6 8.9 %fusion.30.q_main.k_main.v_main = f32[768,1536]{1,0:T(8,128)S(1)} fusion(bf16[768,2048]{1,0:T(8,128)(2,1)} %copy-done.12, bf16[2048,3584]{1,0:T(8,128)(2,1)} %all-gather.5.cloned.1.call-done, f32[1536]{0:T(1024)S(1)} %concatenate.26), kind=kOutput, calls=%fused_computation.38 | convolution fusion | flops 4833017856 | bytes 14161920 | tf_op jit(solution)/shard_map/dot_general | solution.py:27
  123.5 12.1 %fusion.23 = (bf16[768,2048]{1,0:T(8,128)(2,1)S(1)}, f32[768,2048]{1,0:T(8,128)}) fusion(f32[2048]{0:T(1024)S(1)} %concatenate.27, bf16[768,2048]{1,0:T(8,128)(2,1)S(1)} %copy-done.13, bf16[2048,3584]{1,0:T(8,128)(2,1)} %all-gather.5.cloned.1.call-done), kind=kOutput, calls=%fused_computation.30 | convolution fusion | flops 6458179584 | bytes 20979712 | tf_op jit(solution)/shard_map/dot_general | solution.py:27
  147.3 17.3 %shard_map.164 = (bf16[1024,512]{1,0:T(8,128)(2,1)S(1)}, f32[1024,512]{1,0:T(8,128)S(1)}, bf16[1024,512]{1,0:T(8,128)(2,1)S(1)}, bf16[1024,512]{1,0:T(8,128)(2,1)S(1)}, bf16[1024,512]{1,0:T(8,128)(2,1)S(1)}) custom-call(s32[8]{0:T(128)S(1)} %select_reduce_fusion.place_ref, f32[768,1536]{1,0:T(8,128)S(1)} %fusion.30.q_main.k_main.v_main, ...), custom_call_target="tpu_custom_call" | custom-call | flops 4294967296 | bytes 15728640 | tf_op jit(solution)/shard_map/pallas_call | solution.py:306
  169.9 7.5 %multiply_convert_fusion = (bf16[256,2048]{1,0:T(8,128)(2,1)S(1)}, f32[256,2048]{1,0:T(8,128)}) fusion(f32[2048]{0:T(1024)S(1)} %concatenate.27, bf16[256,2048]{1,0:T(8,128)(2,1)S(1)} %shard_map.163, bf16[2048,3584]{1,0:T(8,128)(2,1)} %all-gather.5.cloned.1.call-done), kind=kOutput, calls=%fused_computation.65 | convolution fusion | flops 2152726528 | bytes 12591104 | tf_op jit(solution)/shard_map/dot_general | solution.py:27
  180.8 15.2 %convolution_convert_fusion.3 = bf16[1024,2048]{1,0:T(8,128)(2,1)S(1)} fusion(bf16[1024,2560]{1,0:T(8,128)(2,1)} %copy-done.4, bf16[2560,2048]{1,0:T(8,128)(2,1)} %all-gather.7.cloned.1.call-done), kind=kOutput, calls=%fused_computation.37 | convolution fusion | flops 10739515392 | bytes 19922944 | tf_op jit(solution)/shard_map/dot_general | solution.py:27
  199.5 8.0 %collective-permute-start.12 = (bf16[256,2048]{1,0:T(8,128)(2,1)}, bf16[256,2048]{1,0:T(8,128)(2,1)}, u32[]{:S(2)}, u32[]{:S(2)}) collective-permute-start(bf16[256,2048]{1,0:T(8,128)(2,1)} %get-tuple-element.239), channel_id=1, source_target_pairs={{0,1},{4,5},{8,9},{12,13},{16,17},{20,21},{24,25},{28,29}} | collective-permute-start | bytes 3145736 | tf_op jit(solution)/shard_map/ppermute | solution.py:455
  211.9 13.4 %convolution_convert_fusion = bf16[2560,2048]{1,0:T(8,128)(2,1)} fusion(bf16[1024,2560]{1,0:T(8,128)(2,1)S(1)} %bitcast.171, bf16[1024,2048]{1,0:T(8,128)(2,1)S(1)} %shard_map.167), kind=kOutput, calls=%fused_computation | convolution fusion | flops 10742661120 | bytes 19922944 | tf_op jit(solution)/shard_map/dot_general | solution.py:27
  238.8 15.1 %fusion.69 = (f32[2048]{0:T(1024)S(1)}, bf16[768,2048]{1,0:T(8,128)(2,1)S(1)}) fusion(f32[768,2048]{1,0:T(8,128)} %get-tuple-element.125, bf16[2560,2048]{1,0:T(8,128)(2,1)} %all-gather.7.cloned.1.call-done, bf16[1024,2048]{1,0:T(8,128)(2,1)S(1)} %copy-done.9), kind=kOutput, calls=%fused_computation.174 | convolution fusion | flops 6475479040 | bytes 20979712 | tf_op jit(solution)/shard_map/dot_general | solution.py:27
  270.9 11.5 %convolution_convert_fusion.2 = bf16[2048,2048]{1,0:T(8,128)(2,1)} fusion(bf16[1024,2048]{1,0:T(8,128)(2,1)S(1)} %shard_map.169, bf16[1024,2048]{1,0:T(8,128)(2,1)S(1)} %shard_map.168), kind=kOutput, calls=%fused_computation.6 | convolution fusion | flops 8594128896 | bytes 16777216 | tf_op jit(solution)/shard_map/dot_general | solution.py:27
  296.7 13.5 %fusion.4 = f32[1024,2048]{1,0:T(8,128)} fusion(bf16[1024,2048]{1,0:T(8,128)(2,1)S(1)} %copy-done.11, bf16[2048,3584]{1,0:T(8,128)(2,1)} %all-gather.5.cloned.1.call-done), kind=kOutput, calls=%fused_computation.11 | convolution fusion | flops 8589934592 | bytes 20971520 | tf_op jit(solution)/shard_map/dot_general | solution.py:27
  317.0 23.1 %shard_map.170 = (bf16[1024,512]{1,0:T(8,128)(2,1)S(1)}, bf16[1024,512]{1,0:T(8,128)(2,1)S(1)}, bf16[1024,512]{1,0:T(8,128)(2,1)S(1)}, f32[8,512]{1,0:T(8,128)S(1)}) custom-call(s32[8]{0:T(128)S(1)} %select_reduce_fusion.place_ref, bf16[1024,512]{1,0:T(8,128)(2,1)S(1)} %copy-done.39, bf16[1024,512]{1,0:T(8,128)(2,1)} %copy-done.40, ...), custom_call_target="tpu_custom_call" | custom-call | flops 10737418240 | bytes 15728640 | tf_op jit(solution)/shard_map/pallas_call | solution.py:337
  348.3 8.8 %convolution_convert_fusion.1 = bf16[2048,1536]{1,0:T(8,128)(2,1)} fusion(bf16[1024,2048]{1,0:T(8,128)(2,1)S(1)} %copy-done.1, bf16[1024,1536]{1,0:T(8,128)(2,1)S(1)} %shard_map.171), kind=kOutput, calls=%fused_computation.5 | convolution fusion | flops 6445596672 | bytes 13631488 | tf_op jit(solution)/shard_map/dot_general | solution.py:27
  357.1 20.4 %collective-permute-done.21.refs_5_ = bf16[320,2048]{1,0:T(8,128)(2,1)} collective-permute-done((bf16[320,2048]{1,0:T(8,128)(2,1)}, bf16[320,2048]{1,0:T(8,128)(2,1)}, u32[]{:S(2)}, u32[]{:S(2)}) %collective-permute-start.21) | collective-permute-done | bytes 1310752 | tf_op jit(solution)/shard_map/ppermute | solution.py:413
  380.1 8.8 %fusion.24 = f32[1024,2048]{1,0:T(8,128)S(1)} fusion(bf16[1024,1536]{1,0:T(8,128)(2,1)S(1)} %shard_map.171, bf16[2048,3584]{1,0:T(8,128)(2,1)} %all-gather.5.cloned.1.call-done), kind=kOutput, calls=%fused_computation.31 | convolution fusion | flops 6442450944 | bytes 17825792 | tf_op jit(solution)/shard_map/dot_general | solution.py:27
  396.8 10.3 %collective-permute-done.23.refs_6_ = bf16[320,2048]{1,0:T(8,128)(2,1)S(1)} collective-permute-done((bf16[320,2048]{1,0:T(8,128)(2,1)}, bf16[320,2048]{1,0:T(8,128)(2,1)S(1)}, u32[]{:S(2)}, u32[]{:S(2)}) %collective-permute-start.23) | collective-permute-done | bytes 1310752 | tf_op jit(solution)/shard_map/ppermute | solution.py:413
  416.5 8.5 %shard_map.173 = f32[1280,2048]{1,0:T(8,128)} custom-call(bf16[4,320,2048]{2,1,0:T(8,128)(2,1)S(1)} %bitcast.167), custom_call_target="tpu_custom_call" | custom-call | bytes 15728640 | tf_op jit(solution)/shard_map/pallas_call | solution.py:630
  439.4 15.9 %collective-permute-done.27.refs_5_ = bf16[256,2048]{1,0:T(8,128)(2,1)S(1)} collective-permute-done((bf16[256,2048]{1,0:T(8,128)(2,1)S(1)}, bf16[256,2048]{1,0:T(8,128)(2,1)S(1)}, u32[]{:S(2)}, u32[]{:S(2)}) %collective-permute-start.27) | collective-permute-done | bytes 1048608 | tf_op jit(solution)/shard_map/ppermute | solution.py:413
  466.6 9.8 %collective-permute-done.31.refs_6_ = bf16[256,2048]{1,0:T(8,128)(2,1)S(1)} collective-permute-done((bf16[256,2048]{1,0:T(8,128)(2,1)S(1)}, bf16[256,2048]{1,0:T(8,128)(2,1)S(1)}, u32[]{:S(2)}, u32[]{:S(2)}) %collective-permute-start.31) | collective-permute-done | bytes 1048608 | tf_op jit(solution)/shard_map/ppermute | solution.py:413
  477.7 10.8 %collective-permute-start.36 = (bf16[256,1536]{1,0:T(8,128)(2,1)}, bf16[256,1536]{1,0:T(8,128)(2,1)}, u32[]{:S(2)}, u32[]{:S(2)}) collective-permute-start(bf16[256,1536]{1,0:T(8,128)(2,1)} %reduce-scatter.8.cloned.1.call-done.refs_3_), channel_id=1, source_target_pairs={{0,1},{1,2},{2,3},{4,5},{5,6},{6,7},{8,9},{9,10},{10,11},{12,13},{... | collective-permute-start | bytes 2359304 | tf_op jit(solution)/shard_map/ppermute | solution.py:411
  522.1 18.1 %collective-permute-done.39.refs_5_ = bf16[256,1536]{1,0:T(8,128)(2,1)} collective-permute-done((bf16[256,1536]{1,0:T(8,128)(2,1)}, bf16[256,1536]{1,0:T(8,128)(2,1)}, u32[]{:S(2)}, u32[]{:S(2)}) %collective-permute-start.39) | collective-permute-done | bytes 786464 | tf_op jit(solution)/shard_map/ppermute | solution.py:413
  566.2 13.8 %collective-permute-done.41.refs_6_ = bf16[256,1536]{1,0:T(8,128)(2,1)S(1)} collective-permute-done((bf16[256,1536]{1,0:T(8,128)(2,1)}, bf16[256,1536]{1,0:T(8,128)(2,1)S(1)}, u32[]{:S(2)}, u32[]{:S(2)}) %collective-permute-start.41) | collective-permute-done | bytes 786464 | tf_op jit(solution)/shard_map/ppermute | solution.py:413
  (326 shorter events, 255.2 us)
Async XLA Ops:
  7.2 107.4 %all-gather.5.cloned.1.call-start = ((), (), s32[]{:S(2)}) async-start(), calls=%async_computation.3 | async-start | bytes 16515072 | tf_op jit(solution)/shard_map/all_gather | solution.py:529
  13.8 167.0 %all-gather.7.cloned.1.call-start = ((), (), s32[]{:S(2)}) async-start(), calls=%async_computation.4 | async-start | bytes 11796480 | tf_op jit(solution)/shard_map/all_gather | solution.py:529
  18.6 291.7 %reduce-scatter.4.cloned.1.call-start = ((), (), s32[]{:S(2)}) async-start(), calls=%async_computation.5 | async-start | bytes 11796480 | tf_op jit(solution)/shard_map/reduce_scatter | solution.py:559
  21.7 28.0 %collective-permute-start.1 = (bf16[256,2048]{1,0:T(8,128)(2,1)S(1)}, bf16[256,2048]{1,0:T(8,128)(2,1)S(1)}, u32[]{:S(2)}, u32[]{:S(2)}) collective-permute-start(bf16[256,2048]{1,0:T(8,128)(2,1)S(1)} %get-tuple-element.241.refs_3_), channel_id=1, source_target_pairs={{3,2},{2,1},{1,0},{7,6},{6,5},{5,4},{11,10},{10,9},{9,8},{15,14},{... | collective-permute-start | bytes 3145736 | tf_op jit(solution)/shard_map/ppermute | solution.py:413
  23.0 27.9 %collective-permute-start = (bf16[256,2048]{1,0:T(8,128)(2,1)S(1)}, bf16[256,2048]{1,0:T(8,128)(2,1)}, u32[]{:S(2)}, u32[]{:S(2)}) collective-permute-start(bf16[256,2048]{1,0:T(8,128)(2,1)S(1)} %get-tuple-element.241.refs_3_), channel_id=1, source_target_pairs={{0,1},{1,2},{2,3},{4,5},{5,6},{6,7},{8,9},{9,10},{10,11},{12,13},{... | collective-permute-start | bytes 3145736 | tf_op jit(solution)/shard_map/ppermute | solution.py:411
  82.8 26.8 %collective-permute-start.6 = (bf16[256,2048]{1,0:T(8,128)(2,1)S(1)}, bf16[256,2048]{1,0:T(8,128)(2,1)}, u32[]{:S(2)}, u32[]{:S(2)}) collective-permute-start(bf16[256,2048]{1,0:T(8,128)(2,1)S(1)} %collective-permute-done.3.refs_3_.refs_4_), channel_id=1, source_target_pairs={{2,1},{1,0},{6,5},{5,4},{10,9},{9,8},{14,13},{13,12},{18,17},{17,1... | collective-permute-start | bytes 3145736 | tf_op jit(solution)/shard_map/ppermute | solution.py:413
  87.4 48.3 %collective-permute-start.5 = (bf16[256,2048]{1,0:T(8,128)(2,1)}, bf16[256,2048]{1,0:T(8,128)(2,1)}, u32[]{:S(2)}, u32[]{:S(2)}) collective-permute-start(bf16[256,2048]{1,0:T(8,128)(2,1)} %collective-permute-done.4.refs_0_.refs_1_), channel_id=1, source_target_pairs={{2,3},{6,7},{10,11},{14,15},{18,19},{22,23},{26,27},{30,31}} | collective-permute-start | bytes 3145736 | tf_op jit(solution)/shard_map/ppermute | solution.py:411
  135.7 30.3 %collective-permute-start.8 = (bf16[256,2048]{1,0:T(8,128)(2,1)}, bf16[256,2048]{1,0:T(8,128)(2,1)}, u32[]{:S(2)}, u32[]{:S(2)}) collective-permute-start(bf16[256,2048]{1,0:T(8,128)(2,1)} %collective-permute-done.refs_2_), channel_id=1, source_target_pairs={{1,2},{2,3},{5,6},{6,7},{9,10},{10,11},{13,14},{14,15},{17,18},{18... | collective-permute-start | bytes 3145736 | tf_op jit(solution)/shard_map/ppermute | solution.py:411
  137.3 28.7 %collective-permute-start.9 = (bf16[256,2048]{1,0:T(8,128)(2,1)S(1)}, bf16[256,2048]{1,0:T(8,128)(2,1)}, u32[]{:S(2)}, u32[]{:S(2)}) collective-permute-start(bf16[256,2048]{1,0:T(8,128)(2,1)S(1)} %copy-done.26), channel_id=1, source_target_pairs={{2,1},{1,0},{6,5},{5,4},{10,9},{9,8},{14,13},{13,12},{18,17},{17,1... | collective-permute-start | bytes 3145736 | tf_op jit(solution)/shard_map/ppermute | solution.py:413
  166.0 30.1 %collective-permute-start.10 = (bf16[256,2048]{1,0:T(8,128)(2,1)}, bf16[256,2048]{1,0:T(8,128)(2,1)}, u32[]{:S(2)}, u32[]{:S(2)}) collective-permute-start(bf16[256,2048]{1,0:T(8,128)(2,1)} %collective-permute-done.8.refs_1_), channel_id=1, source_target_pairs={{2,3},{6,7},{10,11},{14,15},{18,19},{22,23},{26,27},{30,31}} | collective-permute-start | bytes 3145736 | tf_op jit(solution)/shard_map/ppermute | solution.py:411
  168.2 27.9 %collective-permute-start.11 = (bf16[256,2048]{1,0:T(8,128)(2,1)}, bf16[256,2048]{1,0:T(8,128)(2,1)}, u32[]{:S(2)}, u32[]{:S(2)}) collective-permute-start(bf16[256,2048]{1,0:T(8,128)(2,1)} %collective-permute-done.9.refs_5_), channel_id=1, source_target_pairs={{1,0},{5,4},{9,8},{13,12},{17,16},{21,20},{25,24},{29,28}} | collective-permute-start | bytes 3145736 | tf_op jit(solution)/shard_map/ppermute | solution.py:413
  197.7 27.6 %collective-permute-start.13 = (bf16[256,2048]{1,0:T(8,128)(2,1)}, bf16[256,2048]{1,0:T(8,128)(2,1)}, u32[]{:S(2)}, u32[]{:S(2)}) collective-permute-start(bf16[256,2048]{1,0:T(8,128)(2,1)} %get-tuple-element.238), channel_id=1, source_target_pairs={{3,2},{7,6},{11,10},{15,14},{19,18},{23,22},{27,26},{31,30}} | collective-permute-start | bytes 3145736 | tf_op jit(solution)/shard_map/ppermute | solution.py:456
  226.0 182.2 %reduce-scatter.6.cloned.1.call-start = ((), (), s32[]{:S(2)}) async-start(), calls=%async_computation.6 | async-start | bytes 9437184 | tf_op jit(solution)/shard_map/reduce_scatter | solution.py:559
  232.8 29.2 %collective-permute-start.15 = (bf16[256,2048]{1,0:T(8,128)(2,1)S(1)}, bf16[256,2048]{1,0:T(8,128)(2,1)S(1)}, u32[]{:S(2)}, u32[]{:S(2)}) collective-permute-start(bf16[256,2048]{1,0:T(8,128)(2,1)S(1)} %get-tuple-element.236), channel_id=1, source_target_pairs={{3,2},{2,1},{7,6},{6,5},{11,10},{10,9},{15,14},{14,13},{19,18},{18... | collective-permute-start | bytes 3145736 | tf_op jit(solution)/shard_map/ppermute | solution.py:456
  233.7 28.4 %collective-permute-start.14 = (bf16[256,2048]{1,0:T(8,128)(2,1)S(1)}, bf16[256,2048]{1,0:T(8,128)(2,1)S(1)}, u32[]{:S(2)}, u32[]{:S(2)}) collective-permute-start(bf16[256,2048]{1,0:T(8,128)(2,1)S(1)} %get-tuple-element.237), channel_id=1, source_target_pairs={{0,1},{1,2},{4,5},{5,6},{8,9},{9,10},{12,13},{13,14},{16,17},{17,1... | collective-permute-start | bytes 3145736 | tf_op jit(solution)/shard_map/ppermute | solution.py:455
  289.5 188.2 %reduce-scatter.8.cloned.1.call-start = ((), (), s32[]{:S(2)}) async-start(), calls=%async_computation.7 | async-start | bytes 7077888 | tf_op jit(solution)/shard_map/reduce_scatter | solution.py:559
  310.2 30.4 %collective-permute-start.18 = (bf16[320,2048]{1,0:T(8,128)(2,1)}, bf16[320,2048]{1,0:T(8,128)(2,1)}, u32[]{:S(2)}, u32[]{:S(2)}) collective-permute-start(bf16[320,2048]{1,0:T(8,128)(2,1)} %reduce-scatter.4.cloned.1.call-done.refs_3_), channel_id=1, source_target_pairs={{0,1},{1,2},{2,3},{4,5},{5,6},{6,7},{8,9},{9,10},{10,11},{12,13},{... | collective-permute-start | bytes 3932168 | tf_op jit(solution)/shard_map/ppermute | solution.py:411
  315.3 30.0 %collective-permute-start.19 = (bf16[320,2048]{1,0:T(8,128)(2,1)}, bf16[320,2048]{1,0:T(8,128)(2,1)}, u32[]{:S(2)}, u32[]{:S(2)}) collective-permute-start(bf16[320,2048]{1,0:T(8,128)(2,1)} %reduce-scatter.4.cloned.1.call-done.refs_3_), channel_id=1, source_target_pairs={{3,2},{2,1},{1,0},{7,6},{6,5},{5,4},{11,10},{10,9},{9,8},{15,14},{... | collective-permute-start | bytes 3932168 | tf_op jit(solution)/shard_map/ppermute | solution.py:413
  347.0 30.6 %collective-permute-start.21 = (bf16[320,2048]{1,0:T(8,128)(2,1)}, bf16[320,2048]{1,0:T(8,128)(2,1)}, u32[]{:S(2)}, u32[]{:S(2)}) collective-permute-start(bf16[320,2048]{1,0:T(8,128)(2,1)} %collective-permute-done.19.refs_4_), channel_id=1, source_target_pairs={{2,1},{1,0},{6,5},{5,4},{10,9},{9,8},{14,13},{13,12},{18,17},{17,1... | collective-permute-start | bytes 3932168 | tf_op jit(solution)/shard_map/ppermute | solution.py:413
  378.5 28.6 %collective-permute-start.23 = (bf16[320,2048]{1,0:T(8,128)(2,1)}, bf16[320,2048]{1,0:T(8,128)(2,1)S(1)}, u32[]{:S(2)}, u32[]{:S(2)}) collective-permute-start(bf16[320,2048]{1,0:T(8,128)(2,1)} %collective-permute-done.21.refs_5_), channel_id=1, source_target_pairs={{1,0},{5,4},{9,8},{13,12},{17,16},{21,20},{25,24},{29,28}} | collective-permute-start | bytes 3932168 | tf_op jit(solution)/shard_map/ppermute | solution.py:413
  477.7 28.2 %collective-permute-start.36 = (bf16[256,1536]{1,0:T(8,128)(2,1)}, bf16[256,1536]{1,0:T(8,128)(2,1)}, u32[]{:S(2)}, u32[]{:S(2)}) collective-permute-start(bf16[256,1536]{1,0:T(8,128)(2,1)} %reduce-scatter.8.cloned.1.call-done.refs_3_), channel_id=1, source_target_pairs={{0,1},{1,2},{2,3},{4,5},{5,6},{6,7},{8,9},{9,10},{10,11},{12,13},{... | collective-permute-start | bytes 2359304 | tf_op jit(solution)/shard_map/ppermute | solution.py:411
  494.5 48.1 %collective-permute-start.34 = (bf16[256,2048]{1,0:T(8,128)(2,1)}, bf16[256,2048]{1,0:T(8,128)(2,1)}, u32[]{:S(2)}, u32[]{:S(2)}) collective-permute-start(bf16[256,2048]{1,0:T(8,128)(2,1)} %get-tuple-element.198), channel_id=1, source_target_pairs={{0,1},{1,2},{2,3},{4,5},{5,6},{6,7},{8,9},{9,10},{10,11},{12,13},{... | collective-permute-start | bytes 3145736 | tf_op jit(solution)/shard_map/ppermute | solution.py:455
  500.0 42.5 %collective-permute-start.35 = (bf16[256,2048]{1,0:T(8,128)(2,1)}, bf16[256,2048]{1,0:T(8,128)(2,1)}, u32[]{:S(2)}, u32[]{:S(2)}) collective-permute-start(bf16[256,2048]{1,0:T(8,128)(2,1)} %get-tuple-element.199), channel_id=1, source_target_pairs={{3,2},{2,1},{1,0},{7,6},{6,5},{5,4},{11,10},{10,9},{9,8},{15,14},{... | collective-permute-start | bytes 3145736 | tf_op jit(solution)/shard_map/ppermute | solution.py:456
  512.8 27.4 %collective-permute-start.39 = (bf16[256,1536]{1,0:T(8,128)(2,1)}, bf16[256,1536]{1,0:T(8,128)(2,1)}, u32[]{:S(2)}, u32[]{:S(2)}) collective-permute-start(bf16[256,1536]{1,0:T(8,128)(2,1)} %collective-permute-done.37.refs_4_), channel_id=1, source_target_pairs={{2,1},{1,0},{6,5},{5,4},{10,9},{9,8},{14,13},{13,12},{18,17},{17,1... | collective-permute-start | bytes 2359304 | tf_op jit(solution)/shard_map/ppermute | solution.py:413
  (96 other events, 1305.1 us)
Sparse Core Ops, SparseCore 0:
  13.9 83.9 all-gather.4
  99.8 63.2 all-gather.6
  226.1 82.2 reduce-scatter.3
  311.7 71.2 reduce-scatter.5
  386.5 61.7 reduce-scatter.7

commit v5 on v4

--- a/solution.py
+++ b/solution.py
@@ -692,8 +692,8 @@
     )
     weight_in = gather_shard(in_part)
     weight_qkv, weight_hidden = weight_in[:, : 3 * attn], weight_in[:, 3 * attn :]
+    gate, (normed_here, output_weight) = close([up], normed_here, output_weight)
     out_part = take_rows(output_weight, inner, context) if inner is not None else output_weight
-    gate, (normed_here,) = close([up], normed_here)
     weight_out = gather_shard(out_part)
     if inner is None:
         weight_out = take(weight_out, segments, context, 0)

time: 603 us -> 602 us (level)
    unnamed x150 -> x148, local copies, waits for them, and re-layouts: 21.7 us -> 19.1 us
  transfers between devices with their start and end apart: 52 -> 52, of which waited for: 24 -> 25; matrix products, arithmetic and copies ran while one was open for 30% -> 30% of each run, Pallas kernels for 12% -> 12%
where the time goes in v5:
time: 602 us; the launch traced here: 593 us
  waiting for transfers between devices  177 us (29%)
  matrix products  134 us (22%)
  starting transfers between devices  106 us (18%)
  Pallas kernels  83.3 us (14%)
  other arithmetic  40.8 us (7%)
  local copies, waits for them, and re-layouts  25.4 us (4%)
  between operations  16.7 us (3%)
  blocking collectives  9.98 us (2%)
    dot_general x13, matrix products, dot(): return lax.dot_general(a, b, (dims, ((), ())), preferred_element_type=F32)  134 us
    ppermute x15, waiting for transfers between devices, step(): lax.ppermute(left, 'context', [(a, a - 1) for a in range(n - t, 0, -1)])  131 us
    ppermute x15, starting transfers between devices, step(): lax.ppermute(right, 'context', [(a, a + 1) for a in range(t - 1, n - 1)])  42.5 us
    ppermute x6, starting transfers between devices, step(): self.right = lax.ppermute(right, 'context', [(a, a + 1) for a in range(t)])  34.3 us
    ppermute x15, waiting for transfers between devices, step(): lax.ppermute(right, 'context', [(a, a + 1) for a in range(t - 1, n - 1)])  28.6 us
    pallas_call x1, Pallas kernels, attend_back(): pl.pallas_call(attend_back_kernel, grid_spec=pltpu.PrefetchScalarGridSpec...  23.1 us
    ppermute x15, starting transfers between devices, step(): lax.ppermute(left, 'context', [(a, a - 1) for a in range(n - t, 0, -1)])  20.6 us
    unnamed x148, local copies, waits for them, and re-layouts  19.1 us
  transfers between devices with their start and end apart: 52, of which 25 were waited for; matrix products, arithmetic and copies ran while one was open for 30% of the time, Pallas kernels for 12%

profile of v5, /device:TPU:0, one launch (start us, length us, event | category | flops | bytes accessed | tf_op | source)
XLA Modules:
  0.0 593.0 jit_solution(12723530262960585150)
XLA Ops:
  25.8 10.0 %all-gather.1 = bf16[8,1,2816]{2,1,0:T(2,128)(2,1)S(1)} all-gather(bf16[1,1,2816]{2,1,0:T(2,128)(2,1)S(1)} %reshape.213), channel_id=2, replica_groups=mesh['shard'=8,'context'=4] {'shard'}, dimensions={0}, use_global_device_ids=true | all-gather | bytes 50688 | tf_op jit(solution)/shard_map/all_gather | solution.py:529
  54.4 20.1 %collective-permute-done.2.refs_1_.refs_2_ = bf16[256,2048]{1,0:T(8,128)(2,1)S(1)} collective-permute-done((bf16[256,2048]{1,0:T(8,128)(2,1)S(1)}, bf16[256,2048]{1,0:T(8,128)(2,1)S(1)}, u32[]{:S(2)}, u32[]{:S(2)}) %collective-permute-start.2) | collective-permute-done | bytes 1048608 | tf_op jit(solution)/shard_map/ppermute | solution.py:411
  86.7 20.5 %collective-permute-done.6.refs_4_.refs_5_ = bf16[256,2048]{1,0:T(8,128)(2,1)} collective-permute-done((bf16[256,2048]{1,0:T(8,128)(2,1)S(1)}, bf16[256,2048]{1,0:T(8,128)(2,1)}, u32[]{:S(2)}, u32[]{:S(2)}) %collective-permute-start.6) | collective-permute-done | bytes 1048608 | tf_op jit(solution)/shard_map/ppermute | solution.py:413
  112.4 8.8 %fusion.30.q_main.k_main.v_main = f32[768,1536]{1,0:T(8,128)S(1)} fusion(bf16[768,2048]{1,0:T(8,128)(2,1)} %copy-done.12, bf16[2048,3584]{1,0:T(8,128)(2,1)} %all-gather.5.cloned.1.call-done, f32[1536]{0:T(1024)S(1)} %concatenate.26), kind=kOutput, calls=%fused_computation.38 | convolution fusion | flops 4833017856 | bytes 14161920 | tf_op jit(solution)/shard_map/dot_general | solution.py:27
  121.2 12.1 %fusion.23 = (bf16[768,2048]{1,0:T(8,128)(2,1)S(1)}, f32[768,2048]{1,0:T(8,128)}) fusion(f32[2048]{0:T(1024)S(1)} %concatenate.27, bf16[768,2048]{1,0:T(8,128)(2,1)S(1)} %copy-done.13, bf16[2048,3584]{1,0:T(8,128)(2,1)} %all-gather.5.cloned.1.call-done), kind=kOutput, calls=%fused_computation.30 | convolution fusion | flops 6458179584 | bytes 20979712 | tf_op jit(solution)/shard_map/dot_general | solution.py:27
  145.1 17.3 %shard_map.164 = (bf16[1024,512]{1,0:T(8,128)(2,1)S(1)}, f32[1024,512]{1,0:T(8,128)S(1)}, bf16[1024,512]{1,0:T(8,128)(2,1)S(1)}, bf16[1024,512]{1,0:T(8,128)(2,1)S(1)}, bf16[1024,512]{1,0:T(8,128)(2,1)S(1)}) custom-call(s32[8]{0:T(128)S(1)} %select_reduce_fusion.place_ref, f32[768,1536]{1,0:T(8,128)S(1)} %fusion.30.q_main.k_main.v_main, ...), custom_call_target="tpu_custom_call" | custom-call | flops 4294967296 | bytes 15728640 | tf_op jit(solution)/shard_map/pallas_call | solution.py:306
  167.6 7.5 %multiply_convert_fusion = (bf16[256,2048]{1,0:T(8,128)(2,1)S(1)}, f32[256,2048]{1,0:T(8,128)}) fusion(f32[2048]{0:T(1024)S(1)} %concatenate.27, bf16[256,2048]{1,0:T(8,128)(2,1)S(1)} %shard_map.163, bf16[2048,3584]{1,0:T(8,128)(2,1)} %all-gather.5.cloned.1.call-done), kind=kOutput, calls=%fused_computation.65 | convolution fusion | flops 2152726528 | bytes 12591104 | tf_op jit(solution)/shard_map/dot_general | solution.py:27
  178.5 15.2 %convolution_convert_fusion.3 = bf16[1024,2048]{1,0:T(8,128)(2,1)S(1)} fusion(bf16[1024,2560]{1,0:T(8,128)(2,1)} %copy-done.4, bf16[2560,2048]{1,0:T(8,128)(2,1)} %all-gather.7.cloned.1.call-done), kind=kOutput, calls=%fused_computation.37 | convolution fusion | flops 10739515392 | bytes 19922944 | tf_op jit(solution)/shard_map/dot_general | solution.py:27
  197.2 7.9 %collective-permute-start.12 = (bf16[256,2048]{1,0:T(8,128)(2,1)}, bf16[256,2048]{1,0:T(8,128)(2,1)}, u32[]{:S(2)}, u32[]{:S(2)}) collective-permute-start(bf16[256,2048]{1,0:T(8,128)(2,1)} %get-tuple-element.241), channel_id=1, source_target_pairs={{0,1},{4,5},{8,9},{12,13},{16,17},{20,21},{24,25},{28,29}} | collective-permute-start | bytes 3145736 | tf_op jit(solution)/shard_map/ppermute | solution.py:455
  209.5 13.4 %convolution_convert_fusion = bf16[2560,2048]{1,0:T(8,128)(2,1)} fusion(bf16[1024,2560]{1,0:T(8,128)(2,1)S(1)} %bitcast.171, bf16[1024,2048]{1,0:T(8,128)(2,1)S(1)} %shard_map.167), kind=kOutput, calls=%fused_computation | convolution fusion | flops 10742661120 | bytes 19922944 | tf_op jit(solution)/shard_map/dot_general | solution.py:27
  236.2 15.1 %fusion.69 = (f32[2048]{0:T(1024)S(1)}, bf16[768,2048]{1,0:T(8,128)(2,1)S(1)}) fusion(f32[768,2048]{1,0:T(8,128)} %get-tuple-element.127, bf16[2560,2048]{1,0:T(8,128)(2,1)} %all-gather.7.cloned.1.call-done, bf16[1024,2048]{1,0:T(8,128)(2,1)S(1)} %copy-done.9), kind=kOutput, calls=%fused_computation.174 | convolution fusion | flops 6475479040 | bytes 20979712 | tf_op jit(solution)/shard_map/dot_general | solution.py:27
  268.3 11.5 %convolution_convert_fusion.2 = bf16[2048,2048]{1,0:T(8,128)(2,1)} fusion(bf16[1024,2048]{1,0:T(8,128)(2,1)S(1)} %shard_map.169, bf16[1024,2048]{1,0:T(8,128)(2,1)S(1)} %shard_map.168), kind=kOutput, calls=%fused_computation.6 | convolution fusion | flops 8594128896 | bytes 16777216 | tf_op jit(solution)/shard_map/dot_general | solution.py:27
  293.8 13.5 %fusion.4 = f32[1024,2048]{1,0:T(8,128)} fusion(bf16[1024,2048]{1,0:T(8,128)(2,1)S(1)} %copy-done.11, bf16[2048,3584]{1,0:T(8,128)(2,1)} %all-gather.5.cloned.1.call-done), kind=kOutput, calls=%fused_computation.11 | convolution fusion | flops 8589934592 | bytes 20971520 | tf_op jit(solution)/shard_map/dot_general | solution.py:27
  314.3 23.1 %shard_map.170 = (bf16[1024,512]{1,0:T(8,128)(2,1)S(1)}, bf16[1024,512]{1,0:T(8,128)(2,1)S(1)}, bf16[1024,512]{1,0:T(8,128)(2,1)S(1)}, f32[8,512]{1,0:T(8,128)S(1)}) custom-call(s32[8]{0:T(128)S(1)} %select_reduce_fusion.place_ref, bf16[1024,512]{1,0:T(8,128)(2,1)S(1)} %copy-done.39, bf16[1024,512]{1,0:T(8,128)(2,1)} %copy-done.40, ...), custom_call_target="tpu_custom_call" | custom-call | flops 10737418240 | bytes 15728640 | tf_op jit(solution)/shard_map/pallas_call | solution.py:337
  345.7 8.7 %convolution_convert_fusion.1 = bf16[2048,1536]{1,0:T(8,128)(2,1)} fusion(bf16[1024,2048]{1,0:T(8,128)(2,1)S(1)} %copy-done.1, bf16[1024,1536]{1,0:T(8,128)(2,1)S(1)} %shard_map.171), kind=kOutput, calls=%fused_computation.5 | convolution fusion | flops 6445596672 | bytes 13631488 | tf_op jit(solution)/shard_map/dot_general | solution.py:27
  354.5 21.0 %collective-permute-done.21.refs_5_ = bf16[320,2048]{1,0:T(8,128)(2,1)} collective-permute-done((bf16[320,2048]{1,0:T(8,128)(2,1)}, bf16[320,2048]{1,0:T(8,128)(2,1)}, u32[]{:S(2)}, u32[]{:S(2)}) %collective-permute-start.21) | collective-permute-done | bytes 1310752 | tf_op jit(solution)/shard_map/ppermute | solution.py:413
  378.0 8.8 %fusion.24 = f32[1024,2048]{1,0:T(8,128)S(1)} fusion(bf16[1024,1536]{1,0:T(8,128)(2,1)S(1)} %shard_map.171, bf16[2048,3584]{1,0:T(8,128)(2,1)} %all-gather.5.cloned.1.call-done), kind=kOutput, calls=%fused_computation.31 | convolution fusion | flops 6442450944 | bytes 17825792 | tf_op jit(solution)/shard_map/dot_general | solution.py:27
  394.8 10.7 %collective-permute-done.23.refs_6_ = bf16[320,2048]{1,0:T(8,128)(2,1)S(1)} collective-permute-done((bf16[320,2048]{1,0:T(8,128)(2,1)}, bf16[320,2048]{1,0:T(8,128)(2,1)S(1)}, u32[]{:S(2)}, u32[]{:S(2)}) %collective-permute-start.23) | collective-permute-done | bytes 1310752 | tf_op jit(solution)/shard_map/ppermute | solution.py:413
  414.8 8.5 %shard_map.173 = f32[1280,2048]{1,0:T(8,128)} custom-call(bf16[4,320,2048]{2,1,0:T(8,128)(2,1)S(1)} %bitcast.167), custom_call_target="tpu_custom_call" | custom-call | bytes 15728640 | tf_op jit(solution)/shard_map/pallas_call | solution.py:630
  438.1 15.3 %collective-permute-done.27.refs_5_ = bf16[256,2048]{1,0:T(8,128)(2,1)S(1)} collective-permute-done((bf16[256,2048]{1,0:T(8,128)(2,1)S(1)}, bf16[256,2048]{1,0:T(8,128)(2,1)S(1)}, u32[]{:S(2)}, u32[]{:S(2)}) %collective-permute-start.27) | collective-permute-done | bytes 1048608 | tf_op jit(solution)/shard_map/ppermute | solution.py:413
  465.0 10.2 %collective-permute-done.31.refs_6_ = bf16[256,2048]{1,0:T(8,128)(2,1)S(1)} collective-permute-done((bf16[256,2048]{1,0:T(8,128)(2,1)S(1)}, bf16[256,2048]{1,0:T(8,128)(2,1)S(1)}, u32[]{:S(2)}, u32[]{:S(2)}) %collective-permute-start.31) | collective-permute-done | bytes 1048608 | tf_op jit(solution)/shard_map/ppermute | solution.py:413
  476.6 11.2 %collective-permute-start.36 = (bf16[256,1536]{1,0:T(8,128)(2,1)}, bf16[256,1536]{1,0:T(8,128)(2,1)}, u32[]{:S(2)}, u32[]{:S(2)}) collective-permute-start(bf16[256,1536]{1,0:T(8,128)(2,1)} %reduce-scatter.8.cloned.1.call-done.refs_3_), channel_id=1, source_target_pairs={{0,1},{1,2},{2,3},{4,5},{5,6},{6,7},{8,9},{9,10},{10,11},{12,13},{... | collective-permute-start | bytes 2359304 | tf_op jit(solution)/shard_map/ppermute | solution.py:411
  521.3 18.9 %collective-permute-done.39.refs_5_ = bf16[256,1536]{1,0:T(8,128)(2,1)} collective-permute-done((bf16[256,1536]{1,0:T(8,128)(2,1)}, bf16[256,1536]{1,0:T(8,128)(2,1)}, u32[]{:S(2)}, u32[]{:S(2)}) %collective-permute-start.39) | collective-permute-done | bytes 786464 | tf_op jit(solution)/shard_map/ppermute | solution.py:413
  565.7 13.8 %collective-permute-done.41.refs_6_ = bf16[256,1536]{1,0:T(8,128)(2,1)S(1)} collective-permute-done((bf16[256,1536]{1,0:T(8,128)(2,1)}, bf16[256,1536]{1,0:T(8,128)(2,1)S(1)}, u32[]{:S(2)}, u32[]{:S(2)}) %collective-permute-start.41) | collective-permute-done | bytes 786464 | tf_op jit(solution)/shard_map/ppermute | solution.py:413
  (324 shorter events, 253.0 us)
Async XLA Ops:
  7.2 105.2 %all-gather.5.cloned.1.call-start = ((), (), s32[]{:S(2)}) async-start(), calls=%async_computation.3 | async-start | bytes 16515072 | tf_op jit(solution)/shard_map/all_gather | solution.py:529
  13.8 164.7 %all-gather.7.cloned.1.call-start = ((), (), s32[]{:S(2)}) async-start(), calls=%async_computation.4 | async-start | bytes 11796480 | tf_op jit(solution)/shard_map/all_gather | solution.py:529
  17.0 28.0 %collective-permute-start.1 = (bf16[256,2048]{1,0:T(8,128)(2,1)S(1)}, bf16[256,2048]{1,0:T(8,128)(2,1)S(1)}, u32[]{:S(2)}, u32[]{:S(2)}) collective-permute-start(bf16[256,2048]{1,0:T(8,128)(2,1)S(1)} %get-tuple-element.243.refs_3_), channel_id=1, source_target_pairs={{3,2},{2,1},{1,0},{7,6},{6,5},{5,4},{11,10},{10,9},{9,8},{15,14},{... | collective-permute-start | bytes 3145736 | tf_op jit(solution)/shard_map/ppermute | solution.py:413
  18.3 27.9 %collective-permute-start = (bf16[256,2048]{1,0:T(8,128)(2,1)S(1)}, bf16[256,2048]{1,0:T(8,128)(2,1)}, u32[]{:S(2)}, u32[]{:S(2)}) collective-permute-start(bf16[256,2048]{1,0:T(8,128)(2,1)S(1)} %get-tuple-element.243.refs_3_), channel_id=1, source_target_pairs={{0,1},{1,2},{2,3},{4,5},{5,6},{6,7},{8,9},{9,10},{10,11},{12,13},{... | collective-permute-start | bytes 3145736 | tf_op jit(solution)/shard_map/ppermute | solution.py:411
  48.4 258.9 %reduce-scatter.4.cloned.1.call-start = ((), (), s32[]{:S(2)}) async-start(), calls=%async_computation.5 | async-start | bytes 11796480 | tf_op jit(solution)/shard_map/reduce_scatter | solution.py:559
  80.4 26.8 %collective-permute-start.6 = (bf16[256,2048]{1,0:T(8,128)(2,1)S(1)}, bf16[256,2048]{1,0:T(8,128)(2,1)}, u32[]{:S(2)}, u32[]{:S(2)}) collective-permute-start(bf16[256,2048]{1,0:T(8,128)(2,1)S(1)} %collective-permute-done.3.refs_3_.refs_4_), channel_id=1, source_target_pairs={{2,1},{1,0},{6,5},{5,4},{10,9},{9,8},{14,13},{13,12},{18,17},{17,1... | collective-permute-start | bytes 3145736 | tf_op jit(solution)/shard_map/ppermute | solution.py:413
  85.0 48.3 %collective-permute-start.5 = (bf16[256,2048]{1,0:T(8,128)(2,1)}, bf16[256,2048]{1,0:T(8,128)(2,1)}, u32[]{:S(2)}, u32[]{:S(2)}) collective-permute-start(bf16[256,2048]{1,0:T(8,128)(2,1)} %collective-permute-done.4.refs_0_.refs_1_), channel_id=1, source_target_pairs={{2,3},{6,7},{10,11},{14,15},{18,19},{22,23},{26,27},{30,31}} | collective-permute-start | bytes 3145736 | tf_op jit(solution)/shard_map/ppermute | solution.py:411
  133.3 30.4 %collective-permute-start.8 = (bf16[256,2048]{1,0:T(8,128)(2,1)}, bf16[256,2048]{1,0:T(8,128)(2,1)}, u32[]{:S(2)}, u32[]{:S(2)}) collective-permute-start(bf16[256,2048]{1,0:T(8,128)(2,1)} %collective-permute-done.refs_2_), channel_id=1, source_target_pairs={{1,2},{2,3},{5,6},{6,7},{9,10},{10,11},{13,14},{14,15},{17,18},{18... | collective-permute-start | bytes 3145736 | tf_op jit(solution)/shard_map/ppermute | solution.py:411
  134.9 28.8 %collective-permute-start.9 = (bf16[256,2048]{1,0:T(8,128)(2,1)S(1)}, bf16[256,2048]{1,0:T(8,128)(2,1)}, u32[]{:S(2)}, u32[]{:S(2)}) collective-permute-start(bf16[256,2048]{1,0:T(8,128)(2,1)S(1)} %copy-done.26), channel_id=1, source_target_pairs={{2,1},{1,0},{6,5},{5,4},{10,9},{9,8},{14,13},{13,12},{18,17},{17,1... | collective-permute-start | bytes 3145736 | tf_op jit(solution)/shard_map/ppermute | solution.py:413
  163.7 30.1 %collective-permute-start.10 = (bf16[256,2048]{1,0:T(8,128)(2,1)}, bf16[256,2048]{1,0:T(8,128)(2,1)}, u32[]{:S(2)}, u32[]{:S(2)}) collective-permute-start(bf16[256,2048]{1,0:T(8,128)(2,1)} %collective-permute-done.8.refs_1_), channel_id=1, source_target_pairs={{2,3},{6,7},{10,11},{14,15},{18,19},{22,23},{26,27},{30,31}} | collective-permute-start | bytes 3145736 | tf_op jit(solution)/shard_map/ppermute | solution.py:411
  165.9 27.9 %collective-permute-start.11 = (bf16[256,2048]{1,0:T(8,128)(2,1)}, bf16[256,2048]{1,0:T(8,128)(2,1)}, u32[]{:S(2)}, u32[]{:S(2)}) collective-permute-start(bf16[256,2048]{1,0:T(8,128)(2,1)} %collective-permute-done.9.refs_5_), channel_id=1, source_target_pairs={{1,0},{5,4},{9,8},{13,12},{17,16},{21,20},{25,24},{29,28}} | collective-permute-start | bytes 3145736 | tf_op jit(solution)/shard_map/ppermute | solution.py:413
  195.4 27.5 %collective-permute-start.13 = (bf16[256,2048]{1,0:T(8,128)(2,1)}, bf16[256,2048]{1,0:T(8,128)(2,1)}, u32[]{:S(2)}, u32[]{:S(2)}) collective-permute-start(bf16[256,2048]{1,0:T(8,128)(2,1)} %get-tuple-element.240), channel_id=1, source_target_pairs={{3,2},{7,6},{11,10},{15,14},{19,18},{23,22},{27,26},{31,30}} | collective-permute-start | bytes 3145736 | tf_op jit(solution)/shard_map/ppermute | solution.py:456
  223.4 183.2 %reduce-scatter.6.cloned.1.call-start = ((), (), s32[]{:S(2)}) async-start(), calls=%async_computation.6 | async-start | bytes 9437184 | tf_op jit(solution)/shard_map/reduce_scatter | solution.py:559
  230.2 29.2 %collective-permute-start.15 = (bf16[256,2048]{1,0:T(8,128)(2,1)S(1)}, bf16[256,2048]{1,0:T(8,128)(2,1)S(1)}, u32[]{:S(2)}, u32[]{:S(2)}) collective-permute-start(bf16[256,2048]{1,0:T(8,128)(2,1)S(1)} %get-tuple-element.238), channel_id=1, source_target_pairs={{3,2},{2,1},{7,6},{6,5},{11,10},{10,9},{15,14},{14,13},{19,18},{18... | collective-permute-start | bytes 3145736 | tf_op jit(solution)/shard_map/ppermute | solution.py:456
  231.1 28.3 %collective-permute-start.14 = (bf16[256,2048]{1,0:T(8,128)(2,1)S(1)}, bf16[256,2048]{1,0:T(8,128)(2,1)S(1)}, u32[]{:S(2)}, u32[]{:S(2)}) collective-permute-start(bf16[256,2048]{1,0:T(8,128)(2,1)S(1)} %get-tuple-element.239), channel_id=1, source_target_pairs={{0,1},{1,2},{4,5},{5,6},{8,9},{9,10},{12,13},{13,14},{16,17},{17,1... | collective-permute-start | bytes 3145736 | tf_op jit(solution)/shard_map/ppermute | solution.py:455
  286.5 190.1 %reduce-scatter.8.cloned.1.call-start = ((), (), s32[]{:S(2)}) async-start(), calls=%async_computation.7 | async-start | bytes 7077888 | tf_op jit(solution)/shard_map/reduce_scatter | solution.py:559
  307.3 30.7 %collective-permute-start.18 = (bf16[320,2048]{1,0:T(8,128)(2,1)}, bf16[320,2048]{1,0:T(8,128)(2,1)}, u32[]{:S(2)}, u32[]{:S(2)}) collective-permute-start(bf16[320,2048]{1,0:T(8,128)(2,1)} %reduce-scatter.4.cloned.1.call-done.refs_3_), channel_id=1, source_target_pairs={{0,1},{1,2},{2,3},{4,5},{5,6},{6,7},{8,9},{9,10},{10,11},{12,13},{... | collective-permute-start | bytes 3932168 | tf_op jit(solution)/shard_map/ppermute | solution.py:411
  312.6 30.1 %collective-permute-start.19 = (bf16[320,2048]{1,0:T(8,128)(2,1)}, bf16[320,2048]{1,0:T(8,128)(2,1)}, u32[]{:S(2)}, u32[]{:S(2)}) collective-permute-start(bf16[320,2048]{1,0:T(8,128)(2,1)} %reduce-scatter.4.cloned.1.call-done.refs_3_), channel_id=1, source_target_pairs={{3,2},{2,1},{1,0},{7,6},{6,5},{5,4},{11,10},{10,9},{9,8},{15,14},{... | collective-permute-start | bytes 3932168 | tf_op jit(solution)/shard_map/ppermute | solution.py:413
  344.4 31.1 %collective-permute-start.21 = (bf16[320,2048]{1,0:T(8,128)(2,1)}, bf16[320,2048]{1,0:T(8,128)(2,1)}, u32[]{:S(2)}, u32[]{:S(2)}) collective-permute-start(bf16[320,2048]{1,0:T(8,128)(2,1)} %collective-permute-done.19.refs_4_), channel_id=1, source_target_pairs={{2,1},{1,0},{6,5},{5,4},{10,9},{9,8},{14,13},{13,12},{18,17},{17,1... | collective-permute-start | bytes 3932168 | tf_op jit(solution)/shard_map/ppermute | solution.py:413
  376.4 29.0 %collective-permute-start.23 = (bf16[320,2048]{1,0:T(8,128)(2,1)}, bf16[320,2048]{1,0:T(8,128)(2,1)S(1)}, u32[]{:S(2)}, u32[]{:S(2)}) collective-permute-start(bf16[320,2048]{1,0:T(8,128)(2,1)} %collective-permute-done.21.refs_5_), channel_id=1, source_target_pairs={{1,0},{5,4},{9,8},{13,12},{17,16},{21,20},{25,24},{29,28}} | collective-permute-start | bytes 3932168 | tf_op jit(solution)/shard_map/ppermute | solution.py:413
  476.6 28.5 %collective-permute-start.36 = (bf16[256,1536]{1,0:T(8,128)(2,1)}, bf16[256,1536]{1,0:T(8,128)(2,1)}, u32[]{:S(2)}, u32[]{:S(2)}) collective-permute-start(bf16[256,1536]{1,0:T(8,128)(2,1)} %reduce-scatter.8.cloned.1.call-done.refs_3_), channel_id=1, source_target_pairs={{0,1},{1,2},{2,3},{4,5},{5,6},{6,7},{8,9},{9,10},{10,11},{12,13},{... | collective-permute-start | bytes 2359304 | tf_op jit(solution)/shard_map/ppermute | solution.py:411
  493.7 48.5 %collective-permute-start.34 = (bf16[256,2048]{1,0:T(8,128)(2,1)}, bf16[256,2048]{1,0:T(8,128)(2,1)}, u32[]{:S(2)}, u32[]{:S(2)}) collective-permute-start(bf16[256,2048]{1,0:T(8,128)(2,1)} %get-tuple-element.200), channel_id=1, source_target_pairs={{0,1},{1,2},{2,3},{4,5},{5,6},{6,7},{8,9},{9,10},{10,11},{12,13},{... | collective-permute-start | bytes 3145736 | tf_op jit(solution)/shard_map/ppermute | solution.py:455
  499.2 43.0 %collective-permute-start.35 = (bf16[256,2048]{1,0:T(8,128)(2,1)}, bf16[256,2048]{1,0:T(8,128)(2,1)}, u32[]{:S(2)}, u32[]{:S(2)}) collective-permute-start(bf16[256,2048]{1,0:T(8,128)(2,1)} %get-tuple-element.201), channel_id=1, source_target_pairs={{3,2},{2,1},{1,0},{7,6},{6,5},{5,4},{11,10},{10,9},{9,8},{15,14},{... | collective-permute-start | bytes 3145736 | tf_op jit(solution)/shard_map/ppermute | solution.py:456
  512.0 28.2 %collective-permute-start.39 = (bf16[256,1536]{1,0:T(8,128)(2,1)}, bf16[256,1536]{1,0:T(8,128)(2,1)}, u32[]{:S(2)}, u32[]{:S(2)}) collective-permute-start(bf16[256,1536]{1,0:T(8,128)(2,1)} %collective-permute-done.37.refs_4_), channel_id=1, source_target_pairs={{2,1},{1,0},{6,5},{5,4},{10,9},{9,8},{14,13},{13,12},{18,17},{17,1... | collective-permute-start | bytes 2359304 | tf_op jit(solution)/shard_map/ppermute | solution.py:413
  (95 other events, 1288.0 us)
Sparse Core Ops, SparseCore 0:
  13.9 83.8 all-gather.4
  99.7 63.2 all-gather.6
  223.5 82.2 reduce-scatter.3
  309.1 71.2 reduce-scatter.5
  384.0 61.7 reduce-scatter.7
